TPU v7x, 32 devices: a whole 2x2x4 slice. The times are simulated.
32 devices in a mesh: section: 2 (over core), shard: 16 (over z, y, x).
Axes of the slice: x: 2, y: 2, z: 4, core: 2. Of those that a mesh axis runs over, the one named last changes fastest.
Arguments:
- tokens: bfloat16 [2, 1024, 2048], P(None, 'shard'), may hold values from -6 to 6
- cotangent: bfloat16 [2, 1024, 2048], P(None, 'shard'), may hold values from -6 to 6
- block_ids: int32 [2, 1024], replicated, may hold values from 0 to 7, never falling along the last dimension, each value on 1 to 256 neighbouring positions
- token_ids: int32 [2, 1024], P(None, 'shard'), may hold values from 0 to 65535
- attn_weight: bfloat16 [2, 5760, 2048], P('section', 'shard'), may hold values from -0.125 to 0.125
- ff_weight: bfloat16 [2, 3, 8192, 2048], P('section', None, 'shard'), may hold values from -0.125 to 0.125
- gains: bfloat16 [2, 12800], P('section', 'shard'), may hold values from 0.5 to 1.5
- table: bfloat16 [2, 65536, 256], P('section', 'shard'), may hold values from -6 to 6
Outputs:
- layer_outputs: bfloat16 [2, 2, 1024, 2048], P('section', None, 'shard')
- input_grads: bfloat16 [2, 2, 1024, 2048], P('section', None, 'shard')
- attn_grad: float32 [2, 5760, 2048], P('section', 'shard')
- ff_grad: float32 [2, 3, 8192, 2048], P('section', None, 'shard')
- gain_grad: float32 [2, 12800], P('section', 'shard')
- table_grad: float32 [2, 65536, 256], P('section', 'shard')
Inputs may be any that keep to these rules, and one draw needn't show every extreme that they name: `block_ids`: along each sequence the block numbers never fall; every block holds 1 to 256 positions and some block exactly 256.
All inputs are finite; a program needn't handle non-finite values.
Results may differ from a plain program's by a relative error of at most 0.022.
Values may be sent and summed in bfloat16 or wider, within the bound.
No kernel may reach another device: no remote copies, remote signals or barrier semaphores. Data moves between devices by JAX's collectives and lax.ppermute only.
A program may use at most 512 MiB of HBM per device.

v0:
```python
from functools import partial

import jax
import jax.numpy as jnp
from jax import lax
from jax.sharding import PartitionSpec as P

D = 2048
FF = 8192
HEADS = 8
KV_HEADS = 2
HEAD_DIM = 256
RANK = 64
PLD = 256
MICRO = 2
GAINS = 12800


EPS = 1e-06
ROPE_BASE = 10000.0
INV_ROOT2 = 0.7071067811865476
MASKED = -1e30


def shifted(value, axis, by):
    devices = lax.axis_size(axis)
    pairs = [(i, i + by) for i in range(devices) if 0 <= i + by < devices]
    return lax.ppermute(value, axis, pairs)


def rms_norm(values):
    return values * lax.rsqrt(jnp.mean(values * values, axis=-1, keepdims=True) + EPS)


def scaled_norm(values, gain_vec):
    return rms_norm(values) * gain_vec


def rope_tables(positions):
    half_width = HEAD_DIM // 2
    frequency = ROPE_BASE ** (-jnp.arange(half_width, dtype=jnp.float32) * (2.0 / HEAD_DIM))
    angles = positions.astype(jnp.float32)[:, None] * frequency[None, :]
    return (jnp.cos(angles), jnp.sin(angles))


def rotate(vectors, cosine_part, sine_part):
    half_width = vectors.shape[-1] // 2
    first_half = vectors[..., :half_width]
    second_half = vectors[..., half_width:]
    cosine_rows = cosine_part[:, None, :]
    sine_rows = sine_part[:, None, :]
    return jnp.concatenate(
        [
            first_half * cosine_rows - second_half * sine_rows,
            second_half * cosine_rows + first_half * sine_rows,
        ],
        axis=-1,
    )


def split_heads(projected_in, query_gain, key_gain, cosine_part, sine_part):
    row_count = projected_in.shape[0]
    query_width = HEADS * HEAD_DIM
    key_width = KV_HEADS * HEAD_DIM
    queries = projected_in[:, :query_width].reshape(row_count, HEADS, HEAD_DIM)
    key_heads = projected_in[:, query_width : query_width + key_width].reshape(
        row_count, KV_HEADS, HEAD_DIM
    )
    value_heads = projected_in[:, query_width + key_width : query_width + 2 * key_width].reshape(
        row_count, KV_HEADS, HEAD_DIM
    )
    latent = projected_in[:, query_width + 2 * key_width :]
    queries = rotate(rms_norm(queries) * query_gain, cosine_part, sine_part)
    key_heads = rotate(rms_norm(key_heads) * key_gain, cosine_part, sine_part)
    value_heads = rms_norm(value_heads)
    return (queries, key_heads, value_heads, latent)


def join_piece(hidden_in, normed, attended, laurel_raw, gain_laurel, gain_attn, gain_ffin):
    joined = (
        hidden_in + rms_norm(attended) * gain_attn + normed + rms_norm(laurel_raw) * gain_laurel
    ) * INV_ROOT2
    return (joined, rms_norm(joined) * gain_ffin)


def gated_gelu(gate_pre, up_pre):
    return jax.nn.gelu(gate_pre, approximate=True) * up_pre


def add_branch(residual, branch, gain_out):
    return residual + rms_norm(branch) * gain_out


def contract_last(left_side, right_side):
    return lax.dot_general(
        left_side, right_side, (((1,), (1,)), ((), ())), preferred_element_type=jnp.float32
    )


def contract_first(left_side, right_side):
    return lax.dot_general(
        left_side, right_side, (((0,), (0,)), ((), ())), preferred_element_type=jnp.float32
    )


def split_gains(gain_flat):
    gain_values = gain_flat.astype(jnp.float32)
    return (
        gain_values[: 6 * D].reshape(6, D),
        gain_values[6 * D : 6 * D + HEAD_DIM],
        gain_values[6 * D + HEAD_DIM :],
    )


def group_queries(queries_b):
    return queries_b.reshape(queries_b.shape[0], KV_HEADS, HEADS // KV_HEADS, HEAD_DIM)


def masked_scores(grouped, key_heads, blocks_own, blocks_all):
    scores = jnp.einsum(
        "qkgd,jkd->kgqj", grouped, key_heads, preferred_element_type=jnp.float32
    ) * HEAD_DIM ** (-0.5)
    allowed = blocks_all[None, :] <= blocks_own[:, None]
    return jnp.where(allowed, scores, MASKED)


def empty_slots(item_array):
    return jnp.zeros((MICRO + 1,) + item_array.shape, item_array.dtype)


def store_slot(buffer_array, item_array, slot_index):
    return lax.dynamic_update_index_in_dim(buffer_array, item_array, slot_index, 0)


def read_slot(buffer_array, slot_index):
    return lax.dynamic_index_in_dim(buffer_array, slot_index, 0, keepdims=False)


def stack_rows(buffer_array):
    valid_part = buffer_array[:MICRO]
    return valid_part.reshape((MICRO * valid_part.shape[1],) + valid_part.shape[2:])


def per_device(tokens, cotangent, block_ids, token_ids, attn_weight, ff_weight, gains, table):
    section_index = lax.axis_index("section")
    last_section = lax.axis_size("section") - 1
    shard_index = lax.axis_index("shard")
    seq_dev = tokens.shape[1]
    query_width = HEADS * HEAD_DIM
    key_width = KV_HEADS * HEAD_DIM
    input_rows = query_width + 2 * key_width + RANK
    output_start = input_rows + PLD
    laurel_start = output_start + query_width
    side_start = laurel_start + RANK
    step_count = MICRO + last_section
    score_scale = HEAD_DIM ** (-0.5)
    positions = shard_index * seq_dev + jnp.arange(seq_dev, dtype=jnp.int32)
    cosine_part, sine_part = rope_tables(positions)
    head_split = partial(split_heads, cosine_part=cosine_part, sine_part=sine_part)
    all_ids = lax.all_gather(token_ids, "shard", axis=1, tiled=True)
    vocab_dev = table.shape[1]
    local_ids = all_ids - shard_index * vocab_dev
    inside = (local_ids >= 0) & (local_ids < vocab_dev)
    clipped = jnp.clip(local_ids, 0, vocab_dev - 1)
    looked_up = jnp.where(
        inside[..., None], jnp.take(table[0], clipped, axis=0).astype(jnp.float32), 0.0
    )
    per_layer_all = lax.psum_scatter(looked_up, "shard", scatter_dimension=1, tiled=True)
    weights_fwd = (
        lax.all_gather(attn_weight[0], "shard", axis=0, tiled=True),
        lax.all_gather(ff_weight[0], "shard", axis=1, tiled=True),
        lax.all_gather(gains[0], "shard", axis=0, tiled=True),
    )
    received = jnp.zeros((seq_dev, D), jnp.bfloat16)
    out_buffer = jnp.zeros((MICRO + 1, seq_dev, D), jnp.bfloat16)
    saved_items = None
    for step_index in range(step_count):
        micro_index = step_index - section_index
        is_valid = (micro_index >= 0) & (micro_index < MICRO)
        slot_index = jnp.where(is_valid, micro_index, MICRO)
        micro_clip = jnp.clip(micro_index, 0, MICRO - 1)
        layer_in_b = jnp.where(section_index == 0, tokens[min(step_index, MICRO - 1)], received)
        per_layer = lax.dynamic_index_in_dim(per_layer_all, micro_clip, 0, keepdims=False)
        blocks_all = lax.dynamic_index_in_dim(block_ids, micro_clip, 0, keepdims=False)
        forward_attn_full, forward_ff_full, forward_gain_flat = weights_fwd
        forward_gain_rows, forward_query_gain, forward_key_gain = split_gains(forward_gain_flat)
        forward_hidden_in = layer_in_b.astype(jnp.float32)
        forward_normed = scaled_norm(forward_hidden_in, forward_gain_rows[0])
        normed_b = forward_normed.astype(jnp.bfloat16)
        forward_projected_in = contract_last(normed_b, forward_attn_full[:input_rows])
        queries, forward_key_heads, forward_value_heads, latent = head_split(
            forward_projected_in, forward_query_gain, forward_key_gain
        )
        forward_queries_b = queries.astype(jnp.bfloat16)
        key_local = forward_key_heads.reshape(seq_dev, key_width).astype(jnp.bfloat16)
        value_local = forward_value_heads.reshape(seq_dev, key_width).astype(jnp.bfloat16)
        forward_key_all = lax.all_gather(key_local, "shard", axis=0, tiled=True)
        forward_value_all = lax.all_gather(value_local, "shard", axis=0, tiled=True)
        forward_blocks_own = lax.dynamic_slice_in_dim(blocks_all, shard_index * seq_dev, seq_dev)
        forward_scores = masked_scores(
            group_queries(forward_queries_b),
            forward_key_all.reshape(-1, KV_HEADS, HEAD_DIM),
            forward_blocks_own,
            blocks_all,
        )
        row_max = jnp.max(forward_scores, axis=-1, keepdims=True)
        exponentials = jnp.exp(forward_scores - row_max)
        denominator = jnp.sum(exponentials, axis=-1, keepdims=True)
        forward_probabilities = exponentials / denominator
        forward_log_total = row_max + jnp.log(denominator)
        mixed_heads = jnp.einsum(
            "kgqj,jkd->qkgd",
            forward_probabilities.astype(jnp.bfloat16),
            forward_value_all.reshape(-1, KV_HEADS, HEAD_DIM),
            preferred_element_type=jnp.float32,
        )
        forward_mixed_b = mixed_heads.reshape(seq_dev, query_width).astype(jnp.bfloat16)
        forward_attended = jnp.dot(
            forward_mixed_b,
            forward_attn_full[output_start:laurel_start],
            preferred_element_type=jnp.float32,
        )
        forward_latent_b = latent.astype(jnp.bfloat16)
        forward_laurel_raw = jnp.dot(
            forward_latent_b,
            forward_attn_full[laurel_start:side_start],
            preferred_element_type=jnp.float32,
        )
        forward_joined, forward_prenorm = join_piece(
            forward_hidden_in,
            forward_normed,
            forward_attended,
            forward_laurel_raw,
            forward_gain_rows[1],
            forward_gain_rows[2],
            forward_gain_rows[3],
        )
        forward_prenorm_b = forward_prenorm.astype(jnp.bfloat16)
        forward_gate_up = jnp.einsum(
            "rd,cfd->crf",
            forward_prenorm_b,
            forward_ff_full[:2],
            preferred_element_type=jnp.float32,
        )
        forward_hidden_ff_b = gated_gelu(forward_gate_up[0], forward_gate_up[1]).astype(
            jnp.bfloat16
        )
        forward_down_out = jnp.dot(
            forward_hidden_ff_b, forward_ff_full[2], preferred_element_type=jnp.float32
        )
        forward_settled = add_branch(forward_joined, forward_down_out, forward_gain_rows[4])
        forward_side_gate = contract_last(
            forward_settled.astype(jnp.bfloat16), forward_attn_full[input_rows:output_start]
        )
        forward_gated_b = gated_gelu(forward_side_gate, per_layer).astype(jnp.bfloat16)
        forward_projected = jnp.dot(
            forward_gated_b, forward_attn_full[side_start:], preferred_element_type=jnp.float32
        )
        layer_out = add_branch(forward_settled, forward_projected, forward_gain_rows[5])
        forward_kept_items = (
            layer_in_b,
            forward_projected_in,
            forward_queries_b,
            key_local,
            value_local,
            forward_log_total,
            forward_mixed_b,
            forward_attended,
            forward_latent_b,
            forward_laurel_raw,
            forward_prenorm_b,
            forward_gate_up,
            forward_hidden_ff_b,
            forward_down_out,
            forward_settled,
            forward_side_gate,
            forward_gated_b,
            forward_projected,
        )
        layer_out, kept_items = (layer_out, forward_kept_items)
        layer_out_b = layer_out.astype(jnp.bfloat16)
        out_buffer = store_slot(out_buffer, layer_out_b, slot_index)
        if saved_items is None:
            saved_items = jax.tree.map(empty_slots, kept_items)
        saved_items = jax.tree.map(
            partial(store_slot, slot_index=slot_index), saved_items, kept_items
        )
        if step_index + 1 < step_count:
            received = shifted(layer_out_b, "section", 1)
    grad_received = jnp.zeros((seq_dev, D), jnp.bfloat16)
    grad_in_buffer = jnp.zeros((MICRO + 1, seq_dev, D), jnp.bfloat16)
    gain_total = jnp.zeros((GAINS,), jnp.float32)
    per_layer_grads = jnp.zeros((MICRO + 1, seq_dev, PLD), jnp.float32)
    operand_store = None
    for step_index in range(step_count):
        micro_index = MICRO - 1 - step_index + last_section - section_index
        is_valid = (micro_index >= 0) & (micro_index < MICRO)
        slot_index = jnp.where(is_valid, micro_index, MICRO)
        micro_clip = jnp.clip(micro_index, 0, MICRO - 1)
        top_grad = lax.dynamic_index_in_dim(cotangent, micro_clip, 0, keepdims=False)
        grad_out = jnp.where(section_index == last_section, top_grad, grad_received).astype(
            jnp.float32
        )
        kept_items = jax.tree.map(partial(read_slot, slot_index=slot_index), saved_items)
        per_layer = lax.dynamic_index_in_dim(per_layer_all, micro_clip, 0, keepdims=False)
        blocks_all = lax.dynamic_index_in_dim(block_ids, micro_clip, 0, keepdims=False)
        (
            backward_layer_in_b,
            projected_in,
            queries_b,
            key_keep,
            value_keep,
            log_total,
            mixed_b,
            attended,
            latent_b,
            laurel_raw,
            prenorm_b,
            gate_up,
            hidden_ff_b,
            down_out,
            settled,
            side_gate,
            gated_b,
            projected,
        ) = kept_items
        attn_full, ff_full, gain_flat = weights_fwd
        gain_rows, query_gain, key_gain = split_gains(gain_flat)
        hidden_in = backward_layer_in_b.astype(jnp.float32)
        normed = scaled_norm(hidden_in, gain_rows[0])
        joined, prenorm = join_piece(
            hidden_in, normed, attended, laurel_raw, gain_rows[1], gain_rows[2], gain_rows[3]
        )
        key_all = lax.all_gather(key_keep, "shard", axis=0, tiled=True)
        value_all = lax.all_gather(value_keep, "shard", axis=0, tiled=True)
        grad_settled, grad_projected, grad_gain5 = jax.vjp(
            add_branch, settled, projected, gain_rows[5]
        )[1](grad_out)
        grad_projected_b = grad_projected.astype(jnp.bfloat16)
        grad_gated = contract_last(grad_projected_b, attn_full[side_start:])
        grad_side_gate, grad_per_layer = jax.vjp(gated_gelu, side_gate, per_layer)[1](grad_gated)
        grad_side_gate_b = grad_side_gate.astype(jnp.bfloat16)
        grad_settled = grad_settled + jnp.dot(
            grad_side_gate_b, attn_full[input_rows:output_start], preferred_element_type=jnp.float32
        )
        grad_joined, grad_down, grad_gain4 = jax.vjp(add_branch, joined, down_out, gain_rows[4])[1](
            grad_settled
        )
        grad_down_b = grad_down.astype(jnp.bfloat16)
        grad_hidden_ff = contract_last(grad_down_b, ff_full[2])
        grad_gate, grad_up = jax.vjp(gated_gelu, gate_up[0], gate_up[1])[1](grad_hidden_ff)
        grad_gate_up_b = jnp.stack([grad_gate, grad_up]).astype(jnp.bfloat16)
        grad_prenorm = jnp.einsum(
            "crf,cfd->rd", grad_gate_up_b, ff_full[:2], preferred_element_type=jnp.float32
        )
        join_pull = jax.vjp(
            join_piece,
            hidden_in,
            normed,
            attended,
            laurel_raw,
            gain_rows[1],
            gain_rows[2],
            gain_rows[3],
        )[1]
        grad_hidden, grad_normed, grad_attended, grad_laurel, grad_gain1, grad_gain2, grad_gain3 = (
            join_pull((grad_joined, grad_prenorm))
        )
        grad_attended_b = grad_attended.astype(jnp.bfloat16)
        grad_laurel_b = grad_laurel.astype(jnp.bfloat16)
        grad_mixed_b = contract_last(grad_attended_b, attn_full[output_start:laurel_start]).astype(
            jnp.bfloat16
        )
        grad_latent = contract_last(grad_laurel_b, attn_full[laurel_start:side_start])
        grouped = group_queries(queries_b)
        key_heads = key_all.reshape(-1, KV_HEADS, HEAD_DIM)
        value_heads = value_all.reshape(-1, KV_HEADS, HEAD_DIM)
        blocks_own = lax.dynamic_slice_in_dim(blocks_all, shard_index * seq_dev, seq_dev)
        scores = masked_scores(grouped, key_heads, blocks_own, blocks_all)
        probabilities = jnp.exp(scores - log_total)
        grad_mixed_heads = grad_mixed_b.reshape(seq_dev, KV_HEADS, HEADS // KV_HEADS, HEAD_DIM)
        grad_probs = jnp.einsum(
            "qkgd,jkd->kgqj", grad_mixed_heads, value_heads, preferred_element_type=jnp.float32
        )
        row_dot = jnp.sum(grad_probs * probabilities, axis=-1, keepdims=True)
        grad_scores_b = (probabilities * (grad_probs - row_dot)).astype(jnp.bfloat16)
        grad_queries = (
            jnp.einsum(
                "kgqj,jkd->qkgd", grad_scores_b, key_heads, preferred_element_type=jnp.float32
            )
            * score_scale
        )
        grad_keys_all = (
            jnp.einsum("kgqj,qkgd->jkd", grad_scores_b, grouped, preferred_element_type=jnp.float32)
            * score_scale
        ).reshape(-1, key_width)
        grad_values_all = jnp.einsum(
            "kgqj,qkgd->jkd",
            probabilities.astype(jnp.bfloat16),
            grad_mixed_heads,
            preferred_element_type=jnp.float32,
        ).reshape(-1, key_width)
        grad_keys = lax.psum_scatter(grad_keys_all, "shard", scatter_dimension=0, tiled=True)
        grad_values = lax.psum_scatter(grad_values_all, "shard", scatter_dimension=0, tiled=True)
        head_pull = jax.vjp(head_split, projected_in, query_gain, key_gain)[1]
        grad_projected_in, grad_query_gain, grad_key_gain = head_pull(
            (
                grad_queries.reshape(seq_dev, HEADS, HEAD_DIM),
                grad_keys.reshape(seq_dev, KV_HEADS, HEAD_DIM),
                grad_values.reshape(seq_dev, KV_HEADS, HEAD_DIM),
                grad_latent,
            )
        )
        grad_projected_in_b = grad_projected_in.astype(jnp.bfloat16)
        grad_normed = grad_normed + jnp.dot(
            grad_projected_in_b, attn_full[:input_rows], preferred_element_type=jnp.float32
        )
        grad_front, grad_gain0 = jax.vjp(scaled_norm, hidden_in, gain_rows[0])[1](grad_normed)
        grad_hidden = grad_hidden + grad_front
        gain_vec = jnp.concatenate(
            [
                grad_gain0,
                grad_gain1,
                grad_gain2,
                grad_gain3,
                grad_gain4,
                grad_gain5,
                grad_query_gain,
                grad_key_gain,
            ]
        )
        operands = (
            normed.astype(jnp.bfloat16),
            grad_projected_in_b,
            settled.astype(jnp.bfloat16),
            grad_side_gate_b,
            mixed_b,
            grad_attended_b,
            latent_b,
            grad_laurel_b,
            gated_b,
            grad_projected_b,
            prenorm_b,
            grad_gate_up_b,
            hidden_ff_b,
            grad_down_b,
        )
        grad_hidden, gain_vec, grad_per_layer, operands = (
            grad_hidden,
            gain_vec,
            grad_per_layer,
            operands,
        )
        grad_hidden_b = grad_hidden.astype(jnp.bfloat16)
        grad_in_buffer = store_slot(grad_in_buffer, grad_hidden_b, slot_index)
        gain_total = gain_total + jnp.where(is_valid, gain_vec, 0.0)
        per_layer_grads = store_slot(per_layer_grads, grad_per_layer, slot_index)
        if operand_store is None:
            operand_store = jax.tree.map(empty_slots, operands)
        operand_store = jax.tree.map(
            partial(store_slot, slot_index=slot_index), operand_store, operands
        )
        if step_index + 1 < step_count:
            grad_received = shifted(grad_hidden_b, "section", -1)
    (
        normed_store,
        grad_proj_store,
        settled_store,
        grad_side_store,
        mixed_store,
        grad_attended_store,
        latent_store,
        grad_laurel_store,
        gated_store,
        grad_projected_store,
        prenorm_store,
        grad_gate_up_store,
        hidden_ff_store,
        grad_down_store,
    ) = operand_store
    attn_term = jnp.concatenate(
        [
            contract_first(stack_rows(grad_proj_store), stack_rows(normed_store)),
            contract_first(stack_rows(grad_side_store), stack_rows(settled_store)),
            contract_first(stack_rows(mixed_store), stack_rows(grad_attended_store)),
            contract_first(stack_rows(latent_store), stack_rows(grad_laurel_store)),
            contract_first(stack_rows(gated_store), stack_rows(grad_projected_store)),
        ],
        axis=0,
    )
    attn_grad, gain_grad = (
        lax.psum_scatter(attn_term, "shard", scatter_dimension=0, tiled=True),
        lax.psum_scatter(gain_total, "shard", scatter_dimension=0, tiled=True),
    )
    prenorm_all = stack_rows(prenorm_store)
    hidden_ff_all = stack_rows(hidden_ff_store)
    grad_down_all = stack_rows(grad_down_store)
    grad_gate_up_all = (
        grad_gate_up_store[:MICRO].transpose(1, 0, 2, 3).reshape(2, MICRO * seq_dev, FF)
    )
    unit_values = jnp.concatenate([grad_gate_up_all, hidden_ff_all[None]], axis=0)
    owned_columns = lax.all_to_all(unit_values, "shard", split_axis=2, concat_axis=1, tiled=True)
    gate_up_term = jnp.einsum(
        "cnf,nd->fcd",
        owned_columns[:2],
        lax.all_gather(prenorm_all, "shard", axis=0, tiled=True),
        preferred_element_type=jnp.float32,
    )
    down_term = contract_first(
        owned_columns[2], lax.all_gather(grad_down_all, "shard", axis=0, tiled=True)
    )
    ff_local = jnp.concatenate([gate_up_term, down_term[:, None, :]], axis=1)
    ff_grad = ff_local.transpose(1, 0, 2)
    grad_pl_b = per_layer_grads[:MICRO].astype(jnp.bfloat16)
    grad_pl_all = lax.all_gather(grad_pl_b, "shard", axis=1, tiled=True)
    table_grad = (
        jnp.zeros((vocab_dev, PLD), jnp.float32)
        .at[clipped]
        .add(jnp.where(inside[..., None], grad_pl_all.astype(jnp.float32), 0.0))
    )
    return (
        out_buffer[:MICRO][None],
        grad_in_buffer[:MICRO][None],
        attn_grad[None],
        ff_grad[None],
        gain_grad[None],
        table_grad[None],
    )


def solution(mesh):
    placed = (
        P(None, "shard", None),
        P(None, "shard", None),
        P(),
        P(None, "shard"),
        P("section", "shard", None),
        P("section", None, "shard", None),
        P("section", "shard"),
        P("section", "shard", None),
    )
    return jax.shard_map(
        per_device,
        mesh=mesh,
        in_specs=placed,
        out_specs=(
            P("section", None, "shard", None),
            P("section", None, "shard", None),
            P("section", "shard", None),
            P("section", None, "shard", None),
            P("section", "shard"),
            P("section", "shard", None),
        ),
        check_vma=False,
    )
```

profile of v0, /device:TPU:27, one launch (start us, length us, event | category | flops | bytes accessed | tf_op | source)
XLA Modules:
  0.0 3916.1 jit_solution(8814937554234117302)
XLA Ops:
  10.9 56.7 %all-reduce.24 = bf16[12800]{0:T(1024)(128)(2,1)S(1)} all-reduce(bf16[12800]{0:T(1024)(128)(2,1)S(1)} %dynamic-update-slice), channel_id=2, replica_groups=mesh['section'=2,'shard'=16] {'shard'}, use_global_device_ids=true, to_apply=%add.24 | all-reduce | flops 12800 | bytes 51200
  69.7 197.9 %all-gather.46.cloned.1.call-done = bf16[1,5760,2048]{2,1,0:T(8,128)(2,1)} async-done(((bf16[1,360,2048]{2,1,0:T(8,128)(2,1)}), bf16[1,5760,2048]{2,1,0:T(8,128)(2,1)}) %all-gather.46.cloned.1.call-update) | async-done | bytes 23592976 | tf_op jit(solution)/shard_map/all_gather | solution.py:170
  269.1 7.9 bitcast_dynamic-update-slice_fusion.7
  283.9 24.8 all-gather.9
  309.0 7.5 gather_fusion
  322.7 10.7 all-gather.30.cloned.1.call-done
  338.0 52.9 %all-gather.28.cloned.1.call-done = bf16[1024,512]{1,0:T(8,128)(2,1)} async-done(((bf16[64,512]{1,0:T(8,128)(2,1)}), bf16[1024,512]{1,0:T(8,128)(2,1)}) %all-gather.28.cloned.1.call-update) | async-done | bytes 1048592 | tf_op jit(solution)/shard_map/all_gather | solution.py:198
  395.2 5.1 multiply_reduce_fusion.40
  400.8 977.3 %all-gather.48.cloned.1.call-done = bf16[1,3,8192,2048]{3,2,1,0:T(8,128)(2,1)} async-done(((bf16[1,3,512,2048]{3,2,1,0:T(8,128)(2,1)}), bf16[1,3,8192,2048]{3,2,1,0:T(8,128)(2,1)}) %all-gather.48.cloned.1.call-update) | async-done | bytes 100663312 | tf_op jit(solution)/shard_map/all_gather | solution.py:171
  1378.0 6.3 broadcast_in_dim.570
  1384.3 31.5 bitcast_dynamic-update-slice_fusion.4
  1421.8 14.6 multiply_reduce_fusion.37
  1437.9 6.6 reduce-scatter.15.cloned.1.call-done
  1451.7 11.7 collective-permute-done
  1463.7 9.6 bitcast_dynamic-update-slice_fusion.6
  1486.5 45.1 %all-gather.34.cloned.1.call-done = bf16[1024,512]{1,0:T(8,128)(2,1)} async-done(((bf16[64,512]{1,0:T(8,128)(2,1)}), bf16[1024,512]{1,0:T(8,128)(2,1)}) %all-gather.34.cloned.1.call-update) | async-done | bytes 1048592 | tf_op jit(solution)/shard_map/all_gather | solution.py:197
  1537.6 50.9 %all-gather.32.cloned.1.call-done = bf16[1024,512]{1,0:T(8,128)(2,1)} async-done(((bf16[64,512]{1,0:T(8,128)(2,1)}), bf16[1024,512]{1,0:T(8,128)(2,1)}) %all-gather.32.cloned.1.call-update) | async-done | bytes 1048592 | tf_op jit(solution)/shard_map/all_gather | solution.py:198
  1593.7 5.1 multiply_reduce_fusion.34
  1599.6 31.5 bitcast_dynamic-update-slice_fusion.3
  1631.1 4.3 constant_dynamic-update-slice_fusion.1
  1635.4 14.8 multiply_reduce_fusion.31
  1664.5 9.5 bitcast_dynamic-update-slice_fusion.5
  1699.9 28.7 all-gather.38.cloned.1.call-done
  1734.6 50.9 %all-gather.36.cloned.1.call-done = bf16[1024,512]{1,0:T(8,128)(2,1)} async-done(((bf16[64,512]{1,0:T(8,128)(2,1)}), bf16[1024,512]{1,0:T(8,128)(2,1)}) %all-gather.36.cloned.1.call-update) | async-done | bytes 1048592 | tf_op jit(solution)/shard_map/all_gather | solution.py:198
  1790.7 5.8 bitcast_dynamic-update-slice_fusion.14
  1801.5 31.5 bitcast_dynamic-update-slice_fusion.2
  1833.1 4.3 constant_dynamic-update-slice_fusion
  1837.4 14.8 multiply_reduce_fusion.25
  1867.6 19.4 fusion.47
  1887.0 25.6 multiply_reduce_fusion.9
  1919.4 6.7 fusion.38
  1966.0 46.8 %all-gather.56.cloned.1.call-done = bf16[1,1024,512]{2,1,0:T(8,128)(2,1)} async-done(((bf16[1,64,512]{2,1,0:T(8,128)(2,1)}), bf16[1,1024,512]{2,1,0:T(8,128)(2,1)}) %all-gather.56.cloned.1.call-update) | async-done | bytes 1048592 | tf_op jit(solution)/shard_map/all_gather | solution.py:335
  2028.0 53.2 %reduce-scatter.17.cloned.1.call-done = f32[64,512]{1,0:T(8,128)} async-done(((f32[1024,512]{1,0:T(8,128)}), f32[64,512]{1,0:T(8,128)}) %reduce-scatter.17.cloned.1.call-update) | async-done | bytes 131088 | tf_op jit(solution)/shard_map/reduce_scatter | solution.py:404
  2105.4 56.7 %reduce-scatter.25.cloned.1.call-done = f32[64,512]{1,0:T(8,128)} async-done(((f32[1024,512]{1,0:T(8,128)}), f32[64,512]{1,0:T(8,128)}) %reduce-scatter.25.cloned.1.call-update) | async-done | bytes 131088
  2177.3 6.9 fusion.178
  2185.5 12.2 collective-permute-start.2
  2208.9 19.1 fusion.54
  2228.0 25.4 multiply_reduce_fusion.5
  2258.3 6.7 fusion.39
  2304.6 38.0 reduce-scatter.19.cloned.1.call-done
  2352.7 70.4 %reduce-scatter.27.cloned.1.call-done = f32[64,512]{1,0:T(8,128)} async-done(((f32[1024,512]{1,0:T(8,128)}), f32[64,512]{1,0:T(8,128)}) %reduce-scatter.27.cloned.1.call-update) | async-done | bytes 131088
  2438.3 7.8 fusion.175
  2447.3 13.1 collective-permute-start.3
  2460.4 30.9 all-gather.58.cloned.1.call-done
  2493.7 54.5 %all-gather.60.cloned.1.call-done = bf16[1,1024,512]{2,1,0:T(8,128)(2,1)} async-done(((bf16[1,64,512]{2,1,0:T(8,128)(2,1)}), bf16[1,1024,512]{2,1,0:T(8,128)(2,1)}) %all-gather.60.cloned.1.call-update) | async-done | bytes 1048592 | tf_op jit(solution)/shard_map/all_gather | solution.py:335
  2559.6 19.1 fusion.61
  2578.7 25.4 multiply_reduce_fusion.1
  2608.5 6.1 fusion.40
  2657.6 29.8 reduce-scatter.21.cloned.1.call-done
  2691.8 77.3 %reduce-scatter.29.cloned.1.call-done = f32[64,512]{1,0:T(8,128)} async-done(((f32[1024,512]{1,0:T(8,128)}), f32[64,512]{1,0:T(8,128)}) %reduce-scatter.29.cloned.1.call-update) | async-done | bytes 131088
  2772.6 7.5 fusion.172
  2781.2 13.2 bitcast_dynamic-update-slice_fusion
  2797.2 9.3 bitcast_dynamic-update-slice_fusion.1
  2824.4 13.1 copy.491
  2837.7 9.9 all-to-all-start
  2852.4 14.6 scatter_custom_fusion
  2867.1 303.3 %all-reduce.25 = f32[12800]{0:T(1024)S(1)} all-reduce(f32[12800]{0:T(1024)S(1)} %select_add_fusion), channel_id=19, replica_groups=mesh['section'=2,'shard'=16] {'shard'}, use_global_device_ids=true, to_apply=%region_122.123.clone | all-reduce | flops 12800 | bytes 102400
  3181.3 6.2 copy.493
  3187.5 14.6 fusion.20
  3202.1 41.3 %all-gather.42.cloned.1.call-done = bf16[2048,2048]{1,0:T(8,128)(2,1)} async-done(((bf16[128,2048]{1,0:T(8,128)(2,1)}), bf16[2048,2048]{1,0:T(8,128)(2,1)}) %all-gather.42.cloned.1.call-update) | async-done | bytes 8388624 | tf_op jit(solution)/shard_map/all_gather | solution.py:510
  3243.4 7.0 convolution_bitcast_fusion
  3250.4 10.1 maximum_bitcast_fusion
  3260.4 12.9 copy.496
  3273.4 635.7 %reduce-scatter.23.cloned.1.call-done = f32[360,2048]{1,0:T(8,128)} async-done(((f32[5760,2048]{1,0:T(8,128)}), f32[360,2048]{1,0:T(8,128)}) %reduce-scatter.23.cloned.1.call-update) | async-done | bytes 2949136 | tf_op jit(solution)/shard_map/reduce_scatter | solution.py:492
  (1108 shorter events, 427.6 us)
Async XLA Ops:
  7.2 301.8 %copy-start = (bf16[1,4096,256]{2,1,0:T(8,128)(2,1)S(1)}, bf16[1,4096,256]{2,1,0:T(8,128)(2,1)}, u32[]{:S(2)}) copy-start(bf16[1,4096,256]{2,1,0:T(8,128)(2,1)} %param.15) | copy-start | bytes 6291460
  7.2 262.0 %copy-start.48 = (bf16[2,64,2048]{2,1,0:T(8,128)(2,1)S(1)}, bf16[2,64,2048]{2,1,0:T(8,128)(2,1)}, u32[]{:S(2)}) copy-start(bf16[2,64,2048]{2,1,0:T(8,128)(2,1)} %param.8) | copy-start | bytes 1572868
  7.2 260.4 %all-gather.46.cloned.1.call-start = ((), (), s32[]{:S(2)}) async-start(), calls=%async_computation.23 | async-start | bytes 25067520 | tf_op jit(solution)/shard_map/all_gather | solution.py:170
  7.9 325.4 %all-gather.30.cloned.1.call-start = ((), (), s32[]{:S(2)}) async-start(), calls=%async_computation.10 | async-start | bytes 1114112 | tf_op jit(solution)/shard_map/all_gather | solution.py:197
  68.9 208.2 %copy-start.230 = (f32[64]{0:T(128)}, f32[64]{0:T(128)S(1)}, u32[]{:S(2)}) copy-start(f32[64]{0:T(128)S(1)} %add_rsqrt_fusion.23) | copy-start | bytes 772
  280.5 110.3 %all-gather.28.cloned.1.call-start = ((), (), s32[]{:S(2)}) async-start(), calls=%async_computation.9 | async-start | bytes 1114112 | tf_op jit(solution)/shard_map/all_gather | solution.py:198
  283.3 1094.8 %all-gather.48.cloned.1.call-start = ((), (), s32[]{:S(2)}) async-start(), calls=%async_computation.24 | async-start | bytes 106954752 | tf_op jit(solution)/shard_map/all_gather | solution.py:171
  283.9 1160.6 %reduce-scatter.15.cloned.1.call-start = ((), (), s32[]{:S(2)}) async-start(), calls=%async_computation.11 | async-start | bytes 2228224 | tf_op jit(solution)/shard_map/reduce_scatter | solution.py:168
  318.8 1212.9 %all-gather.34.cloned.1.call-start = ((), (), s32[]{:S(2)}) async-start(), calls=%async_computation.13 | async-start | bytes 1114112 | tf_op jit(solution)/shard_map/all_gather | solution.py:197
  337.9 56.8 %copy-start.168 = (f32[2,4,64]{2,1,0:T(4,128)}, f32[2,4,64]{2,1,0:T(4,128)S(1)}, u32[]{:S(2)}) copy-start(f32[2,4,64]{2,1,0:T(4,128)S(1)} %fusion.121) | copy-start | bytes 6148
  400.3 984.0 %copy-start.78 = (f32[64,2048]{1,0:T(8,128)}, f32[64,2048]{1,0:T(8,128)S(1)}, u32[]{:S(2)}) copy-start(f32[64,2048]{1,0:T(8,128)S(1)} %get-tuple-element.313) | copy-start | bytes 1572868
  400.7 1035.9 %copy-start.39 = (f32[64,2048]{1,0:T(8,128)}, f32[64,2048]{1,0:T(8,128)S(1)}, u32[]{:S(2)}) copy-start(f32[64,2048]{1,0:T(8,128)S(1)} %get-tuple-element.188) | copy-start | bytes 1572868
  400.8 983.6 %copy-start.210 = (f32[64]{0:T(128)}, f32[64]{0:T(128)S(1)}, u32[]{:S(2)}) copy-start(f32[64]{0:T(128)S(1)} %rsqrt_multiply_fusion.2) | copy-start | bytes 772
  1449.7 13.8 collective-permute-start
  1476.0 112.5 %all-gather.32.cloned.1.call-start = ((), (), s32[]{:S(2)}) async-start(), calls=%async_computation.12 | async-start | bytes 1114112 | tf_op jit(solution)/shard_map/all_gather | solution.py:198
  1478.9 249.8 %all-gather.38.cloned.1.call-start = ((), (), s32[]{:S(2)}) async-start(), calls=%async_computation.15 | async-start | bytes 1114112 | tf_op jit(solution)/shard_map/all_gather | solution.py:197
  1483.6 50.3 %copy-start.143 = (pred[64,1024]{1,0:T(8,128)(4,1)S(1)}, pred[64,1024]{1,0:T(8,128)(4,1)}, u32[]{:S(2)}) copy-start(pred[64,1024]{1,0:T(8,128)(4,1)} %broadcast_compare_fusion.1) | copy-start | bytes 196612
  1483.7 52.0 %copy-start.94 = (bf16[64,8,128]{2,1,0:T(8,128)(2,1)}, bf16[64,8,128]{2,1,0:T(8,128)(2,1)S(1)}, u32[]{:S(2)}) copy-start(bf16[64,8,128]{2,1,0:T(8,128)(2,1)S(1)} %get-tuple-element.232) | copy-start | bytes 393220
  1483.7 52.0 %copy-start.96 = (bf16[64,8,128]{2,1,0:T(8,128)(2,1)}, bf16[64,8,128]{2,1,0:T(8,128)(2,1)S(1)}, u32[]{:S(2)}) copy-start(bf16[64,8,128]{2,1,0:T(8,128)(2,1)S(1)} %get-tuple-element.233) | copy-start | bytes 393220
  1535.8 55.0 %copy-start.170 = (f32[2,4,64]{2,1,0:T(4,128)}, f32[2,4,64]{2,1,0:T(4,128)S(1)}, u32[]{:S(2)}) copy-start(f32[2,4,64]{2,1,0:T(4,128)S(1)} %get-tuple-element.321) | copy-start | bytes 6148
  1537.6 55.6 %copy-start.172 = (f32[2,4,64]{2,1,0:T(4,128)}, f32[2,4,64]{2,1,0:T(4,128)S(1)}, u32[]{:S(2)}) copy-start(f32[2,4,64]{2,1,0:T(4,128)S(1)} %fusion.122) | copy-start | bytes 6148
  1599.6 50.6 %copy-start.28 = (f32[64,2048]{1,0:T(8,128)}, f32[64,2048]{1,0:T(8,128)S(1)}, u32[]{:S(2)}) copy-start(f32[64,2048]{1,0:T(8,128)S(1)} %get-tuple-element.184) | copy-start | bytes 1572868
  1658.5 4.3 collective-permute-start.1
  1676.2 109.3 %all-gather.36.cloned.1.call-start = ((), (), s32[]{:S(2)}) async-start(), calls=%async_computation.14 | async-start | bytes 1114112 | tf_op jit(solution)/shard_map/all_gather | solution.py:198
  1677.4 249.9 %all-gather.50.cloned.1.call-start = ((), (), s32[]{:S(2)}) async-start(), calls=%async_computation.25 | async-start | bytes 1114112 | tf_op jit(solution)/shard_map/all_gather | solution.py:334
  1679.1 250.4 %all-gather.52.cloned.1.call-start = ((), (), s32[]{:S(2)}) async-start(), calls=%async_computation.26 | async-start | bytes 1114112 | tf_op jit(solution)/shard_map/all_gather | solution.py:335
  1685.9 277.7 %all-gather.54.cloned.1.call-start = ((), (), s32[]{:S(2)}) async-start(), calls=%async_computation.27 | async-start | bytes 1114112 | tf_op jit(solution)/shard_map/all_gather | solution.py:334
  1692.0 320.7 %all-gather.56.cloned.1.call-start = ((), (), s32[]{:S(2)}) async-start(), calls=%async_computation.28 | async-start | bytes 1114112 | tf_op jit(solution)/shard_map/all_gather | solution.py:335
  1695.1 35.8 copy-start.238
  1695.3 35.7 copy-start.220
  1695.5 35.5 copy-start.145
  1696.2 34.7 copy-start.151
  1699.9 381.4 %reduce-scatter.17.cloned.1.call-start = ((), (), s32[]{:S(2)}) async-start(), calls=%async_computation.16 | async-start | bytes 2228224 | tf_op jit(solution)/shard_map/reduce_scatter | solution.py:404
  1734.6 53.2 %copy-start.173 = (f32[2,4,64]{2,1,0:T(4,128)}, f32[2,4,64]{2,1,0:T(4,128)S(1)}, u32[]{:S(2)}) copy-start(f32[2,4,64]{2,1,0:T(4,128)S(1)} %fusion.123) | copy-start | bytes 6148
  1801.5 50.7 %copy-start.30 = (f32[64,2048]{1,0:T(8,128)}, f32[64,2048]{1,0:T(8,128)S(1)}, u32[]{:S(2)}) copy-start(f32[64,2048]{1,0:T(8,128)S(1)} %get-tuple-element.281) | copy-start | bytes 1572868
  1801.5 31.5 copy-start.214
  1941.3 220.8 %reduce-scatter.25.cloned.1.call-start = ((), (), s32[]{:S(2)}) async-start(), calls=%async_computation.31 | async-start | bytes 2228224
  1960.7 381.9 %reduce-scatter.19.cloned.1.call-start = ((), (), s32[]{:S(2)}) async-start(), calls=%async_computation.17 | async-start | bytes 2228224 | tf_op jit(solution)/shard_map/reduce_scatter | solution.py:404
  1963.7 52.5 %copy-start.223 = (f32[64]{0:T(128)S(1)}, f32[64]{0:T(128)}, u32[]{:S(2)}) copy-start(f32[64]{0:T(128)} %get-tuple-element.71) | copy-start | bytes 772
  1963.7 58.8 %copy-start.183 = (f32[64]{0:T(128)S(1)}, f32[64]{0:T(128)}, u32[]{:S(2)}) copy-start(f32[64]{0:T(128)} %fusion.406) | copy-start | bytes 772
  2018.5 179.2 %copy-start.188 = (f32[64]{0:T(128)}, f32[64]{0:T(128)S(1)}, u32[]{:S(2)}) copy-start(f32[64]{0:T(128)S(1)} %fusion.418) | copy-start | bytes 772
  2097.5 79.8 %copy-start.197 = (f32[64]{0:T(128)S(1)}, f32[64]{0:T(128)}, u32[]{:S(2)}) copy-start(f32[64]{0:T(128)} %fusion.405) | copy-start | bytes 772
  2185.5 16.3 collective-permute-start.2
  2274.4 148.8 %reduce-scatter.27.cloned.1.call-start = ((), (), s32[]{:S(2)}) async-start(), calls=%async_computation.32 | async-start | bytes 2228224
  2282.8 208.6 %all-gather.58.cloned.1.call-start = ((), (), s32[]{:S(2)}) async-start(), calls=%async_computation.29 | async-start | bytes 1114112 | tf_op jit(solution)/shard_map/all_gather | solution.py:334
  2283.4 264.9 %all-gather.60.cloned.1.call-start = ((), (), s32[]{:S(2)}) async-start(), calls=%async_computation.30 | async-start | bytes 1114112 | tf_op jit(solution)/shard_map/all_gather | solution.py:335
  2290.0 397.5 %reduce-scatter.21.cloned.1.call-start = ((), (), s32[]{:S(2)}) async-start(), calls=%async_computation.18 | async-start | bytes 2228224 | tf_op jit(solution)/shard_map/reduce_scatter | solution.py:404
  2345.4 92.8 %copy-start.38 = (f32[64,2048]{1,0:T(8,128)S(1)}, f32[64,2048]{1,0:T(8,128)}, u32[]{:S(2)}) copy-start(f32[64,2048]{1,0:T(8,128)} %copy-done.37) | copy-start | bytes 1572868
  2447.3 103.7 %collective-permute-start.3 = (bf16[64,2048]{1,0:T(8,128)(2,1)}, bf16[64,2048]{1,0:T(8,128)(2,1)}, u32[]{:S(2)}, u32[]{:S(2)}) collective-permute-start(bf16[64,2048]{1,0:T(8,128)(2,1)} %get-tuple-element.159), channel_id=1, source_target_pairs={{16,0},{17,1},{18,2},{19,3},{20,4},{21,5},{22,6},{23,7},{24,8},{25... | collective-permute-start | bytes 786440 | tf_op jit(solution)/shard_map/ppermute | solution.py:28
  2460.4 90.1 %copy-start.222 = (f32[64]{0:T(128)S(1)}, f32[64]{0:T(128)}, u32[]{:S(2)}) copy-start(f32[64]{0:T(128)} %get-tuple-element.155) | copy-start | bytes 772
  2460.4 90.6 %copy-start.203 = (f32[64]{0:T(128)S(1)}, f32[64]{0:T(128)}, u32[]{:S(2)}) copy-start(f32[64]{0:T(128)} %fusion.414) | copy-start | bytes 772
  2493.7 58.8 %copy-start.219 = (f32[64]{0:T(128)S(1)}, f32[64]{0:T(128)}, u32[]{:S(2)}) copy-start(f32[64]{0:T(128)} %get-tuple-element.66) | copy-start | bytes 772
  2493.7 58.8 %copy-start.27 = (f32[64,2048]{1,0:T(8,128)S(1)}, f32[64,2048]{1,0:T(8,128)}, u32[]{:S(2)}) copy-start(f32[64,2048]{1,0:T(8,128)} %copy-done.26) | copy-start | bytes 1572868
  2621.7 147.4 %reduce-scatter.29.cloned.1.call-start = ((), (), s32[]{:S(2)}) async-start(), calls=%async_computation.33 | async-start | bytes 2228224
  2627.2 222.2 %all-gather.44.cloned.1.call-start = ((), (), s32[]{:S(2)}) async-start(), calls=%async_computation.22 | async-start | bytes 1114112 | tf_op jit(solution)/shard_map/all_gather | solution.py:515
  2628.8 558.7 %all-gather.40.cloned.1.call-start = ((), (), s32[]{:S(2)}) async-start(), calls=%async_computation.20 | async-start | bytes 8912896 | tf_op jit(solution)/shard_map/all_gather | solution.py:506
  2630.7 612.7 %all-gather.42.cloned.1.call-start = ((), (), s32[]{:S(2)}) async-start(), calls=%async_computation.21 | async-start | bytes 8912896 | tf_op jit(solution)/shard_map/all_gather | solution.py:510
  2632.7 1276.4 %reduce-scatter.23.cloned.1.call-start = ((), (), s32[]{:S(2)}) async-start(), calls=%async_computation.19 | async-start | bytes 50135040 | tf_op jit(solution)/shard_map/reduce_scatter | solution.py:492
  2689.6 82.9 %copy-start.34 = (f32[64,2048]{1,0:T(8,128)S(1)}, f32[64,2048]{1,0:T(8,128)}, u32[]{:S(2)}) copy-start(f32[64,2048]{1,0:T(8,128)} %copy-done.33) | copy-start | bytes 1572868
  2689.7 82.9 %copy-start.187 = (f32[64]{0:T(128)S(1)}, f32[64]{0:T(128)}, u32[]{:S(2)}) copy-start(f32[64]{0:T(128)} %copy-done.186) | copy-start | bytes 772
  2837.7 334.2 %all-to-all-start = ((bf16[3,128,8192]{1,0,2:T(4,128)(2,1)}), bf16[3,128,8192]{1,0,2:T(4,128)(2,1)}, u32[]{:S(2)}, u32[]{:S(2)}) async-start(bf16[3,128,8192]{1,0,2:T(4,128)(2,1)} %copy.491), calls=%async_computation.5 | async-start | bytes 16777216 | tf_op jit(solution)/shard_map/all_to_all | solution.py:502
  2852.4 318.7 %copy-start.75 = (bf16[3,64,2048]{2,1,0:T(8,128)(2,1)S(1)}, bf16[3,64,2048]{2,1,0:T(8,128)(2,1)}, u32[]{:S(2)}) copy-start(bf16[3,64,2048]{2,1,0:T(8,128)(2,1)} %get-tuple-element.219) | copy-start | bytes 2359300
  3187.5 55.9 %copy-start.82 = (bf16[1,16,128,512]{3,2,1,0:T(8,128)(2,1)S(1)}, bf16[1,16,128,512]{3,2,1,0:T(8,128)(2,1)}, u32[]{:S(2)}) copy-start(bf16[1,16,128,512]{3,2,1,0:T(8,128)(2,1)} %copy.494) | copy-start | bytes 6291460
  3260.4 648.7 %copy-start.1 = (bf16[1,4096,256]{2,1,0:T(8,128)(2,1)S(1)}, bf16[1,4096,256]{2,1,0:T(8,128)(2,1)}, u32[]{:S(2)}) copy-start(bf16[1,4096,256]{2,1,0:T(8,128)(2,1)} %param.15) | copy-start | bytes 6291460
  (213 other events, 1332.5 us)
Sparse Core Ops, SparseCore 0:
  10.8 256.6 all-gather.45
  280.6 52.6 all-gather.29
  336.7 54.0 all-gather.27
  393.5 984.5 all-gather.47
  1380.2 64.2 reduce-scatter.14
  1476.2 55.4 all-gather.33
  1534.4 54.0 all-gather.31
  1676.3 52.2 all-gather.37
  1731.4 54.0 all-gather.35
  1788.1 54.0 all-gather.49
  1845.0 54.0 all-gather.51
  1901.7 54.0 all-gather.53
  1958.6 54.0 all-gather.55
  2014.9 66.3 reduce-scatter.16
  2083.9 78.0 reduce-scatter.24
  2274.5 68.1 reduce-scatter.18
  2345.3 77.7 reduce-scatter.26
  2425.8 65.5 all-gather.57
  2494.1 54.0 all-gather.59
  2621.8 65.5 reduce-scatter.20
  2690.3 78.7 reduce-scatter.28
  2771.9 64.8 all-gather.43
  2839.5 283.4 all-gather.39
  3125.7 117.6 all-gather.41
  3250.1 658.9 reduce-scatter.22
where the time goes:
time: 3930 us; the launch traced here: 3920 us
  waiting for transfers between devices  2570 us (65%)
  matrix products  479 us (12%)
  blocking collectives  385 us (10%)
  local copies, waits for them, and re-layouts  243 us (6%)
  other arithmetic  176 us (4%)
  starting transfers between devices  40.6 us (1%)
    all_gather x1, waiting for transfers between devices, per_device(): lax.all_gather(ff_weight[0], 'shard', axis=1, tiled=True)  977 us
    reduce_scatter x1, waiting for transfers between devices, per_device(): lax.psum_scatter(attn_term, 'shard', scatter_dimension=0, tiled=True)  636 us
    unnamed x2, blocking collectives  360 us
    unnamed x28, waiting for transfers between devices  207 us
    all_gather x1, waiting for transfers between devices, per_device(): lax.all_gather(attn_weight[0], 'shard', axis=0, tiled=True)  198 us
    all_gather x3, waiting for transfers between devices, per_device(): forward_value_all = lax.all_gather(value_local, 'shard', axis=0, tiled=True)  155 us
    dot_general x18, matrix products, contract_last(): lax.dot_general(left_side, right_side, (((1,), (1,)), ((), ())), preferre...  124 us
    reduce_scatter x3, waiting for transfers between devices, per_device(): lax.psum_scatter(grad_values_all, 'shard', scatter_dimension=0, tiled=True)  121 us
  transfers between devices with their start and end apart: 30, of which 22 were waited for; matrix products, arithmetic and copies ran while one was open for 15% of the time, Pallas kernels for 0%

commit v1 on v0

v1 whole, which is shorter than its diff:
```python
import itertools
import math
from functools import partial

import jax
import jax.numpy as jnp
from jax import lax
from jax.sharding import PartitionSpec as P

D = 2048
HEADS = 8
KV_HEADS = 2
HEAD_DIM = 256
RANK = 64
PLD = 256
HALF = D // 2
QW = HEADS * HEAD_DIM
KW = KV_HEADS * HEAD_DIM
IN_ROWS = QW + 2 * KW + RANK
OUT_START = IN_ROWS + PLD
LAUREL_START = OUT_START + QW
SIDE_START = LAUREL_START + RANK

EPS = 1e-06
ROPE_BASE = 10000.0
INV_ROOT2 = 0.7071067811865476
MASKED = -1e30
SCALE = HEAD_DIM ** (-0.5)
BF = jnp.bfloat16
F32 = jnp.float32

ZXY = (0, 2, 1)
ZYX = (0, 1, 2)
ZY = (0, 1)
X_ONLY = (2,)


def chip_dims(n):
    side = math.isqrt(n // 4)
    return (4, side, side)


def ring_pairs(n, dim, step):
    sizes = chip_dims(n)
    stride = (sizes[1] * sizes[2], sizes[2], 1)[dim]
    pairs = []
    for i in range(n):
        place = (i // stride) % sizes[dim]
        pairs.append((i, i + ((place + step) % sizes[dim] - place) * stride))
    return pairs


def hop(value, n, dim, step):
    return lax.ppermute(value, "shard", ring_pairs(n, dim, step))


def swap_cores(value):
    return lax.ppermute(value, "section", [(0, 1), (1, 0)])


def offsets_of(n, order):
    sizes = chip_dims(n)
    return list(itertools.product(*[range(sizes[d]) for d in order]))


def tree(n, order):
    edges = []
    for offset in offsets_of(n, order):
        if sum(offset) == 0:
            continue
        last = max(i for i, steps in enumerate(offset) if steps > 0)
        parent = tuple(steps - (i == last) for i, steps in enumerate(offset))
        edges.append((sum(offset), offset, parent, order[last]))
    return edges


def source_index(me, n, order, offset):
    sizes = chip_dims(n)
    strides = (sizes[1] * sizes[2], sizes[2], 1)
    index = me
    for dim, steps in zip(order, offset):
        place = (me // strides[dim]) % sizes[dim]
        index = index + ((place - steps) % sizes[dim] - place) * strides[dim]
    return index


def gather_tree(pieces, n, fence=True):
    trees = [tree(n, order) for _, order in pieces]
    found = [{(0,) * len(order): block} for block, order in pieces]
    held = [dict(blocks) for blocks in found]
    rounds = max(edge[0] for edges in trees for edge in edges)
    for number in range(1, rounds + 1):
        if fence and number > 1:
            keys = [(p, offset) for p in range(len(pieces)) for offset in held[p]]
            values = lax.optimization_barrier([held[p][offset] for p, offset in keys])
            for (p, offset), value in zip(keys, values):
                held[p][offset] = value
        for p, edges in enumerate(trees):
            for edge_round, offset, parent, dim in edges:
                if edge_round == number:
                    value = hop(held[p][parent], n, dim, 1)
                    found[p][offset] = value
                    held[p][offset] = value
    return found


def scatter_tree(pieces, n, fence=False):
    trees = [tree(n, order) for _, order in pieces]
    sums = [dict(terms) for terms, _ in pieces]
    rounds = max(edge[0] for edges in trees for edge in edges)
    for number in range(rounds, 0, -1):
        todo = [
            (p, offset, parent, dim)
            for p, edges in enumerate(trees)
            for edge_round, offset, parent, dim in edges
            if edge_round == number
        ]
        sends = [sums[p][offset].astype(BF) for p, offset, _, _ in todo]
        if fence:
            sends = lax.optimization_barrier(sends)
        for (p, offset, parent, dim), send in zip(todo, sends):
            sums[p][parent] = sums[p][parent].astype(F32) + hop(send, n, dim, -1).astype(F32)
    return [total[(0,) * len(order)] for total, (_, order) in zip(sums, pieces)]


def rms_norm(values):
    return values * lax.rsqrt(jnp.mean(values * values, axis=-1, keepdims=True) + EPS)


def scaled_norm(values, gain_vec):
    return rms_norm(values) * gain_vec


def rope_tables(positions):
    half_width = HEAD_DIM // 2
    frequency = ROPE_BASE ** (-jnp.arange(half_width, dtype=F32) * (2.0 / HEAD_DIM))
    angles = positions.astype(F32)[:, None] * frequency[None, :]
    return (jnp.cos(angles), jnp.sin(angles))


def rotate(vectors, cosine_part, sine_part):
    half_width = vectors.shape[-1] // 2
    first_half = vectors[..., :half_width]
    second_half = vectors[..., half_width:]
    cosine_rows = cosine_part[:, None, :]
    sine_rows = sine_part[:, None, :]
    return jnp.concatenate(
        [
            first_half * cosine_rows - second_half * sine_rows,
            second_half * cosine_rows + first_half * sine_rows,
        ],
        axis=-1,
    )


def split_heads(projected_in, query_gain, key_gain, cosine_part, sine_part):
    row_count = projected_in.shape[0]
    queries = projected_in[:, :QW].reshape(row_count, HEADS, HEAD_DIM)
    key_heads = projected_in[:, QW : QW + KW].reshape(row_count, KV_HEADS, HEAD_DIM)
    value_heads = projected_in[:, QW + KW : QW + 2 * KW].reshape(row_count, KV_HEADS, HEAD_DIM)
    latent = projected_in[:, QW + 2 * KW :]
    queries = rotate(rms_norm(queries) * query_gain, cosine_part, sine_part)
    key_heads = rotate(rms_norm(key_heads) * key_gain, cosine_part, sine_part)
    value_heads = rms_norm(value_heads)
    return (queries, key_heads, value_heads, latent)


def join_piece(hidden_in, normed, attended, laurel_raw, gain_laurel, gain_attn, gain_ffin):
    joined = (
        hidden_in + rms_norm(attended) * gain_attn + normed + rms_norm(laurel_raw) * gain_laurel
    ) * INV_ROOT2
    return (joined, rms_norm(joined) * gain_ffin)


def gated_gelu(gate_pre, up_pre):
    return jax.nn.gelu(gate_pre, approximate=True) * up_pre


def add_branch(residual, branch, gain_out):
    return residual + rms_norm(branch) * gain_out


def dot(left_side, right_side):
    return jnp.dot(left_side, right_side, preferred_element_type=F32)


def dot_rows(left_side, right_side):
    return lax.dot_general(
        left_side, right_side, (((1,), (1,)), ((), ())), preferred_element_type=F32
    )


def dot_first(left_side, right_side):
    return lax.dot_general(
        left_side, right_side, (((0,), (0,)), ((), ())), preferred_element_type=F32
    )


def halves(value, core):
    left, right = value[..., :HALF], value[..., HALF:]
    return jnp.where(core == 0, left, right), jnp.where(core == 0, right, left)


def rejoin(own, other, core):
    return jnp.concatenate(
        [jnp.where(core == 0, own, other), jnp.where(core == 0, other, own)], axis=-1
    )


def rows_product(value, rows, start, stop, core):
    own, other = halves(value, core)
    return dot_rows(own, rows[0][start:stop]) + dot_rows(other, rows[1][start:stop])


def back_product(value, rows, start, stop, core):
    return rejoin(dot(value, rows[0][start:stop]), dot(value, rows[1][start:stop]), core)


def per_device(tokens, cotangent, block_ids, token_ids, attn_weight, ff_weight, gains, table):
    core = lax.axis_index("section")
    me = lax.axis_index("shard")
    n = lax.axis_size("shard")
    seq = tokens.shape[1]
    rows_dev = attn_weight.shape[1]
    units = ff_weight.shape[2]
    gains_dev = gains.shape[1]
    vocab_dev = table.shape[1]
    side = chip_dims(n)[2]
    plane = n // side

    def by_layer(mine, theirs):
        return (jnp.where(core == 0, mine, theirs), jnp.where(core == 0, theirs, mine))

    all_ids = lax.all_gather(token_ids.reshape(-1), "shard", axis=0, tiled=True)
    one_hot = (
        (all_ids - me * vocab_dev)[:, None] == jnp.arange(vocab_dev, dtype=jnp.int32)[None, :]
    ).astype(BF)
    looked_up = dot(one_hot, table[0]).astype(BF)
    looked_up = lax.psum_scatter(looked_up, "shard", scatter_dimension=0, tiled=True)
    looked_up = looked_up.reshape(2, seq, PLD)
    side_mine = jnp.where(core == 0, looked_up[0], looked_up[1])
    side_theirs = swap_cores(jnp.where(core == 0, looked_up[1], looked_up[0]))
    side_inputs = [value.astype(F32) for value in by_layer(side_mine, side_theirs)]

    own_half, other_half = halves(attn_weight[0], core)
    attn_blocks = by_layer(own_half, swap_cores(other_half))
    gain_blocks = by_layer(gains[0], swap_cores(gains[0]))
    gain_rows_block = jnp.zeros((8, HALF), BF)
    gain_rows_block = gain_rows_block.at[0, :gains_dev].set(gain_blocks[0])
    gain_rows_block = gain_rows_block.at[1, :gains_dev].set(gain_blocks[1])
    first = (rows_dev // 2 + 7) // 8 * 8
    second = rows_dev - first
    orders = (ZXY, ZYX)
    pieces = [
        (attn_blocks[0][:first], orders[0]),
        (jnp.concatenate([attn_blocks[0][first:], gain_rows_block], axis=0), orders[1]),
    ]
    found = gather_tree(pieces, n)
    row_buffers = [jnp.zeros((n, rows_dev, HALF), BF), jnp.zeros((n, rows_dev, HALF), BF)]
    gain_buffer = jnp.zeros((n, 8, HALF), BF)
    for p, (start, count) in enumerate(((0, first), (first, second))):
        for offset, block in found[p].items():
            source = source_index(me, n, orders[p], offset)
            where_to = (source, jnp.int32(start), jnp.int32(0))
            sent = swap_cores(block[:count])
            row_buffers[0] = lax.dynamic_update_slice(row_buffers[0], block[None, :count], where_to)
            row_buffers[1] = lax.dynamic_update_slice(row_buffers[1], sent[None], where_to)
            if p == 1:
                gain_buffer = lax.dynamic_update_slice(
                    gain_buffer, block[None, count:], (source, jnp.int32(0), jnp.int32(0))
                )
    rows_0 = [buffer.reshape(n * rows_dev, HALF) for buffer in row_buffers]
    rows_1_own = lax.all_gather(attn_blocks[1], "shard", axis=0, tiled=True)
    rows_1 = [rows_1_own, swap_cores(rows_1_own)]
    attn_rows = (rows_0, rows_1)
    layer_gains = [
        gain_buffer[:, layer, :gains_dev].reshape(n * gains_dev).astype(F32) for layer in range(2)
    ]

    ff_own = by_layer(ff_weight[0], swap_cores(ff_weight[0]))
    half_units = units // 2

    def ff_units(layer):
        mine = lax.dynamic_slice_in_dim(ff_own[layer], core * half_units, half_units, 1)
        parts = [ff_own[layer]]
        current = mine
        for _ in range(side - 1):
            current = hop(current, n, 2, 1)
            parts += [current, swap_cores(current)]
        return jnp.concatenate(parts, axis=1)

    ff_all = [ff_units(0), ff_units(1)]

    positions = me * seq + jnp.arange(seq, dtype=jnp.int32)
    cosine_part, sine_part = rope_tables(positions)
    head_split = partial(split_heads, cosine_part=cosine_part, sine_part=sine_part)
    key_offsets = offsets_of(n, ZXY)
    sources = jnp.stack([source_index(me, n, ZXY, offset) for offset in key_offsets])
    blocks = jnp.where(core == 0, block_ids[0], block_ids[1]).reshape(n, seq)
    key_blocks = jnp.take(blocks, sources, axis=0).reshape(-1)
    allowed = key_blocks[None, :] <= key_blocks[:seq, None]
    hidden_b = jnp.where(core == 0, tokens[0], tokens[1])

    def plane_gather(value):
        found = gather_tree([(value, ZY)], n, fence=False)[0]
        return jnp.concatenate([found[offset] for offset in offsets_of(n, ZY)], axis=0)

    def plane_scatter(value):
        terms = {
            offset: value[i * seq : (i + 1) * seq] for i, offset in enumerate(offsets_of(n, ZY))
        }
        return scatter_tree([(terms, ZY)], n)[0]

    def forward(layer, hidden_b):
        rows = attn_rows[layer]
        gain_flat = layer_gains[layer]
        gain_rows = gain_flat[: 6 * D].reshape(6, D)
        query_gain = gain_flat[6 * D : 6 * D + HEAD_DIM]
        key_gain = gain_flat[6 * D + HEAD_DIM :]
        hidden_in = hidden_b.astype(F32)
        normed = scaled_norm(hidden_in, gain_rows[0])
        normed_b = normed.astype(BF)
        projected_in = rows_product(normed_b, rows, 0, IN_ROWS, core)
        queries, key_heads, value_heads, latent = head_split(projected_in, query_gain, key_gain)
        queries_b = queries.astype(BF).reshape(seq, KV_HEADS, HEADS // KV_HEADS, HEAD_DIM)
        local = jnp.concatenate(
            [key_heads.reshape(seq, KW), value_heads.reshape(seq, KW)], axis=1
        ).astype(BF)
        found = gather_tree([(local, ZXY)], n, fence=False)[0]
        key_value = jnp.concatenate([found[offset] for offset in key_offsets], axis=0)
        keys_b = key_value[:, :KW].reshape(-1, KV_HEADS, HEAD_DIM)
        values_b = key_value[:, KW:].reshape(-1, KV_HEADS, HEAD_DIM)
        scores = (
            jnp.einsum("qkgd,jkd->kgqj", queries_b, keys_b, preferred_element_type=F32) * SCALE
        )
        scores = jnp.where(allowed, scores, MASKED)
        row_max = jnp.max(scores, axis=-1, keepdims=True)
        exponentials = jnp.exp(scores - row_max)
        probabilities = exponentials / jnp.sum(exponentials, axis=-1, keepdims=True)
        mixed_b = (
            jnp.einsum(
                "kgqj,jkd->qkgd", probabilities.astype(BF), values_b, preferred_element_type=F32
            )
            .reshape(seq, QW)
            .astype(BF)
        )
        attended = back_product(mixed_b, rows, OUT_START, LAUREL_START, core)
        latent_b = latent.astype(BF)
        laurel_raw = back_product(latent_b, rows, LAUREL_START, SIDE_START, core)
        joined, prenorm = join_piece(
            hidden_in, normed, attended, laurel_raw, gain_rows[1], gain_rows[2], gain_rows[3]
        )
        prenorm_all = plane_gather(prenorm.astype(BF))
        weights = ff_all[layer]
        gate = dot_rows(prenorm_all, weights[0])
        up = dot_rows(prenorm_all, weights[1])
        hidden_ff_b = gated_gelu(gate, up).astype(BF)
        down_out = plane_scatter(dot(hidden_ff_b, weights[2]))
        settled = add_branch(joined, down_out, gain_rows[4])
        settled_b = settled.astype(BF)
        side_gate = rows_product(settled_b, rows, IN_ROWS, OUT_START, core)
        gated_b = gated_gelu(side_gate, side_inputs[layer]).astype(BF)
        projected = back_product(gated_b, rows, SIDE_START, SIDE_START + PLD, core)
        layer_out_b = add_branch(settled, projected, gain_rows[5]).astype(BF)
        return layer_out_b, dict(
            hidden_in=hidden_in,
            normed=normed,
            normed_b=normed_b,
            projected_in=projected_in,
            queries_b=queries_b,
            keys_b=keys_b,
            values_b=values_b,
            probabilities=probabilities,
            mixed_b=mixed_b,
            attended=attended,
            latent_b=latent_b,
            laurel_raw=laurel_raw,
            joined=joined,
            prenorm_all=prenorm_all,
            gate=gate,
            up=up,
            hidden_ff_b=hidden_ff_b,
            down_out=down_out,
            settled=settled,
            settled_b=settled_b,
            side_gate=side_gate,
            gated_b=gated_b,
            projected=projected,
        )

    def both(left, right):
        own, other = halves(right, core)
        lefts = jnp.concatenate([left, swap_cores(left)], axis=0)
        rights = jnp.concatenate([own, swap_cores(other)], axis=0)
        return dot_first(lefts, rights).astype(BF)

    def backward(layer, kept, grad_out_b):
        rows = attn_rows[layer]
        weights = ff_all[layer]
        gain_flat = layer_gains[layer]
        gain_rows = gain_flat[: 6 * D].reshape(6, D)
        query_gain = gain_flat[6 * D : 6 * D + HEAD_DIM]
        key_gain = gain_flat[6 * D + HEAD_DIM :]
        grad_out = grad_out_b.astype(F32)
        grad_settled, grad_projected, grad_gain5 = jax.vjp(
            add_branch, kept["settled"], kept["projected"], gain_rows[5]
        )[1](grad_out)
        grad_projected_b = grad_projected.astype(BF)
        grad_gated = rows_product(grad_projected_b, rows, SIDE_START, SIDE_START + PLD, core)
        grad_side_gate, grad_side = jax.vjp(gated_gelu, kept["side_gate"], side_inputs[layer])[1](
            grad_gated
        )
        grad_side_gate_b = grad_side_gate.astype(BF)
        grad_settled = grad_settled + back_product(
            grad_side_gate_b, rows, IN_ROWS, OUT_START, core
        )
        grad_joined, grad_down, grad_gain4 = jax.vjp(
            add_branch, kept["joined"], kept["down_out"], gain_rows[4]
        )[1](grad_settled)
        grad_down_all = plane_gather(grad_down.astype(BF))
        grad_hidden_ff = dot_rows(grad_down_all, weights[2])
        grad_gate, grad_up = jax.vjp(gated_gelu, kept["gate"], kept["up"])[1](grad_hidden_ff)
        grad_gate_b, grad_up_b = grad_gate.astype(BF), grad_up.astype(BF)
        grad_prenorm = plane_scatter(dot(grad_gate_b, weights[0]) + dot(grad_up_b, weights[1]))
        ff_term = jnp.stack(
            [
                dot_first(grad_gate_b, kept["prenorm_all"]).astype(BF),
                dot_first(grad_up_b, kept["prenorm_all"]).astype(BF),
                dot_first(kept["hidden_ff_b"], grad_down_all).astype(BF),
            ]
        )
        passed = None
        for steps in range(side - 1, 0, -1):
            start = units + 2 * (steps - 1) * half_units
            near = ff_term[:, start : start + half_units].astype(F32)
            far = swap_cores(ff_term[:, start + half_units : start + 2 * half_units])
            term = near + far.astype(F32)
            if passed is not None:
                term = term + passed.astype(F32)
            passed = hop(term.astype(BF), n, 2, -1)
        ff_sum = (ff_term[:, :units], passed)
        join_pull = jax.vjp(
            join_piece,
            kept["hidden_in"],
            kept["normed"],
            kept["attended"],
            kept["laurel_raw"],
            gain_rows[1],
            gain_rows[2],
            gain_rows[3],
        )[1]
        grad_hidden, grad_normed, grad_attended, grad_laurel, grad_gain1, grad_gain2, grad_gain3 = (
            join_pull((grad_joined, grad_prenorm))
        )
        grad_attended_b = grad_attended.astype(BF)
        grad_laurel_b = grad_laurel.astype(BF)
        grad_mixed_b = rows_product(grad_attended_b, rows, OUT_START, LAUREL_START, core).astype(BF)
        grad_latent = rows_product(grad_laurel_b, rows, LAUREL_START, SIDE_START, core)
        grad_mixed_heads = grad_mixed_b.reshape(seq, KV_HEADS, HEADS // KV_HEADS, HEAD_DIM)
        probabilities = kept["probabilities"]
        grad_probs = jnp.einsum(
            "qkgd,jkd->kgqj", grad_mixed_heads, kept["values_b"], preferred_element_type=F32
        )
        row_dot = jnp.sum(grad_probs * probabilities, axis=-1, keepdims=True)
        grad_scores_b = (probabilities * (grad_probs - row_dot)).astype(BF)
        grad_queries = (
            jnp.einsum("kgqj,jkd->qkgd", grad_scores_b, kept["keys_b"], preferred_element_type=F32)
            * SCALE
        )
        grad_keys_all = (
            jnp.einsum(
                "kgqj,qkgd->jkd", grad_scores_b, kept["queries_b"], preferred_element_type=F32
            )
            * SCALE
        )
        grad_values_all = jnp.einsum(
            "kgqj,qkgd->jkd",
            probabilities.astype(BF),
            grad_mixed_heads,
            preferred_element_type=F32,
        )
        grad_key_value = jnp.concatenate(
            [grad_keys_all.reshape(-1, KW), grad_values_all.reshape(-1, KW)], axis=1
        )
        terms = {
            offset: grad_key_value[i * seq : (i + 1) * seq] for i, offset in enumerate(key_offsets)
        }
        grad_local = scatter_tree([(terms, ZXY)], n)[0]
        head_pull = jax.vjp(head_split, kept["projected_in"], query_gain, key_gain)[1]
        grad_projected_in, grad_query_gain, grad_key_gain = head_pull(
            (
                grad_queries.reshape(seq, HEADS, HEAD_DIM),
                grad_local[:, :KW].reshape(seq, KV_HEADS, HEAD_DIM),
                grad_local[:, KW:].reshape(seq, KV_HEADS, HEAD_DIM),
                grad_latent,
            )
        )
        grad_projected_in_b = grad_projected_in.astype(BF)
        grad_normed = grad_normed + back_product(grad_projected_in_b, rows, 0, IN_ROWS, core)
        grad_front, grad_gain0 = jax.vjp(scaled_norm, kept["hidden_in"], gain_rows[0])[1](
            grad_normed
        )
        grad_hidden_b = (grad_hidden + grad_front).astype(BF)
        gain_vec = jnp.concatenate(
            [
                grad_gain0,
                grad_gain1,
                grad_gain2,
                grad_gain3,
                grad_gain4,
                grad_gain5,
                grad_query_gain,
                grad_key_gain,
            ]
        )
        attn_term = jnp.concatenate(
            [
                both(grad_projected_in_b, kept["normed_b"]),
                both(grad_side_gate_b, kept["settled_b"]),
                both(kept["mixed_b"], grad_attended_b),
                both(kept["latent_b"], grad_laurel_b),
                both(kept["gated_b"], grad_projected_b),
            ],
            axis=0,
        )
        return grad_hidden_b, attn_term, ff_sum, gain_vec, grad_side.astype(BF)

    out_0, kept_0 = forward(0, hidden_b)
    out_1, kept_1 = forward(1, out_0)
    top = jnp.where(core == 0, cotangent[0], cotangent[1])
    grad_1, attn_term_1, ff_sum_1, gain_vec_1, grad_side_1 = backward(1, kept_1, top)
    attn_sum_1 = lax.psum_scatter(attn_term_1, "shard", scatter_dimension=0, tiled=True)
    grad_0, attn_term_0, ff_sum_0, gain_vec_0, grad_side_0 = backward(0, kept_0, grad_1)

    attn_terms = attn_term_0.reshape(n, rows_dev, HALF)
    gain_terms = jnp.stack(
        [gain_vec_0.reshape(n, gains_dev), gain_vec_1.reshape(n, gains_dev)], axis=1
    )
    gain_terms = jnp.pad(gain_terms, ((0, 0), (0, 6), (0, HALF - gains_dev))).astype(BF)
    piece_terms = [{}, {}]
    for p in range(2):
        for offset in offsets_of(n, orders[p]):
            source = source_index(me, n, orders[p], offset)
            block = lax.dynamic_index_in_dim(attn_terms, source, 0, keepdims=False)
            if p == 0:
                piece_terms[0][offset] = block[:first]
            else:
                gain_block = lax.dynamic_index_in_dim(gain_terms, source, 0, keepdims=False)
                piece_terms[1][offset] = jnp.concatenate([block[first:], gain_block], axis=0)
    sum_first, sum_second = scatter_tree(
        [(piece_terms[0], orders[0]), (piece_terms[1], orders[1])], n
    )
    attn_sum_0 = jnp.concatenate([sum_first, sum_second[:second]], axis=0)
    attn_sum_1 = attn_sum_1.astype(F32)
    attn_keep = jnp.where(core == 0, attn_sum_0, attn_sum_1)
    attn_other = swap_cores(jnp.where(core == 0, attn_sum_1, attn_sum_0))
    attn_grad = rejoin(attn_keep, attn_other, core)
    gain_sums = sum_second[second : second + 2, :gains_dev]
    gain_grad = jnp.where(core == 0, gain_sums[0], gain_sums[1]) + swap_cores(
        jnp.where(core == 0, gain_sums[1], gain_sums[0])
    )

    def whole_ff(ff_sum):
        base, passed = ff_sum
        zeros = jnp.zeros((3, units - half_units, D), BF)
        placed = jnp.where(
            core == 0,
            jnp.concatenate([passed, zeros], axis=1),
            jnp.concatenate([zeros, passed], axis=1),
        )
        return base.astype(F32) + placed.astype(F32)

    whole_0, whole_1 = whole_ff(ff_sum_0), whole_ff(ff_sum_1)
    ff_grad = jnp.where(core == 0, whole_0, whole_1) + swap_cores(
        jnp.where(core == 0, whole_1, whole_0).astype(BF)
    ).astype(F32)

    side_keep = jnp.where(core == 0, grad_side_0, grad_side_1)
    side_other = swap_cores(jnp.where(core == 0, grad_side_1, grad_side_0))
    side_both = jnp.concatenate(
        [jnp.where(core == 0, side_keep, side_other), jnp.where(core == 0, side_other, side_keep)],
        axis=0,
    )
    side_all = lax.all_gather(side_both, "shard", axis=0, tiled=True)
    table_grad = dot_first(one_hot, side_all)

    def outputs_of(value_0, value_1):
        keep = jnp.where(core == 0, value_0, value_1)
        other = swap_cores(jnp.where(core == 0, value_1, value_0))
        return jnp.stack([jnp.where(core == 0, keep, other), jnp.where(core == 0, other, keep)])

    return (
        outputs_of(out_0, out_1)[None],
        outputs_of(grad_0, grad_1)[None],
        attn_grad[None],
        ff_grad[None],
        gain_grad[None],
        table_grad[None],
    )


def solution(mesh):
    placed = (
        P(None, "shard", None),
        P(None, "shard", None),
        P(),
        P(None, "shard"),
        P("section", "shard", None),
        P("section", None, "shard", None),
        P("section", "shard"),
        P("section", "shard", None),
    )
    return jax.shard_map(
        per_device,
        mesh=mesh,
        in_specs=placed,
        out_specs=(
            P("section", None, "shard", None),
            P("section", None, "shard", None),
            P("section", "shard", None),
            P("section", None, "shard", None),
            P("section", "shard"),
            P("section", "shard", None),
        ),
        check_vma=False,
    )
```

time: 3930 us -> 1440 us (0.37)
  waiting for transfers between devices: 2570 us -> 526 us
  blocking collectives: 385 us -> 25.4 us
  starting transfers between devices: 40.6 us -> 299 us
  matrix products: 479 us -> 223 us
  local copies, waits for them, and re-layouts: 243 us -> 170 us
    all_gather x17 -> x2, waiting for transfers between devices: 1590 us -> 0.01 us  [the longest x1 0.01 us: per_device(): rows_1_own = lax.all_gather(attn_blocks[1], 'shard', axis=0, tiled=True)]
    reduce_scatter x5 -> x2, waiting for transfers between devices: 763 us -> 3.45 us  [the longest x1 3.45 us: per_device(): lax.psum_scatter(looked_up, 'shard', scatter_dimension=0, tiled=True)]
    ppermute x4 -> x247, waiting for transfers between devices: 14.5 us -> 522 us  [the longest x180 506 us: hop(): return lax.ppermute(value, 'shard', ring_pairs(n, dim, step))]
    unnamed x2 -> x0, blocking collectives: 360 us -> none
    ppermute x4 -> x247, starting transfers between devices: 28.6 us -> 299 us  [the longest x180 157 us: hop(): return lax.ppermute(value, 'shard', ring_pairs(n, dim, step))]
    dot_general x70 -> x80, matrix products: 479 us -> 217 us  [the longest x26 78.5 us: dot_rows(): lax.dot_general(left_side, right_side, (((1,), (1,)), ((), ())), preferre...]
    unnamed x28 -> x4, waiting for transfers between devices: 207 us -> 0.07 us
    dynamic_update_slice x43 -> x0, other arithmetic: 45.3 us -> none  [store_slot(): lax.dynamic_update_index_in_dim(buffer_array, item_array, slot_index, 0)]
  transfers between devices with their start and end apart: 30 -> 251, of which waited for: 22 -> 93; matrix products, arithmetic and copies ran while one was open for 15% -> 36% of each run, Pallas kernels for 0% -> 0%
where the time goes in v1:
time: 1440 us; the launch traced here: 1430 us
  waiting for transfers between devices  526 us (37%)
  starting transfers between devices  299 us (21%)
  matrix products  223 us (15%)
  local copies, waits for them, and re-layouts  170 us (12%)
  other arithmetic  164 us (11%)
  blocking collectives  25.4 us (2%)
  between operations  21 us (1%)
    ppermute x180, waiting for transfers between devices, hop(): return lax.ppermute(value, 'shard', ring_pairs(n, dim, step))  506 us
    ppermute x180, starting transfers between devices, hop(): return lax.ppermute(value, 'shard', ring_pairs(n, dim, step))  157 us
    ppermute x67, starting transfers between devices, swap_cores(): return lax.ppermute(value, 'section', [(0, 1), (1, 0)])  142 us
    dot_general x26, matrix products, dot_rows(): lax.dot_general(left_side, right_side, (((1,), (1,)), ((), ())), preferre...  78.5 us
    dot_general x27, matrix products, dot(): return jnp.dot(left_side, right_side, preferred_element_type=F32)  66.2 us
    dot_general x17, matrix products, dot_first(): lax.dot_general(left_side, right_side, (((0,), (0,)), ((), ())), preferre...  51.5 us
    dynamic_update_slice x32, local copies, waits for them, and re-layouts, per_device(): lax.dynamic_update_slice(row_buffers[0], block[None, :count], where_to)  45.3 us
    unnamed x753, local copies, waits for them, and re-layouts  29.9 us
  transfers between devices with their start and end apart: 251, of which 93 were waited for; matrix products, arithmetic and copies ran while one was open for 36% of the time, Pallas kernels for 0%

profile of v1, /device:TPU:27, one launch (start us, length us, event | category | flops | bytes accessed | tf_op | source)
XLA Modules:
  0.0 1428.5 jit_solution(14869921951415716108)
XLA Ops:
  13.2 25.4 %all-gather = s32[16,1,128]{2,1,0:T(1,128)S(1)} all-gather(s32[1,1,128]{2,1,0:T(1,128)S(1)} %reshape.1454), channel_id=1, replica_groups=mesh['section'=2,'shard'=16] {'shard'}, dimensions={0}, use_global_device_ids=true | all-gather | bytes 8704 | tf_op jit(solution)/shard_map/all_gather | solution.py:234
  60.0 9.4 collective-permute-start.32
  69.5 5.8 broadcast.716.clone.1
  85.2 6.0 broadcast.716.clone
  123.4 22.5 %collective-permute-done.16 = bf16[184,1024]{1,0:T(8,128)(2,1)S(1)} collective-permute-done((bf16[184,1024]{1,0:T(8,128)(2,1)S(1)}, bf16[184,1024]{1,0:T(8,128)(2,1)S(1)}, u32[]{:S(2)}, u32[]{:S(2)}) %collective-permute-start.16) | collective-permute-done | bytes 376864 | tf_op jit(solution)/shard_map/ppermute | solution.py:54
  148.5 4.8 collective-permute-start.36
  158.6 8.4 collective-permute-done.23
  179.6 28.7 %collective-permute-done.24 = bf16[184,1024]{1,0:T(8,128)(2,1)S(1)} collective-permute-done((bf16[184,1024]{1,0:T(8,128)(2,1)S(1)}, bf16[184,1024]{1,0:T(8,128)(2,1)S(1)}, u32[]{:S(2)}, u32[]{:S(2)}) %collective-permute-start.24) | collective-permute-done | bytes 376864 | tf_op jit(solution)/shard_map/ppermute | solution.py:54
  208.9 6.3 collective-permute-start.40
  215.3 9.9 collective-permute-done.27
  225.2 6.6 collective-permute-start.86
  234.3 8.2 collective-permute-done.42
  299.4 5.7 fusion.18
  337.9 8.0 broadcast_select_fusion
  373.6 37.7 %collective-permute-done.87 = bf16[3,256,2048]{2,1,0:T(8,128)(2,1)} collective-permute-done((bf16[3,256,2048]{2,1,0:T(8,128)(2,1)}, bf16[3,256,2048]{2,1,0:T(8,128)(2,1)}, u32[]{:S(2)}, u32[]{:S(2)}) %collective-permute-start.87) | collective-permute-done | bytes 3145760 | tf_op jit(solution)/shard_map/ppermute | solution.py:54
  411.2 7.8 collective-permute-start.88
  423.9 7.2 fusion.63
  434.5 4.8 collective-permute-done.82
  460.4 6.2 pad_maximum_fusion
  477.3 4.6 collective-permute-done.92
  494.8 10.7 collective-permute-start.96
  510.3 28.6 %collective-permute-done.120 = bf16[3,256,2048]{2,1,0:T(8,128)(2,1)} collective-permute-done((bf16[3,256,2048]{2,1,0:T(8,128)(2,1)}, bf16[3,256,2048]{2,1,0:T(8,128)(2,1)}, u32[]{:S(2)}, u32[]{:S(2)}) %collective-permute-start.120) | collective-permute-done | bytes 3145760 | tf_op jit(solution)/shard_map/ppermute | solution.py:54
  551.6 5.0 fusion.10
  556.6 4.9 fusion.28
  619.6 13.3 pad_maximum_fusion.1
  633.4 5.2 collective-permute-done.116
  641.9 5.3 collective-permute-done.118
  647.9 5.6 collective-permute-done.119
  670.5 6.4 collective-permute-done.126
  677.4 7.3 collective-permute-done.127
  684.9 7.0 collective-permute-done.128
  706.8 12.4 collective-permute-start.129
  749.3 7.4 fusion.89
  775.0 5.3 pad_maximum_fusion.3
  785.4 5.9 collective-permute-done.143
  838.6 15.6 %collective-permute-start.235 = (bf16[64,64]{1,0:T(8,128)(2,1)}, bf16[64,64]{1,0:T(8,128)(2,1)}, u32[]{:S(2)}, u32[]{:S(2)}) collective-permute-start(bf16[64,64]{1,0:T(8,128)(2,1)} %slice.2037), channel_id=1, source_target_pairs={{0,16},{16,0},{1,17},{17,1},{2,18},{18,2},{3,19},{19,3},{4,20},{20... | collective-permute-start | bytes 24584 | tf_op jit(solution)/shard_map/ppermute | solution.py:58
  887.1 4.5 collective-permute-start.246
  903.4 5.5 fusion.7
  926.1 6.5 collective-permute-done.164
  944.6 7.4 fusion.82
  965.0 6.2 pad_maximum_fusion.2
  987.0 7.8 collective-permute-done.171
  995.1 12.6 fusion.24
  1007.8 6.2 collective-permute-done.172
  1048.1 5.1 collective-permute-done.183
  1065.3 4.5 collective-permute-done.179
  1073.7 15.3 %collective-permute-start.190 = (bf16[64,1024]{1,0:T(8,128)(2,1)}, bf16[64,1024]{1,0:T(8,128)(2,1)}, u32[]{:S(2)}, u32[]{:S(2)}) collective-permute-start(bf16[64,1024]{1,0:T(8,128)(2,1)} %get-tuple-element.302), channel_id=1, source_target_pairs={{0,16},{16,0},{1,17},{17,1},{2,18},{18,2},{3,19},{19,3},{4,20},{20... | collective-permute-start | bytes 393224 | tf_op jit(solution)/shard_map/ppermute | solution.py:58
  1105.4 4.8 add_convert_fusion.1
  1111.4 4.9 fusion.16
  1122.8 64.0 %collective-permute-done.243 = bf16[3,256,2048]{2,1,0:T(8,128)(2,1)} collective-permute-done((bf16[3,256,2048]{2,1,0:T(8,128)(2,1)}, bf16[3,256,2048]{2,1,0:T(8,128)(2,1)}, u32[]{:S(2)}, u32[]{:S(2)}) %collective-permute-start.243) | collective-permute-done | bytes 3145760 | tf_op jit(solution)/shard_map/ppermute | solution.py:54
  1188.0 66.2 %collective-permute-done.241 = bf16[3,256,2048]{2,1,0:T(8,128)(2,1)} collective-permute-done((bf16[3,256,2048]{2,1,0:T(8,128)(2,1)}, bf16[3,256,2048]{2,1,0:T(8,128)(2,1)}, u32[]{:S(2)}, u32[]{:S(2)}) %collective-permute-start.241) | collective-permute-done | bytes 3145760 | tf_op jit(solution)/shard_map/ppermute | solution.py:54
  1255.0 14.8 %select_convert_fusion = bf16[3,512,2048]{2,1,0:T(8,128)(2,1)} fusion(pred[]{:T(512)S(6)} %eq.593, bf16[3,256,2048]{2,1,0:T(8,128)(2,1)} %collective-permute-done.241, bf16[3,256,2048]{2,1,0:T(8,128)(2,1)} %collective-permute-done.243, bf16[3,1024,2048]{2,1,0:T(8,128)(2,1)} %pad_maximum_fusion.3, bf16[3,1024,2048]{2,1,0:T(8,128)(2,1)} %pad_maximum_fusion.2), kind=kLoop, calls=%fused_computation.13 | loop fusion | flops 31457280 | bytes 25165824 | tf_op jit(solution)/shard_map/convert_element_type | solution.py:575
  1286.5 7.5 collective-permute-done.224
  1295.6 6.9 collective-permute-done.209
  1303.8 6.8 collective-permute-done.206
  1311.7 6.9 collective-permute-done.203
  1322.5 5.1 collective-permute-done.225
  1329.7 6.8 collective-permute-done.217
  1338.2 6.4 collective-permute-done.210
  1347.4 5.3 collective-permute-done.215
  1353.9 6.9 collective-permute-done.207
  1378.8 5.4 collective-permute-done.228
  1384.5 6.1 collective-permute-start.245
  1397.9 20.1 %add_bitcast_fusion = f32[1,3,512,2048]{3,2,1,0:T(8,128)} fusion(bf16[3,512,2048]{2,1,0:T(8,128)(2,1)} %collective-permute-done.244, pred[]{:T(512)S(6)} %eq.593, bf16[3,256,2048]{2,1,0:T(8,128)(2,1)} %collective-permute-done.241, bf16[3,256,2048]{2,1,0:T(8,128)(2,1)} %collective-permute-done.243, bf16[3,1024,2048]{2,1,0:T(8,128)(2,1)} %pad_maximum_fusion.3, ...), kind=kLoop, calls=%fused_computation.12 | loop fusion | flops 34603008 | bytes 37748736 | tf_op jit(solution)/shard_map/broadcast_in_dim | solution.py:596
  (1692 shorter events, 711.0 us)
Async XLA Ops:
  7.2 416.2 %all-gather.4.cloned.1.call-start = ((), (), s32[]{:S(2)}) async-start(), calls=%async_computation.3 | async-start | bytes 12533760 | tf_op jit(solution)/shard_map/all_gather | solution.py:273
  8.1 33.0 %collective-permute-start = (bf16[800]{0:T(1024)(128)(2,1)S(1)}, bf16[800]{0:T(1024)(128)(2,1)S(1)}, u32[]{:S(2)}, u32[]{:S(2)}) collective-permute-start(bf16[800]{0:T(1024)(128)(2,1)S(1)} %reduce.4), channel_id=1, source_target_pairs={{0,16},{16,0},{1,17},{17,1},{2,18},{18,2},{3,19},{19,3},{4,20},{20... | collective-permute-start | bytes 4808 | tf_op jit(solution)/shard_map/ppermute | solution.py:58
  10.2 31.1 %collective-permute-start.1 = (bf16[360,1024]{1,0:T(8,128)(2,1)S(1)}, bf16[360,1024]{1,0:T(8,128)(2,1)}, u32[]{:S(2)}, u32[]{:S(2)}) collective-permute-start(bf16[360,1024]{1,0:T(8,128)(2,1)S(1)} %broadcast_select_fusion.4), channel_id=1, source_target_pairs={{0,16},{16,0},{1,17},{17,1},{2,18},{18,2},{3,19},{19,3},{4,20},{20... | collective-permute-start | bytes 2211848 | tf_op jit(solution)/shard_map/ppermute | solution.py:58
  51.0 25.1 %collective-permute-start.4 = (bf16[184,1024]{1,0:T(8,128)(2,1)}, bf16[184,1024]{1,0:T(8,128)(2,1)}, u32[]{:S(2)}, u32[]{:S(2)}) collective-permute-start(bf16[184,1024]{1,0:T(8,128)(2,1)} %pad_maximum_fusion.15), channel_id=1, source_target_pairs={{0,4},{1,5},{2,6},{3,7},{4,8},{5,9},{6,10},{7,11},{8,12},{9,13},{1... | collective-permute-start | bytes 1130504 | tf_op jit(solution)/shard_map/ppermute | solution.py:54
  56.2 19.9 %collective-permute-start.5 = (bf16[184,1024]{1,0:T(8,128)(2,1)}, bf16[184,1024]{1,0:T(8,128)(2,1)}, u32[]{:S(2)}, u32[]{:S(2)}) collective-permute-start(bf16[184,1024]{1,0:T(8,128)(2,1)} %slice.1246), channel_id=1, source_target_pairs={{0,2},{1,3},{2,0},{3,1},{4,6},{5,7},{6,4},{7,5},{8,10},{9,11},{10,... | collective-permute-start | bytes 1130504 | tf_op jit(solution)/shard_map/ppermute | solution.py:54
  60.0 23.8 %collective-permute-start.32 = (bf16[184,1024]{1,0:T(8,128)(2,1)}, bf16[184,1024]{1,0:T(8,128)(2,1)}, u32[]{:S(2)}, u32[]{:S(2)}) collective-permute-start(bf16[184,1024]{1,0:T(8,128)(2,1)} %slice.1246), channel_id=1, source_target_pairs={{0,16},{16,0},{1,17},{17,1},{2,18},{18,2},{3,19},{19,3},{4,20},{20... | collective-permute-start | bytes 1130504 | tf_op jit(solution)/shard_map/ppermute | solution.py:58
  69.5 424.5 %reduce-scatter.3.cloned.1.call-start = ((), (), s32[]{:S(2)}) async-start(), calls=%async_computation.2 | async-start | bytes 1114112 | tf_op jit(solution)/shard_map/reduce_scatter | solution.py:239
  76.1 24.1 %collective-permute-start.9 = (bf16[184,1024]{1,0:T(8,128)(2,1)}, bf16[184,1024]{1,0:T(8,128)(2,1)S(1)}, u32[]{:S(2)}, u32[]{:S(2)}) collective-permute-start(bf16[184,1024]{1,0:T(8,128)(2,1)} %collective-permute-done.4), channel_id=1, source_target_pairs={{0,1},{1,0},{2,3},{3,2},{4,5},{5,4},{6,7},{7,6},{8,9},{9,8},{10,11... | collective-permute-start | bytes 1130504 | tf_op jit(solution)/shard_map/ppermute | solution.py:54
  77.2 24.1 %collective-permute-start.10 = (bf16[184,1024]{1,0:T(8,128)(2,1)}, bf16[184,1024]{1,0:T(8,128)(2,1)S(1)}, u32[]{:S(2)}, u32[]{:S(2)}) collective-permute-start(bf16[184,1024]{1,0:T(8,128)(2,1)} %collective-permute-done.4), channel_id=1, source_target_pairs={{0,2},{1,3},{2,0},{3,1},{4,6},{5,7},{6,4},{7,5},{8,10},{9,11},{10,... | collective-permute-start | bytes 1130504 | tf_op jit(solution)/shard_map/ppermute | solution.py:54
  77.2 25.9 %collective-permute-start.11 = (bf16[184,1024]{1,0:T(8,128)(2,1)}, bf16[184,1024]{1,0:T(8,128)(2,1)S(1)}, u32[]{:S(2)}, u32[]{:S(2)}) collective-permute-start(bf16[184,1024]{1,0:T(8,128)(2,1)} %collective-permute-done.4), channel_id=1, source_target_pairs={{0,4},{1,5},{2,6},{3,7},{4,8},{5,9},{6,10},{7,11},{8,12},{9,13},{1... | collective-permute-start | bytes 1130504 | tf_op jit(solution)/shard_map/ppermute | solution.py:54
  77.2 23.0 %collective-permute-start.8 = (bf16[184,1024]{1,0:T(8,128)(2,1)}, bf16[184,1024]{1,0:T(8,128)(2,1)S(1)}, u32[]{:S(2)}, u32[]{:S(2)}) collective-permute-start(bf16[184,1024]{1,0:T(8,128)(2,1)} %collective-permute-done.3), channel_id=1, source_target_pairs={{0,1},{1,0},{2,3},{3,2},{4,5},{5,4},{6,7},{7,6},{8,9},{9,8},{10,11... | collective-permute-start | bytes 1130504 | tf_op jit(solution)/shard_map/ppermute | solution.py:54
  83.7 21.3 %collective-permute-start.12 = (bf16[184,1024]{1,0:T(8,128)(2,1)}, bf16[184,1024]{1,0:T(8,128)(2,1)S(1)}, u32[]{:S(2)}, u32[]{:S(2)}) collective-permute-start(bf16[184,1024]{1,0:T(8,128)(2,1)} %collective-permute-done.6), channel_id=1, source_target_pairs={{0,2},{1,3},{2,0},{3,1},{4,6},{5,7},{6,4},{7,5},{8,10},{9,11},{10,... | collective-permute-start | bytes 1130504 | tf_op jit(solution)/shard_map/ppermute | solution.py:54
  111.6 34.2 %collective-permute-start.17 = (bf16[184,1024]{1,0:T(8,128)(2,1)S(1)}, bf16[184,1024]{1,0:T(8,128)(2,1)S(1)}, u32[]{:S(2)}, u32[]{:S(2)}) collective-permute-start(bf16[184,1024]{1,0:T(8,128)(2,1)S(1)} %collective-permute-done.11), channel_id=1, source_target_pairs={{0,1},{1,0},{2,3},{3,2},{4,5},{5,4},{6,7},{7,6},{8,9},{9,8},{10,11... | collective-permute-start | bytes 1130504 | tf_op jit(solution)/shard_map/ppermute | solution.py:54
  112.7 34.1 %collective-permute-start.18 = (bf16[184,1024]{1,0:T(8,128)(2,1)S(1)}, bf16[184,1024]{1,0:T(8,128)(2,1)S(1)}, u32[]{:S(2)}, u32[]{:S(2)}) collective-permute-start(bf16[184,1024]{1,0:T(8,128)(2,1)S(1)} %collective-permute-done.11), channel_id=1, source_target_pairs={{0,2},{1,3},{2,0},{3,1},{4,6},{5,7},{6,4},{7,5},{8,10},{9,11},{10,... | collective-permute-start | bytes 1130504 | tf_op jit(solution)/shard_map/ppermute | solution.py:54
  115.7 32.8 %collective-permute-start.19 = (bf16[184,1024]{1,0:T(8,128)(2,1)S(1)}, bf16[184,1024]{1,0:T(8,128)(2,1)S(1)}, u32[]{:S(2)}, u32[]{:S(2)}) collective-permute-start(bf16[184,1024]{1,0:T(8,128)(2,1)S(1)} %collective-permute-done.11), channel_id=1, source_target_pairs={{0,4},{1,5},{2,6},{3,7},{4,8},{5,9},{6,10},{7,11},{8,12},{9,13},{1... | collective-permute-start | bytes 1130504 | tf_op jit(solution)/shard_map/ppermute | solution.py:54
  118.3 27.5 %collective-permute-start.16 = (bf16[184,1024]{1,0:T(8,128)(2,1)S(1)}, bf16[184,1024]{1,0:T(8,128)(2,1)S(1)}, u32[]{:S(2)}, u32[]{:S(2)}) collective-permute-start(bf16[184,1024]{1,0:T(8,128)(2,1)S(1)} %collective-permute-done.10), channel_id=1, source_target_pairs={{0,1},{1,0},{2,3},{3,2},{4,5},{5,4},{6,7},{7,6},{8,9},{9,8},{10,11... | collective-permute-start | bytes 1130504 | tf_op jit(solution)/shard_map/ppermute | solution.py:54
  119.1 34.2 %collective-permute-start.20 = (bf16[184,1024]{1,0:T(8,128)(2,1)S(1)}, bf16[184,1024]{1,0:T(8,128)(2,1)S(1)}, u32[]{:S(2)}, u32[]{:S(2)}) collective-permute-start(bf16[184,1024]{1,0:T(8,128)(2,1)S(1)} %collective-permute-done.14), channel_id=1, source_target_pairs={{0,2},{1,3},{2,0},{3,1},{4,6},{5,7},{6,4},{7,5},{8,10},{9,11},{10,... | collective-permute-start | bytes 1130504 | tf_op jit(solution)/shard_map/ppermute | solution.py:54
  146.8 20.2 %collective-permute-start.23 = (bf16[184,1024]{1,0:T(8,128)(2,1)S(1)}, bf16[184,1024]{1,0:T(8,128)(2,1)S(1)}, u32[]{:S(2)}, u32[]{:S(2)}) collective-permute-start(bf16[184,1024]{1,0:T(8,128)(2,1)S(1)} %collective-permute-done.15), channel_id=1, source_target_pairs={{0,4},{1,5},{2,6},{3,7},{4,8},{5,9},{6,10},{7,11},{8,12},{9,13},{1... | collective-permute-start | bytes 1130504 | tf_op jit(solution)/shard_map/ppermute | solution.py:54
  148.5 21.9 %collective-permute-start.36 = (bf16[184,1024]{1,0:T(8,128)(2,1)S(1)}, bf16[184,1024]{1,0:T(8,128)(2,1)S(1)}, u32[]{:S(2)}, u32[]{:S(2)}) collective-permute-start(bf16[184,1024]{1,0:T(8,128)(2,1)S(1)} %collective-permute-done.12), channel_id=1, source_target_pairs={{0,16},{16,0},{1,17},{17,1},{2,18},{18,2},{3,19},{19,3},{4,20},{20... | collective-permute-start | bytes 1130504 | tf_op jit(solution)/shard_map/ppermute | solution.py:58
  153.4 20.0 %collective-permute-start.38 = (bf16[184,1024]{1,0:T(8,128)(2,1)S(1)}, bf16[184,1024]{1,0:T(8,128)(2,1)S(1)}, u32[]{:S(2)}, u32[]{:S(2)}) collective-permute-start(bf16[184,1024]{1,0:T(8,128)(2,1)S(1)} %collective-permute-done.14), channel_id=1, source_target_pairs={{0,16},{16,0},{1,17},{17,1},{2,18},{18,2},{3,19},{19,3},{4,20},{20... | collective-permute-start | bytes 1130504 | tf_op jit(solution)/shard_map/ppermute | solution.py:58
  166.9 41.9 %collective-permute-start.25 = (bf16[184,1024]{1,0:T(8,128)(2,1)S(1)}, bf16[184,1024]{1,0:T(8,128)(2,1)S(1)}, u32[]{:S(2)}, u32[]{:S(2)}) collective-permute-start(bf16[184,1024]{1,0:T(8,128)(2,1)S(1)} %collective-permute-done.19), channel_id=1, source_target_pairs={{0,1},{1,0},{2,3},{3,2},{4,5},{5,4},{6,7},{7,6},{8,9},{9,8},{10,11... | collective-permute-start | bytes 1130504 | tf_op jit(solution)/shard_map/ppermute | solution.py:54
  170.5 44.7 %collective-permute-start.26 = (bf16[184,1024]{1,0:T(8,128)(2,1)S(1)}, bf16[184,1024]{1,0:T(8,128)(2,1)S(1)}, u32[]{:S(2)}, u32[]{:S(2)}) collective-permute-start(bf16[184,1024]{1,0:T(8,128)(2,1)S(1)} %collective-permute-done.19), channel_id=1, source_target_pairs={{0,2},{1,3},{2,0},{3,1},{4,6},{5,7},{6,4},{7,5},{8,10},{9,11},{10,... | collective-permute-start | bytes 1130504 | tf_op jit(solution)/shard_map/ppermute | solution.py:54
  171.7 60.0 %collective-permute-start.28 = (bf16[184,1024]{1,0:T(8,128)(2,1)S(1)}, bf16[184,1024]{1,0:T(8,128)(2,1)S(1)}, u32[]{:S(2)}, u32[]{:S(2)}) collective-permute-start(bf16[184,1024]{1,0:T(8,128)(2,1)S(1)} %collective-permute-done.23), channel_id=1, source_target_pairs={{0,2},{1,3},{2,0},{3,1},{4,6},{5,7},{6,4},{7,5},{8,10},{9,11},{10,... | collective-permute-start | bytes 1130504 | tf_op jit(solution)/shard_map/ppermute | solution.py:54
  173.5 58.4 %collective-permute-start.29 = (bf16[184,1024]{1,0:T(8,128)(2,1)S(1)}, bf16[184,1024]{1,0:T(8,128)(2,1)}, u32[]{:S(2)}, u32[]{:S(2)}) collective-permute-start(bf16[184,1024]{1,0:T(8,128)(2,1)S(1)} %collective-permute-done.23), channel_id=1, source_target_pairs={{0,1},{1,0},{2,3},{3,2},{4,5},{5,4},{6,7},{7,6},{8,9},{9,8},{10,11... | collective-permute-start | bytes 1130504 | tf_op jit(solution)/shard_map/ppermute | solution.py:54
  175.3 33.0 %collective-permute-start.24 = (bf16[184,1024]{1,0:T(8,128)(2,1)S(1)}, bf16[184,1024]{1,0:T(8,128)(2,1)S(1)}, u32[]{:S(2)}, u32[]{:S(2)}) collective-permute-start(bf16[184,1024]{1,0:T(8,128)(2,1)S(1)} %collective-permute-done.18), channel_id=1, source_target_pairs={{0,1},{1,0},{2,3},{3,2},{4,5},{5,4},{6,7},{7,6},{8,9},{9,8},{10,11... | collective-permute-start | bytes 1130504 | tf_op jit(solution)/shard_map/ppermute | solution.py:54
  208.9 23.4 %collective-permute-start.40 = (bf16[184,1024]{1,0:T(8,128)(2,1)S(1)}, bf16[184,1024]{1,0:T(8,128)(2,1)S(1)}, u32[]{:S(2)}, u32[]{:S(2)}) collective-permute-start(bf16[184,1024]{1,0:T(8,128)(2,1)S(1)} %collective-permute-done.20), channel_id=1, source_target_pairs={{0,16},{16,0},{1,17},{17,1},{2,18},{18,2},{3,19},{19,3},{4,20},{20... | collective-permute-start | bytes 1130504 | tf_op jit(solution)/shard_map/ppermute | solution.py:58
  225.2 112.7 %collective-permute-start.86 = (bf16[3,512,2048]{2,1,0:T(8,128)(2,1)}, bf16[3,512,2048]{2,1,0:T(8,128)(2,1)}, u32[]{:S(2)}, u32[]{:S(2)}) collective-permute-start(bf16[3,512,2048]{2,1,0:T(8,128)(2,1)} %bitcast.125), channel_id=1, source_target_pairs={{0,16},{16,0},{1,17},{17,1},{2,18},{18,2},{3,19},{19,3},{4,20},{20... | collective-permute-start | bytes 18874376 | tf_op jit(solution)/shard_map/ppermute | solution.py:58
  231.8 58.4 %collective-permute-start.48 = (bf16[176,1024]{1,0:T(8,128)(2,1)}, bf16[176,1024]{1,0:T(8,128)(2,1)}, u32[]{:S(2)}, u32[]{:S(2)}) collective-permute-start(bf16[176,1024]{1,0:T(8,128)(2,1)} %slice.1242), channel_id=1, source_target_pairs={{0,16},{16,0},{1,17},{17,1},{2,18},{18,2},{3,19},{19,3},{4,20},{20... | collective-permute-start | bytes 1081352 | tf_op jit(solution)/shard_map/ppermute | solution.py:58
  231.9 59.6 %collective-permute-start.49 = (bf16[176,1024]{1,0:T(8,128)(2,1)}, bf16[176,1024]{1,0:T(8,128)(2,1)}, u32[]{:S(2)}, u32[]{:S(2)}) collective-permute-start(bf16[176,1024]{1,0:T(8,128)(2,1)} %slice.1263), channel_id=1, source_target_pairs={{0,16},{16,0},{1,17},{17,1},{2,18},{18,2},{3,19},{19,3},{4,20},{20... | collective-permute-start | bytes 1081352 | tf_op jit(solution)/shard_map/ppermute | solution.py:58
  252.8 31.9 %collective-permute-start.44 = (bf16[184,1024]{1,0:T(8,128)(2,1)}, bf16[184,1024]{1,0:T(8,128)(2,1)}, u32[]{:S(2)}, u32[]{:S(2)}) collective-permute-start(bf16[184,1024]{1,0:T(8,128)(2,1)} %collective-permute-done.27), channel_id=1, source_target_pairs={{0,16},{16,0},{1,17},{17,1},{2,18},{18,2},{3,19},{19,3},{4,20},{20... | collective-permute-start | bytes 1130504 | tf_op jit(solution)/shard_map/ppermute | solution.py:58
  255.9 31.3 %collective-permute-start.45 = (bf16[184,1024]{1,0:T(8,128)(2,1)}, bf16[184,1024]{1,0:T(8,128)(2,1)S(1)}, u32[]{:S(2)}, u32[]{:S(2)}) collective-permute-start(bf16[184,1024]{1,0:T(8,128)(2,1)} %copy-done.148), channel_id=1, source_target_pairs={{0,16},{16,0},{1,17},{17,1},{2,18},{18,2},{3,19},{19,3},{4,20},{20... | collective-permute-start | bytes 1130504 | tf_op jit(solution)/shard_map/ppermute | solution.py:58
  348.2 63.0 %collective-permute-start.87 = (bf16[3,256,2048]{2,1,0:T(8,128)(2,1)}, bf16[3,256,2048]{2,1,0:T(8,128)(2,1)}, u32[]{:S(2)}, u32[]{:S(2)}) collective-permute-start(bf16[3,256,2048]{2,1,0:T(8,128)(2,1)} %constant_dynamic-slice_fusion.17), channel_id=1, source_target_pairs={{0,1},{1,0},{2,3},{3,2},{4,5},{5,4},{6,7},{7,6},{8,9},{9,8},{10,11... | collective-permute-start | bytes 9437192 | tf_op jit(solution)/shard_map/ppermute | solution.py:54
  411.2 49.2 %collective-permute-start.88 = (bf16[3,256,2048]{2,1,0:T(8,128)(2,1)}, bf16[3,256,2048]{2,1,0:T(8,128)(2,1)}, u32[]{:S(2)}, u32[]{:S(2)}) collective-permute-start(bf16[3,256,2048]{2,1,0:T(8,128)(2,1)} %collective-permute-done.87), channel_id=1, source_target_pairs={{0,16},{16,0},{1,17},{17,1},{2,18},{18,2},{3,19},{19,3},{4,20},{20... | collective-permute-start | bytes 9437192 | tf_op jit(solution)/shard_map/ppermute | solution.py:58
  423.3 128.2 %collective-permute-start.97 = (bf16[5760,1024]{1,0:T(8,128)(2,1)}, bf16[5760,1024]{1,0:T(8,128)(2,1)}, u32[]{:S(2)}, u32[]{:S(2)}) collective-permute-start(bf16[5760,1024]{1,0:T(8,128)(2,1)} %all-gather.4.cloned.1.call-done), channel_id=1, source_target_pairs={{0,16},{16,0},{1,17},{17,1},{2,18},{18,2},{3,19},{19,3},{4,20},{20... | collective-permute-start | bytes 35389448 | tf_op jit(solution)/shard_map/ppermute | solution.py:58
  431.2 564.0 %all-gather.6.cloned.1.call-start = ((), (), s32[]{:S(2)}) async-start(), calls=%async_computation.5 | async-start | bytes 1114112 | tf_op jit(solution)/shard_map/all_gather | solution.py:584
  459.5 79.3 %collective-permute-start.120 = (bf16[3,256,2048]{2,1,0:T(8,128)(2,1)}, bf16[3,256,2048]{2,1,0:T(8,128)(2,1)}, u32[]{:S(2)}, u32[]{:S(2)}) collective-permute-start(bf16[3,256,2048]{2,1,0:T(8,128)(2,1)} %constant_dynamic-slice_fusion.16), channel_id=1, source_target_pairs={{0,1},{1,0},{2,3},{3,2},{4,5},{5,4},{6,7},{7,6},{8,9},{9,8},{10,11... | collective-permute-start | bytes 9437192 | tf_op jit(solution)/shard_map/ppermute | solution.py:54
  483.6 21.9 %collective-permute-start.90 = (bf16[64,2048]{1,0:T(8,128)(2,1)S(1)}, bf16[64,2048]{1,0:T(8,128)(2,1)S(1)}, u32[]{:S(2)}, u32[]{:S(2)}) collective-permute-start(bf16[64,2048]{1,0:T(8,128)(2,1)S(1)} %get-tuple-element.214), channel_id=1, source_target_pairs={{0,2},{1,3},{2,0},{3,1},{4,6},{5,7},{6,4},{7,5},{8,10},{9,11},{10,... | collective-permute-start | bytes 786440 | tf_op jit(solution)/shard_map/ppermute | solution.py:54
  494.8 50.8 %collective-permute-start.96 = (bf16[64,256]{1,0:T(8,128)(2,1)S(1)}, bf16[64,256]{1,0:T(8,128)(2,1)S(1)}, u32[]{:S(2)}, u32[]{:S(2)}) collective-permute-start(bf16[64,256]{1,0:T(8,128)(2,1)S(1)} %broadcast_select_fusion.56), channel_id=1, source_target_pairs={{0,16},{16,0},{1,17},{17,1},{2,18},{18,2},{3,19},{19,3},{4,20},{20... | collective-permute-start | bytes 98312 | tf_op jit(solution)/shard_map/ppermute | solution.py:58
  505.6 36.6 %collective-permute-start.89 = (bf16[64,2048]{1,0:T(8,128)(2,1)S(1)}, bf16[64,2048]{1,0:T(8,128)(2,1)S(1)}, u32[]{:S(2)}, u32[]{:S(2)}) collective-permute-start(bf16[64,2048]{1,0:T(8,128)(2,1)S(1)} %get-tuple-element.211), channel_id=1, source_target_pairs={{0,2},{1,3},{2,0},{3,1},{4,6},{5,7},{6,4},{7,5},{8,10},{9,11},{10,... | collective-permute-start | bytes 786440 | tf_op jit(solution)/shard_map/ppermute | solution.py:54
  509.4 32.8 %collective-permute-start.95 = (bf16[64,2048]{1,0:T(8,128)(2,1)S(1)}, bf16[64,2048]{1,0:T(8,128)(2,1)S(1)}, u32[]{:S(2)}, u32[]{:S(2)}) collective-permute-start(bf16[64,2048]{1,0:T(8,128)(2,1)S(1)} %fusion.208), channel_id=1, source_target_pairs={{0,12},{1,13},{2,14},{3,15},{4,0},{5,1},{6,2},{7,3},{8,4},{9,5},{1... | collective-permute-start | bytes 786440 | tf_op jit(solution)/shard_map/ppermute | solution.py:54
  538.8 80.7 %collective-permute-start.121 = (bf16[3,256,2048]{2,1,0:T(8,128)(2,1)}, bf16[3,256,2048]{2,1,0:T(8,128)(2,1)}, u32[]{:S(2)}, u32[]{:S(2)}) collective-permute-start(bf16[3,256,2048]{2,1,0:T(8,128)(2,1)} %collective-permute-done.120), channel_id=1, source_target_pairs={{0,16},{16,0},{1,17},{17,1},{2,18},{18,2},{3,19},{19,3},{4,20},{20... | collective-permute-start | bytes 9437192 | tf_op jit(solution)/shard_map/ppermute | solution.py:58
  720.7 182.1 %collective-permute-start.230 = (bf16[64,1024]{1,0:T(8,128)(2,1)}, bf16[64,1024]{1,0:T(8,128)(2,1)}, u32[]{:S(2)}, u32[]{:S(2)}) collective-permute-start(bf16[64,1024]{1,0:T(8,128)(2,1)} %copy-done.174), channel_id=1, source_target_pairs={{0,16},{16,0},{1,17},{17,1},{2,18},{18,2},{3,19},{19,3},{4,20},{20... | collective-permute-start | bytes 393224 | tf_op jit(solution)/shard_map/ppermute | solution.py:58
  763.4 22.0 %collective-permute-start.137 = (bf16[64,2048]{1,0:T(8,128)(2,1)S(1)}, bf16[64,2048]{1,0:T(8,128)(2,1)S(1)}, u32[]{:S(2)}, u32[]{:S(2)}) collective-permute-start(bf16[64,2048]{1,0:T(8,128)(2,1)S(1)} %get-tuple-element.201), channel_id=1, source_target_pairs={{0,2},{1,3},{2,0},{3,1},{4,6},{5,7},{6,4},{7,5},{8,10},{9,11},{10,... | collective-permute-start | bytes 786440 | tf_op jit(solution)/shard_map/ppermute | solution.py:54
  833.7 20.5 %collective-permute-start.147 = (bf16[64,1024]{1,0:T(8,128)(2,1)S(1)}, bf16[64,1024]{1,0:T(8,128)(2,1)S(1)}, u32[]{:S(2)}, u32[]{:S(2)}) collective-permute-start(bf16[64,1024]{1,0:T(8,128)(2,1)S(1)} %copy-done.187), channel_id=1, source_target_pairs={{0,2},{1,3},{2,0},{3,1},{4,6},{5,7},{6,4},{7,5},{8,10},{9,11},{10,... | collective-permute-start | bytes 393224 | tf_op jit(solution)/shard_map/ppermute | solution.py:54
  838.6 80.5 %collective-permute-start.235 = (bf16[64,64]{1,0:T(8,128)(2,1)}, bf16[64,64]{1,0:T(8,128)(2,1)}, u32[]{:S(2)}, u32[]{:S(2)}) collective-permute-start(bf16[64,64]{1,0:T(8,128)(2,1)} %slice.2037), channel_id=1, source_target_pairs={{0,16},{16,0},{1,17},{17,1},{2,18},{18,2},{3,19},{19,3},{4,20},{20... | collective-permute-start | bytes 24584 | tf_op jit(solution)/shard_map/ppermute | solution.py:58
  859.3 51.3 %collective-permute-start.233 = (bf16[64,2048]{1,0:T(8,128)(2,1)}, bf16[64,2048]{1,0:T(8,128)(2,1)}, u32[]{:S(2)}, u32[]{:S(2)}) collective-permute-start(bf16[64,2048]{1,0:T(8,128)(2,1)} %convert_element_type.801), channel_id=1, source_target_pairs={{0,16},{16,0},{1,17},{17,1},{2,18},{18,2},{3,19},{19,3},{4,20},{20... | collective-permute-start | bytes 786440 | tf_op jit(solution)/shard_map/ppermute | solution.py:58
  895.3 498.0 %reduce-scatter.5.cloned.1.call-start = ((), (), s32[]{:S(2)}) async-start(), calls=%async_computation.4 | async-start | bytes 12533760 | tf_op jit(solution)/shard_map/reduce_scatter | solution.py:532
  919.8 62.9 %collective-permute-start.242 = (bf16[3,256,2048]{2,1,0:T(8,128)(2,1)}, bf16[3,256,2048]{2,1,0:T(8,128)(2,1)}, u32[]{:S(2)}, u32[]{:S(2)}) collective-permute-start(bf16[3,256,2048]{2,1,0:T(8,128)(2,1)} %pad_maximum_fusion.6), channel_id=1, source_target_pairs={{0,16},{16,0},{1,17},{17,1},{2,18},{18,2},{3,19},{19,3},{4,20},{20... | collective-permute-start | bytes 9437192 | tf_op jit(solution)/shard_map/ppermute | solution.py:58
  958.5 28.5 %collective-permute-start.167 = (bf16[64,2048]{1,0:T(8,128)(2,1)S(1)}, bf16[64,2048]{1,0:T(8,128)(2,1)S(1)}, u32[]{:S(2)}, u32[]{:S(2)}) collective-permute-start(bf16[64,2048]{1,0:T(8,128)(2,1)S(1)} %get-tuple-element.192), channel_id=1, source_target_pairs={{0,2},{1,3},{2,0},{3,1},{4,6},{5,7},{6,4},{7,5},{8,10},{9,11},{10,... | collective-permute-start | bytes 786440 | tf_op jit(solution)/shard_map/ppermute | solution.py:54
  959.3 48.4 %collective-permute-start.166 = (bf16[64,2048]{1,0:T(8,128)(2,1)S(1)}, bf16[64,2048]{1,0:T(8,128)(2,1)S(1)}, u32[]{:S(2)}, u32[]{:S(2)}) collective-permute-start(bf16[64,2048]{1,0:T(8,128)(2,1)S(1)} %get-tuple-element.189), channel_id=1, source_target_pairs={{0,2},{1,3},{2,0},{3,1},{4,6},{5,7},{6,4},{7,5},{8,10},{9,11},{10,... | collective-permute-start | bytes 786440 | tf_op jit(solution)/shard_map/ppermute | solution.py:54
  973.5 131.9 %collective-permute-start.240 = (bf16[3,256,2048]{2,1,0:T(8,128)(2,1)}, bf16[3,256,2048]{2,1,0:T(8,128)(2,1)}, u32[]{:S(2)}, u32[]{:S(2)}) collective-permute-start(bf16[3,256,2048]{2,1,0:T(8,128)(2,1)} %pad_maximum_fusion.7), channel_id=1, source_target_pairs={{0,16},{16,0},{1,17},{17,1},{2,18},{18,2},{3,19},{19,3},{4,20},{20... | collective-permute-start | bytes 9437192 | tf_op jit(solution)/shard_map/ppermute | solution.py:58
  1069.7 19.3 %collective-permute-start.176 = (bf16[64,1024]{1,0:T(8,128)(2,1)S(1)}, bf16[64,1024]{1,0:T(8,128)(2,1)S(1)}, u32[]{:S(2)}, u32[]{:S(2)}) collective-permute-start(bf16[64,1024]{1,0:T(8,128)(2,1)S(1)} %copy-done.188), channel_id=1, source_target_pairs={{0,2},{1,3},{2,0},{3,1},{4,6},{5,7},{6,4},{7,5},{8,10},{9,11},{10,... | collective-permute-start | bytes 393224 | tf_op jit(solution)/shard_map/ppermute | solution.py:54
  1069.9 19.5 %collective-permute-start.186 = (bf16[64,1024]{1,0:T(8,128)(2,1)S(1)}, bf16[64,1024]{1,0:T(8,128)(2,1)S(1)}, u32[]{:S(2)}, u32[]{:S(2)}) collective-permute-start(bf16[64,1024]{1,0:T(8,128)(2,1)S(1)} %get-tuple-element.164), channel_id=1, source_target_pairs={{0,12},{1,13},{2,14},{3,15},{4,0},{5,1},{6,2},{7,3},{8,4},{9,5},{1... | collective-permute-start | bytes 393224 | tf_op jit(solution)/shard_map/ppermute | solution.py:54
  1073.7 196.3 %collective-permute-start.190 = (bf16[64,1024]{1,0:T(8,128)(2,1)}, bf16[64,1024]{1,0:T(8,128)(2,1)}, u32[]{:S(2)}, u32[]{:S(2)}) collective-permute-start(bf16[64,1024]{1,0:T(8,128)(2,1)} %get-tuple-element.302), channel_id=1, source_target_pairs={{0,16},{16,0},{1,17},{17,1},{2,18},{18,2},{3,19},{19,3},{4,20},{20... | collective-permute-start | bytes 393224 | tf_op jit(solution)/shard_map/ppermute | solution.py:58
  1096.2 183.2 %collective-permute-start.193 = (bf16[64,2048]{1,0:T(8,128)(2,1)}, bf16[64,2048]{1,0:T(8,128)(2,1)}, u32[]{:S(2)}, u32[]{:S(2)}) collective-permute-start(bf16[64,2048]{1,0:T(8,128)(2,1)} %convert_element_type.776), channel_id=1, source_target_pairs={{0,16},{16,0},{1,17},{17,1},{2,18},{18,2},{3,19},{19,3},{4,20},{20... | collective-permute-start | bytes 786440 | tf_op jit(solution)/shard_map/ppermute | solution.py:58
  1096.8 176.7 %collective-permute-start.192 = (bf16[64,1024]{1,0:T(8,128)(2,1)}, bf16[64,1024]{1,0:T(8,128)(2,1)}, u32[]{:S(2)}, u32[]{:S(2)}) collective-permute-start(bf16[64,1024]{1,0:T(8,128)(2,1)} %get-tuple-element.299), channel_id=1, source_target_pairs={{0,16},{16,0},{1,17},{17,1},{2,18},{18,2},{3,19},{19,3},{4,20},{20... | collective-permute-start | bytes 393224 | tf_op jit(solution)/shard_map/ppermute | solution.py:58
  1101.0 85.8 %collective-permute-start.243 = (bf16[3,256,2048]{2,1,0:T(8,128)(2,1)}, bf16[3,256,2048]{2,1,0:T(8,128)(2,1)}, u32[]{:S(2)}, u32[]{:S(2)}) collective-permute-start(bf16[3,256,2048]{2,1,0:T(8,128)(2,1)} %add_convert_fusion), channel_id=1, source_target_pairs={{0,1},{1,0},{2,3},{3,2},{4,5},{5,4},{6,7},{7,6},{8,9},{9,8},{10,11... | collective-permute-start | bytes 9437192 | tf_op jit(solution)/shard_map/ppermute | solution.py:54
  1110.2 144.1 %collective-permute-start.241 = (bf16[3,256,2048]{2,1,0:T(8,128)(2,1)}, bf16[3,256,2048]{2,1,0:T(8,128)(2,1)}, u32[]{:S(2)}, u32[]{:S(2)}) collective-permute-start(bf16[3,256,2048]{2,1,0:T(8,128)(2,1)} %add_convert_fusion.1), channel_id=1, source_target_pairs={{0,1},{1,0},{2,3},{3,2},{4,5},{5,4},{6,7},{7,6},{8,9},{9,8},{10,11... | collective-permute-start | bytes 9437192 | tf_op jit(solution)/shard_map/ppermute | solution.py:54
  1186.8 83.8 %collective-permute-start.189 = (bf16[64,3136]{1,0:T(8,128)(2,1)S(1)}, bf16[64,3136]{1,0:T(8,128)(2,1)S(1)}, u32[]{:S(2)}, u32[]{:S(2)}) collective-permute-start(bf16[64,3136]{1,0:T(8,128)(2,1)S(1)} %add_convert_fusion.2), channel_id=1, source_target_pairs={{0,16},{16,0},{1,17},{17,1},{2,18},{18,2},{3,19},{19,3},{4,20},{20... | collective-permute-start | bytes 1204232 | tf_op jit(solution)/shard_map/ppermute | solution.py:58
  1269.9 128.0 %collective-permute-start.244 = (bf16[3,512,2048]{2,1,0:T(8,128)(2,1)}, bf16[3,512,2048]{2,1,0:T(8,128)(2,1)}, u32[]{:S(2)}, u32[]{:S(2)}) collective-permute-start(bf16[3,512,2048]{2,1,0:T(8,128)(2,1)} %select_convert_fusion), channel_id=1, source_target_pairs={{0,16},{16,0},{1,17},{17,1},{2,18},{18,2},{3,19},{19,3},{4,20},{20... | collective-permute-start | bytes 18874376 | tf_op jit(solution)/shard_map/ppermute | solution.py:58
  1286.0 24.6 %collective-permute-start.206 = (bf16[184,1024]{1,0:T(8,128)(2,1)S(1)}, bf16[184,1024]{1,0:T(8,128)(2,1)S(1)}, u32[]{:S(2)}, u32[]{:S(2)}) collective-permute-start(bf16[184,1024]{1,0:T(8,128)(2,1)S(1)} %get-tuple-element.136), channel_id=1, source_target_pairs={{0,2},{1,3},{2,0},{3,1},{4,6},{5,7},{6,4},{7,5},{8,10},{9,11},{10,... | collective-permute-start | bytes 1130504 | tf_op jit(solution)/shard_map/ppermute | solution.py:54
  1294.0 24.6 %collective-permute-start.203 = (bf16[184,1024]{1,0:T(8,128)(2,1)S(1)}, bf16[184,1024]{1,0:T(8,128)(2,1)S(1)}, u32[]{:S(2)}, u32[]{:S(2)}) collective-permute-start(bf16[184,1024]{1,0:T(8,128)(2,1)S(1)} %get-tuple-element.138), channel_id=1, source_target_pairs={{0,2},{1,3},{2,0},{3,1},{4,6},{5,7},{6,4},{7,5},{8,10},{9,11},{10,... | collective-permute-start | bytes 1130504 | tf_op jit(solution)/shard_map/ppermute | solution.py:54
  1294.4 25.3 %collective-permute-start.223 = (bf16[184,1024]{1,0:T(8,128)(2,1)S(1)}, bf16[184,1024]{1,0:T(8,128)(2,1)S(1)}, u32[]{:S(2)}, u32[]{:S(2)}) collective-permute-start(bf16[184,1024]{1,0:T(8,128)(2,1)S(1)} %pad_maximum_fusion.22), channel_id=1, source_target_pairs={{0,1},{1,0},{2,3},{3,2},{4,5},{5,4},{6,7},{7,6},{8,9},{9,8},{10,11... | collective-permute-start | bytes 1130504 | tf_op jit(solution)/shard_map/ppermute | solution.py:54
  1394.6 23.4 %collective-permute-start.239 = (f32[360,1024]{1,0:T(8,128)S(1)}, f32[360,1024]{1,0:T(8,128)S(1)}, u32[]{:S(2)}, u32[]{:S(2)}) collective-permute-start(f32[360,1024]{1,0:T(8,128)S(1)} %convert_select_fusion), channel_id=1, source_target_pairs={{0,16},{16,0},{1,17},{17,1},{2,18},{18,2},{3,19},{19,3},{4,20},{20... | collective-permute-start | bytes 4423688 | tf_op jit(solution)/shard_map/ppermute | solution.py:58
  (516 other events, 8030.1 us)
Sparse Core Ops, SparseCore 0:
  69.6 193.2 all-gather.3
  431.3 62.6 reduce-scatter.2
  895.4 55.0 all-gather.5
  957.8 231.1 reduce-scatter.4

commit v2 on v1

v2 whole, which is shorter than its diff:
```python
import itertools
import math
from functools import partial

import jax
import jax.numpy as jnp
from jax import lax
from jax.sharding import PartitionSpec as P

D = 2048
HEADS = 8
KV_HEADS = 2
HEAD_DIM = 256
RANK = 64
PLD = 256
HALF = D // 2
QW = HEADS * HEAD_DIM
KW = KV_HEADS * HEAD_DIM
IN_ROWS = QW + 2 * KW + RANK
OUT_START = IN_ROWS + PLD
LAUREL_START = OUT_START + QW
SIDE_START = LAUREL_START + RANK

EPS = 1e-06
ROPE_BASE = 10000.0
INV_ROOT2 = 0.7071067811865476
MASKED = -1e30
SCALE = HEAD_DIM ** (-0.5)
BF = jnp.bfloat16
F32 = jnp.float32

ALL_CHIPS = ((0, 2, 1), (0, 1, 2))
PLANE = ((0, 1), (0, 1))


def tie(*values):
    return lax.optimization_barrier(values)


def chip_dims(n):
    side = math.isqrt(n // 4)
    return (4, side, side)


def chip_strides(n):
    sizes = chip_dims(n)
    return (sizes[1] * sizes[2], sizes[2], 1)


def hop(value, n, dims, step):
    sizes, strides = chip_dims(n), chip_strides(n)
    pairs = []
    for core, dim in enumerate(dims):
        for i in range(n):
            place = (i // strides[dim]) % sizes[dim]
            target = i + ((place + step) % sizes[dim] - place) * strides[dim]
            pairs.append((core * n + i, core * n + target))
    return lax.ppermute(value, ("section", "shard"), pairs)


def swap_cores(value):
    return lax.ppermute(value, "section", [(0, 1), (1, 0)])


def offsets_of(n, orders):
    sizes = chip_dims(n)
    return list(itertools.product(*[range(sizes[d]) for d in orders[0]]))


def tree(n, orders):
    rounds = {}
    for offset in offsets_of(n, orders):
        if sum(offset) > 0:
            last = max(i for i, steps in enumerate(offset) if steps > 0)
            parent = tuple(steps - (i == last) for i, steps in enumerate(offset))
            edge = (offset, parent, (orders[0][last], orders[1][last]))
            rounds.setdefault(sum(offset), []).append(edge)
    return [rounds[number] for number in sorted(rounds)]


def source_index(me, core, n, orders, offset):
    sizes, strides = chip_dims(n), chip_strides(n)
    found = []
    for order in orders:
        index = me
        for dim, steps in zip(order, offset):
            place = (me // strides[dim]) % sizes[dim]
            index = index + ((place - steps) % sizes[dim] - place) * strides[dim]
        found.append(index)
    return jnp.where(core == 0, found[0], found[1])


def gather_tree(block, n, orders):
    found = {(0,) * len(orders[0]): block}
    for edges in tree(n, orders):
        for offset, parent, dims in edges:
            found[offset] = hop(found[parent], n, dims, 1)
    return found


def scatter_steps(terms, n, orders, sums):
    totals = dict(terms)
    for edges in reversed(tree(n, orders)):
        sent = [hop(totals[offset].astype(BF), n, dims, -1) for offset, _, dims in edges]
        sent, _ = yield sent
        for (_, parent, _), value in zip(edges, sent):
            totals[parent] = totals[parent].astype(F32) + value.astype(F32)
    sums.append(totals[(0,) * len(orders[0])])


def run(job):
    sent = next(job)
    while True:
        try:
            sent = job.send((sent, None))
        except StopIteration:
            return


def scatter_tree(terms, n, orders):
    sums = []
    run(scatter_steps(terms, n, orders, sums))
    return sums[0]


class Background:
    def __init__(self):
        self.jobs = []

    def add(self, job):
        self.jobs.append((job, next(job)))

    def stage(self, *values):
        values, flying = lax.optimization_barrier((values, [sent for _, sent in self.jobs]))
        going = []
        for (job, _), sent in zip(self.jobs, flying):
            try:
                going.append((job, job.send((sent, values[0]))))
            except StopIteration:
                pass
        self.jobs = going
        return values

    def drain(self):
        while self.jobs:
            going = []
            for job, sent in self.jobs:
                try:
                    going.append((job, job.send((sent, None))))
                except StopIteration:
                    pass
            self.jobs = going


def after(value, anchor):
    return value if anchor is None else tie(value, anchor)[0]


def gather_small(value, me, n):
    step = 1
    while step < n:
        other = lax.ppermute(value, "shard", [(i, i ^ step) for i in range(n)])
        lower = (me // step) % 2 == 0
        value = jnp.where(
            lower,
            jnp.concatenate([value, other], axis=0),
            jnp.concatenate([other, value], axis=0),
        )
        step *= 2
    return value


def rms_norm(values):
    return values * lax.rsqrt(jnp.mean(values * values, axis=-1, keepdims=True) + EPS)


def scaled_norm(values, gain_vec):
    return rms_norm(values) * gain_vec


def rope_tables(positions):
    half_width = HEAD_DIM // 2
    frequency = ROPE_BASE ** (-jnp.arange(half_width, dtype=F32) * (2.0 / HEAD_DIM))
    angles = positions.astype(F32)[:, None] * frequency[None, :]
    return (jnp.cos(angles), jnp.sin(angles))


def rotate(vectors, cosine_part, sine_part):
    half_width = vectors.shape[-1] // 2
    first_half = vectors[..., :half_width]
    second_half = vectors[..., half_width:]
    cosine_rows = cosine_part[:, None, :]
    sine_rows = sine_part[:, None, :]
    return jnp.concatenate(
        [
            first_half * cosine_rows - second_half * sine_rows,
            second_half * cosine_rows + first_half * sine_rows,
        ],
        axis=-1,
    )


def query_heads(projected, query_gain, cosine_part, sine_part):
    heads = projected.reshape(projected.shape[0], HEADS, HEAD_DIM)
    return rotate(rms_norm(heads) * query_gain, cosine_part, sine_part)


def key_value_heads(projected, key_gain, cosine_part, sine_part):
    row_count = projected.shape[0]
    key_heads = projected[:, :KW].reshape(row_count, KV_HEADS, HEAD_DIM)
    value_heads = projected[:, KW:].reshape(row_count, KV_HEADS, HEAD_DIM)
    key_heads = rotate(rms_norm(key_heads) * key_gain, cosine_part, sine_part)
    return jnp.concatenate(
        [key_heads.reshape(row_count, KW), rms_norm(value_heads).reshape(row_count, KW)], axis=1
    )


def join_piece(hidden_in, normed, attended, laurel_raw, gain_laurel, gain_attn, gain_ffin):
    joined = (
        hidden_in + rms_norm(attended) * gain_attn + normed + rms_norm(laurel_raw) * gain_laurel
    ) * INV_ROOT2
    return (joined, rms_norm(joined) * gain_ffin)


def gated_gelu(gate_pre, up_pre):
    return jax.nn.gelu(gate_pre, approximate=True) * up_pre


def add_branch(residual, branch, gain_out):
    return residual + rms_norm(branch) * gain_out


def dot(left_side, right_side):
    return jnp.dot(left_side, right_side, preferred_element_type=F32)


def dot_rows(left_side, right_side):
    return lax.dot_general(
        left_side, right_side, (((1,), (1,)), ((), ())), preferred_element_type=F32
    )


def dot_first(left_side, right_side):
    return lax.dot_general(
        left_side, right_side, (((0,), (0,)), ((), ())), preferred_element_type=F32
    )


def halves(value, core):
    left, right = value[..., :HALF], value[..., HALF:]
    return jnp.where(core == 0, left, right), jnp.where(core == 0, right, left)


def rejoin(own, other, core):
    return jnp.concatenate(
        [jnp.where(core == 0, own, other), jnp.where(core == 0, other, own)], axis=-1
    )


def rows_product(value, rows, start, stop, core):
    own, other = halves(value, core)
    return dot_rows(own, rows[0][start:stop]) + dot_rows(other, rows[1][start:stop])


def back_product(value, rows, start, stop, core):
    return rejoin(dot(value, rows[0][start:stop]), dot(value, rows[1][start:stop]), core)


def per_device(tokens, cotangent, block_ids, token_ids, attn_weight, ff_weight, gains, table):
    core = lax.axis_index("section")
    me = lax.axis_index("shard")
    n = lax.axis_size("shard")
    seq = tokens.shape[1]
    rows_dev = attn_weight.shape[1]
    units = ff_weight.shape[2]
    half_units = units // 2
    gains_dev = gains.shape[1]
    vocab_dev = table.shape[1]
    side = chip_dims(n)[2]
    background = Background()

    def pick(for_0, for_1):
        return jnp.where(core == 0, for_0, for_1)

    def by_layer(mine, theirs):
        return (pick(mine, theirs), pick(theirs, mine))

    gain_pair = by_layer(gains[0].astype(F32), swap_cores(gains[0]).astype(F32))
    small = jnp.concatenate([gain_pair[0], gain_pair[1], token_ids.reshape(-1).astype(F32)])
    small_all = gather_small(small[None], me, n)
    layer_gains = [
        small_all[:, layer * gains_dev : (layer + 1) * gains_dev].reshape(n * gains_dev)
        for layer in range(2)
    ]
    all_ids = small_all[:, 2 * gains_dev :].astype(jnp.int32).reshape(-1)

    one_hot = (
        (all_ids - me * vocab_dev)[:, None] == jnp.arange(vocab_dev, dtype=jnp.int32)[None, :]
    ).astype(BF)
    looked_up = dot(one_hot, table[0]).astype(BF)
    looked_up = lax.psum_scatter(looked_up, "shard", scatter_dimension=0, tiled=True)
    looked_up = looked_up.reshape(2, seq, PLD)
    side_theirs = swap_cores(pick(looked_up[1], looked_up[0]))
    side_inputs = [
        value.astype(F32) for value in by_layer(pick(looked_up[0], looked_up[1]), side_theirs)
    ]

    own_half, other_half = halves(attn_weight[0], core)
    attn_blocks = by_layer(own_half, swap_cores(other_half))
    ff_own = by_layer(ff_weight[0], swap_cores(ff_weight[0]))
    ff_half = [lax.dynamic_slice_in_dim(own, core * half_units, half_units, 1) for own in ff_own]
    buffers = [jnp.zeros((n, rows_dev, HALF), BF), jnp.zeros((n, rows_dev, HALF), BF)]

    def store_blocks(buffers, fresh):
        for offset, block in fresh.items():
            sources = [source_index(me, c, n, ALL_CHIPS, offset) for c in (core, 1 - core)]
            buffers = [
                lax.dynamic_update_slice(
                    buffer, value[None], (source, jnp.int32(0), jnp.int32(0))
                )
                for buffer, value, source in zip(buffers, (block, swap_cores(block)), sources)
            ]
        return buffers

    fresh = {(0, 0, 0): attn_blocks[0]}
    held = dict(fresh)
    for edges in tree(n, ALL_CHIPS):
        arriving = {offset: hop(held[parent], n, dims, 1) for offset, parent, dims in edges}
        buffers = store_blocks(buffers, fresh)
        fresh, held, buffers = tie(arriving, held, buffers)
        held.update(fresh)
    last_block = fresh[max(fresh)]
    buffers = store_blocks(buffers, fresh)
    rows_0 = [buffer.reshape(n * rows_dev, HALF) for buffer in buffers]
    next_block, last_block, ff_own, ff_half, _ = tie(
        attn_blocks[1], last_block, ff_own, ff_half, looked_up
    )
    rows_1_own = lax.all_gather(next_block, "shard", axis=0, tiled=True)
    rows_1 = [rows_1_own, swap_cores(rows_1_own)]
    attn_rows = (rows_0, rows_1)

    positions = me * seq + jnp.arange(seq, dtype=jnp.int32)
    cosine_part, sine_part = rope_tables(positions)
    query_split = partial(query_heads, cosine_part=cosine_part, sine_part=sine_part)
    key_value_split = partial(key_value_heads, cosine_part=cosine_part, sine_part=sine_part)
    key_offsets = offsets_of(n, ALL_CHIPS)
    plane_offsets = offsets_of(n, PLANE)
    sources = jnp.stack([source_index(me, core, n, ALL_CHIPS, offset) for offset in key_offsets])
    blocks = pick(block_ids[0], block_ids[1]).reshape(n, seq)
    key_blocks = jnp.take(blocks, sources, axis=0).reshape(-1)
    allowed = key_blocks[None, :] <= key_blocks[:seq, None]
    hidden_b = pick(tokens[0], tokens[1])

    def near_units(layer, anchor, near):
        for which in range(3):
            current = after(ff_half[layer][which], anchor)
            parts = []
            for _ in range(side - 1):
                (current,), anchor = yield [hop(current, n, (2, 2), 1)]
                parts.append(current)
            near.append(parts)

    def plane_gather(value):
        found = gather_tree(value, n, PLANE)
        return jnp.concatenate([found[offset] for offset in plane_offsets], axis=0)

    def plane_scatter(value):
        terms = {o: value[i * seq : (i + 1) * seq] for i, o in enumerate(plane_offsets)}
        return scatter_tree(terms, n, PLANE)

    def split_gains(layer):
        flat = layer_gains[layer]
        return flat[: 6 * D].reshape(6, D), flat[6 * D : 6 * D + HEAD_DIM], flat[6 * D + HEAD_DIM :]

    def forward(layer, hidden_b, near):
        rows = attn_rows[layer]
        gain_rows, query_gain, key_gain = split_gains(layer)
        hidden_in = hidden_b.astype(F32)
        normed = scaled_norm(hidden_in, gain_rows[0])
        normed_b = normed.astype(BF)
        projected_kv = rows_product(normed_b, rows, QW, QW + 2 * KW, core)
        local = key_value_split(projected_kv, key_gain).astype(BF)
        (local,) = background.stage(local)
        found = gather_tree(local, n, ALL_CHIPS)
        projected_q = rows_product(normed_b, rows, 0, QW, core)
        queries_b = query_split(projected_q, query_gain).astype(BF)
        queries_b = queries_b.reshape(seq, KV_HEADS, HEADS // KV_HEADS, HEAD_DIM)
        latent_b = rows_product(normed_b, rows, QW + 2 * KW, IN_ROWS, core).astype(BF)
        laurel_raw = back_product(latent_b, rows, LAUREL_START, SIDE_START, core)
        key_value = jnp.concatenate([found[offset] for offset in key_offsets], axis=0)
        key_value, queries_b, laurel_raw = background.stage(key_value, queries_b, laurel_raw)
        keys_b = key_value[:, :KW].reshape(-1, KV_HEADS, HEAD_DIM)
        values_b = key_value[:, KW:].reshape(-1, KV_HEADS, HEAD_DIM)
        scores = (
            jnp.einsum("qkgd,jkd->kgqj", queries_b, keys_b, preferred_element_type=F32) * SCALE
        )
        scores = jnp.where(allowed, scores, MASKED)
        row_max = jnp.max(scores, axis=-1, keepdims=True)
        exponentials = jnp.exp(scores - row_max)
        probabilities = exponentials / jnp.sum(exponentials, axis=-1, keepdims=True)
        mixed_b = (
            jnp.einsum(
                "kgqj,jkd->qkgd", probabilities.astype(BF), values_b, preferred_element_type=F32
            )
            .reshape(seq, QW)
            .astype(BF)
        )
        attended = back_product(mixed_b, rows, OUT_START, LAUREL_START, core)
        joined, prenorm = join_piece(
            hidden_in, normed, attended, laurel_raw, gain_rows[1], gain_rows[2], gain_rows[3]
        )
        (prenorm_b,) = background.stage(prenorm.astype(BF))
        prenorm_all = plane_gather(prenorm_b)
        (prenorm_all,) = background.stage(prenorm_all)
        while len(near) < 3:
            (prenorm_all,) = background.stage(prenorm_all)
        weights = [
            [ff_own[layer][which]]
            + [part for through in near[which] for part in (through, swap_cores(through))]
            for which in range(3)
        ]
        gate = [dot_rows(prenorm_all, part) for part in weights[0]]
        up = [dot_rows(prenorm_all, part) for part in weights[1]]
        hidden_ff_b = [gated_gelu(g, u).astype(BF) for g, u in zip(gate, up)]
        down_out = plane_scatter(sum(dot(h, part) for h, part in zip(hidden_ff_b, weights[2])))
        (down_out,) = background.stage(down_out)
        settled = add_branch(joined, down_out, gain_rows[4])
        settled_b = settled.astype(BF)
        side_gate = rows_product(settled_b, rows, IN_ROWS, OUT_START, core)
        gated_b = gated_gelu(side_gate, side_inputs[layer]).astype(BF)
        projected = back_product(gated_b, rows, SIDE_START, SIDE_START + PLD, core)
        layer_out_b = add_branch(settled, projected, gain_rows[5]).astype(BF)
        return layer_out_b, dict(
            hidden_in=hidden_in,
            normed=normed,
            normed_b=normed_b,
            projected_q=projected_q,
            projected_kv=projected_kv,
            weights=weights,
            queries_b=queries_b,
            keys_b=keys_b,
            values_b=values_b,
            probabilities=probabilities,
            mixed_b=mixed_b,
            attended=attended,
            latent_b=latent_b,
            laurel_raw=laurel_raw,
            joined=joined,
            prenorm_all=prenorm_all,
            gate=gate,
            up=up,
            hidden_ff_b=hidden_ff_b,
            down_out=down_out,
            settled=settled,
            settled_b=settled_b,
            side_gate=side_gate,
            gated_b=gated_b,
            projected=projected,
        )

    def early_products(pairs):
        lefts = jnp.concatenate([left for left, _ in pairs], axis=1)
        lefts = jnp.concatenate([lefts, swap_cores(lefts)], axis=0)
        own, other = halves(jnp.stack([right for _, right in pairs]), core)
        rights = jnp.concatenate([own, swap_cores(other)], axis=1)
        terms = [jnp.zeros((IN_ROWS - upper_rows, HALF), BF)]
        start = 0
        for i, (left, _) in enumerate(pairs):
            stop = start + left.shape[1]
            terms.append(dot_first(lefts[:, start:stop], rights[i]).astype(BF))
            start = stop
        return jnp.concatenate(terms, axis=0)

    first = (rows_dev // 2 + 7) // 8 * 8
    upper_rows = n // 2 * rows_dev

    def early_rows(term, result):
        shaped = term.reshape(n // 2, rows_dev, HALF)
        upper = me >= n // 2
        pieces = {}
        for offset in key_offsets:
            target = source_index(me, core, n, ALL_CHIPS, offset)
            place = (target % (n // 2), jnp.where(target >= n // 2, 0, rows_dev - first), 0)
            pieces[offset] = lax.dynamic_slice(shaped, place, (1, first, HALF))[0]
        sums = []
        yield from scatter_steps(pieces, n, ALL_CHIPS, sums)
        mine = sums[0].astype(BF)
        sent = lax.ppermute(mine, "shard", [(i, i + n // 2) for i in range(n // 2)])
        (sent,), _ = yield [sent]
        whole = jnp.concatenate([mine, sent[2 * first - rows_dev :]], axis=0).astype(F32)
        result.append(jnp.where(upper, whole, 0.0))

    def backward(layer, kept, grad_out_b, passed, early, due):
        rows = attn_rows[layer]
        weights = kept["weights"]
        gain_rows, query_gain, key_gain = split_gains(layer)
        grad_out = grad_out_b.astype(F32)
        grad_settled, grad_projected, grad_gain5 = jax.vjp(
            add_branch, kept["settled"], kept["projected"], gain_rows[5]
        )[1](grad_out)
        grad_projected_b = grad_projected.astype(BF)
        grad_gated = rows_product(grad_projected_b, rows, SIDE_START, SIDE_START + PLD, core)
        grad_side_gate, grad_side = jax.vjp(gated_gelu, kept["side_gate"], side_inputs[layer])[1](
            grad_gated
        )
        grad_side_gate_b = grad_side_gate.astype(BF)
        grad_settled = grad_settled + back_product(
            grad_side_gate_b, rows, IN_ROWS, OUT_START, core
        )
        grad_joined, grad_down, grad_gain4 = jax.vjp(
            add_branch, kept["joined"], kept["down_out"], gain_rows[4]
        )[1](grad_settled)
        due[0].append(grad_side.astype(BF))
        (grad_down_b,) = background.stage(grad_down.astype(BF))
        grad_down_all = plane_gather(grad_down_b)
        (grad_down_all,) = background.stage(grad_down_all)
        grad_hidden_ff = [dot_rows(grad_down_all, part) for part in weights[2]]
        grad_gate_up = [
            jax.vjp(gated_gelu, g, u)[1](grad)
            for g, u, grad in zip(kept["gate"], kept["up"], grad_hidden_ff)
        ]
        grad_gate_b = [pair[0].astype(BF) for pair in grad_gate_up]
        grad_up_b = [pair[1].astype(BF) for pair in grad_gate_up]
        grad_prenorm = sum(
            dot(g, wg) + dot(u, wu)
            for g, u, wg, wu in zip(grad_gate_b, grad_up_b, weights[0], weights[1])
        )
        grad_prenorm, grad_gate_b, grad_up_b = tie(grad_prenorm, grad_gate_b, grad_up_b)
        grad_prenorm = plane_scatter(grad_prenorm)
        ff_terms = [
            [dot_first(g, kept["prenorm_all"]).astype(BF) for g in grad_gate_b],
            [dot_first(u, kept["prenorm_all"]).astype(BF) for u in grad_up_b],
            [dot_first(h, grad_down_all).astype(BF) for h in kept["hidden_ff_b"]],
        ]
        ff_base = jnp.stack([terms[0] for terms in ff_terms])
        pair_sums = [
            [
                (terms[1 + 2 * i].astype(F32) + swap_cores(terms[2 + 2 * i]).astype(F32)).astype(BF)
                for i in range(side - 1)
            ]
            for terms in ff_terms
        ]
        grad_prenorm, pair_sums, ff_base = background.stage(grad_prenorm, pair_sums, ff_base)

        def pass_back():
            anchor = None
            for which in range(3):
                carried = None
                for steps in range(side - 1, 0, -1):
                    term = after(pair_sums[which][steps - 1], anchor)
                    if carried is not None:
                        term = (term.astype(F32) + carried.astype(F32)).astype(BF)
                    (carried,), anchor = yield [hop(term, n, (2, 2), -1)]
                passed.append(carried)

        background.add(pass_back())
        join_pull = jax.vjp(
            join_piece,
            kept["hidden_in"],
            kept["normed"],
            kept["attended"],
            kept["laurel_raw"],
            gain_rows[1],
            gain_rows[2],
            gain_rows[3],
        )[1]
        grad_hidden, grad_normed, grad_attended, grad_laurel, grad_gain1, grad_gain2, grad_gain3 = (
            join_pull((grad_joined, grad_prenorm))
        )
        grad_attended_b = grad_attended.astype(BF)
        grad_laurel_b = grad_laurel.astype(BF)
        grad_mixed_b = rows_product(grad_attended_b, rows, OUT_START, LAUREL_START, core).astype(BF)
        grad_latent = rows_product(grad_laurel_b, rows, LAUREL_START, SIDE_START, core)
        grad_mixed_heads = grad_mixed_b.reshape(seq, KV_HEADS, HEADS // KV_HEADS, HEAD_DIM)
        probabilities = kept["probabilities"]
        grad_probs = jnp.einsum(
            "qkgd,jkd->kgqj", grad_mixed_heads, kept["values_b"], preferred_element_type=F32
        )
        row_dot = jnp.sum(grad_probs * probabilities, axis=-1, keepdims=True)
        grad_scores_b = (probabilities * (grad_probs - row_dot)).astype(BF)
        grad_keys_all = (
            jnp.einsum(
                "kgqj,qkgd->jkd", grad_scores_b, kept["queries_b"], preferred_element_type=F32
            )
            * SCALE
        )
        grad_values_all = jnp.einsum(
            "kgqj,qkgd->jkd",
            probabilities.astype(BF),
            grad_mixed_heads,
            preferred_element_type=F32,
        )
        grad_key_value = jnp.concatenate(
            [grad_keys_all.reshape(-1, KW), grad_values_all.reshape(-1, KW)], axis=1
        ).astype(BF)
        early_pairs = (
            (grad_side_gate_b, kept["settled_b"]),
            (kept["mixed_b"], grad_attended_b),
            (kept["latent_b"], grad_laurel_b),
            (kept["gated_b"], grad_projected_b),
        )
        work = due[1]() if callable(due[1]) else due[1]
        grad_key_value, early_pairs, work = background.stage(grad_key_value, early_pairs, work)
        early_term = early_products(early_pairs)
        due[1] = due[2](work)
        terms = {o: grad_key_value[i * seq : (i + 1) * seq] for i, o in enumerate(key_offsets)}
        grad_local = scatter_tree(terms, n, ALL_CHIPS)
        grad_queries = (
            jnp.einsum("kgqj,jkd->qkgd", grad_scores_b, kept["keys_b"], preferred_element_type=F32)
            * SCALE
        )
        grad_projected_q, grad_query_gain = jax.vjp(query_split, kept["projected_q"], query_gain)[
            1
        ](grad_queries.reshape(seq, HEADS, HEAD_DIM))
        grad_q_b, grad_z_b = grad_projected_q.astype(BF), grad_latent.astype(BF)
        grad_normed = (
            grad_normed
            + back_product(grad_q_b, rows, 0, QW, core)
            + back_product(grad_z_b, rows, QW + 2 * KW, IN_ROWS, core)
        )
        grad_local, grad_normed, early_term, due[1] = background.stage(
            grad_local, grad_normed, early_term, due[1]
        )
        if layer == 1:
            background.add(early_rows(early_term, early))
        else:
            early.append(early_term)
        grad_projected_kv, grad_key_gain = jax.vjp(
            key_value_split, kept["projected_kv"], key_gain
        )[1](grad_local)
        grad_kv_b = grad_projected_kv.astype(BF)
        grad_normed = grad_normed + back_product(grad_kv_b, rows, QW, QW + 2 * KW, core)
        grad_front, grad_gain0 = jax.vjp(scaled_norm, kept["hidden_in"], gain_rows[0])[1](
            grad_normed
        )
        grad_hidden_b = (grad_hidden + grad_front).astype(BF)
        gain_vec = jnp.concatenate(
            [
                grad_gain0,
                grad_gain1,
                grad_gain2,
                grad_gain3,
                grad_gain4,
                grad_gain5,
                grad_query_gain,
                grad_key_gain,
            ]
        )
        late = jnp.concatenate([grad_q_b, grad_kv_b, grad_z_b], axis=1)
        return grad_hidden_b, late, ff_base, gain_vec

    near_0, near_1 = [], []
    background.add(near_units(0, last_block, near_0))
    out_0, kept_0 = forward(0, hidden_b, near_0)
    background.add(near_units(1, out_0, near_1))
    out_1, kept_1 = forward(1, out_0, near_1)
    normed_all_0 = lax.all_gather(
        tie(kept_0["normed_b"], rows_1_own)[0], "shard", axis=0, tiled=True
    )
    normed_all_1 = lax.all_gather(
        tie(kept_1["normed_b"], normed_all_0)[0], "shard", axis=0, tiled=True
    )
    top = pick(cotangent[0], cotangent[1])
    passed_0, passed_1, early_0, early_1, sides = [], [], [], [], []
    due_1 = [sides, normed_all_0, lambda work: work]
    grad_1, late_1, ff_base_1, gain_vec_1 = backward(1, kept_1, top, passed_1, early_1, due_1)
    normed_all_0 = due_1[1]

    def table_grads(work):
        side_all, normed_all = work
        return dot_first(one_hot, side_all), normed_all

    def gather_sides():
        keep = pick(sides[1], sides[0])
        other = swap_cores(pick(sides[0], sides[1]))
        two = jnp.concatenate([pick(keep, other), pick(other, keep)], axis=0)
        return lax.all_gather(two, "shard", axis=0, tiled=True)

    due_0 = [sides, None, table_grads]
    due_0_start = lambda: (gather_sides(), normed_all_1)
    due_0[1] = due_0_start
    grad_0, late_0, ff_base_0, gain_vec_0 = backward(0, kept_0, grad_1, passed_0, early_0, due_0)
    table_grad, normed_all_1 = due_0[1]

    def to_owners(late):
        padded = jnp.pad(late, ((0, 0), (0, n * rows_dev - IN_ROWS)))
        return padded.reshape(seq, n, rows_dev).transpose(1, 0, 2)

    gain_terms = jnp.concatenate(
        [gain_vec_0.reshape(n, gains_dev), gain_vec_1.reshape(n, gains_dev)], axis=1
    ).astype(BF)
    width = 2 * rows_dev
    gain_lines = -(-2 * gains_dev // width)
    gain_lines_padded = -(-gain_lines // 8) * 8
    gain_terms = jnp.pad(gain_terms, ((0, 0), (0, gain_lines_padded * width - 2 * gains_dev)))
    outgoing = jnp.concatenate(
        [
            jnp.concatenate([to_owners(late_0), to_owners(late_1)], axis=2),
            gain_terms.reshape(n, gain_lines_padded, width),
        ],
        axis=1,
    )
    (outgoing, ff_base_0, ff_base_1, early_0[0]) = background.stage(
        outgoing, ff_base_0, ff_base_1, early_0[0]
    )
    incoming = lax.all_to_all(outgoing, "shard", 0, 0, tiled=True)
    late_sums = [
        dot_first(
            incoming[:, :seq, layer * rows_dev : (layer + 1) * rows_dev].reshape(
                n * seq, rows_dev
            ),
            normed_all,
        )
        for layer, normed_all in enumerate((normed_all_0, normed_all_1))
    ]
    run(early_rows(early_0.pop(), early_0))
    background.drain()
    early_keep = pick(early_0[0], early_1[0])
    early_other = swap_cores(pick(early_1[0], early_0[0]))
    attn_grad = (
        pick(late_sums[0], late_sums[1])
        + swap_cores(pick(late_sums[1], late_sums[0]).astype(BF)).astype(F32)
        + rejoin(early_keep, early_other, core)
    )
    gain_sums = jnp.sum(incoming[:, seq:].astype(F32), axis=0).reshape(-1)
    gain_sums = (gain_sums[:gains_dev], gain_sums[gains_dev : 2 * gains_dev])
    gain_grad = pick(gain_sums[0], gain_sums[1]) + swap_cores(pick(gain_sums[1], gain_sums[0]))

    def whole_ff(base, passed):
        passed = jnp.stack(passed)
        zeros = jnp.zeros((3, units - half_units, D), BF)
        placed = pick(
            jnp.concatenate([passed, zeros], axis=1), jnp.concatenate([zeros, passed], axis=1)
        )
        return base.astype(F32) + placed.astype(F32)

    whole_0, whole_1 = whole_ff(ff_base_0, passed_0), whole_ff(ff_base_1, passed_1)
    ff_grad = pick(whole_0, whole_1) + swap_cores(pick(whole_1, whole_0).astype(BF)).astype(F32)

    def outputs_of(value_0, value_1):
        keep = pick(value_0, value_1)
        other = swap_cores(pick(value_1, value_0))
        return jnp.stack([pick(keep, other), pick(other, keep)])

    return (
        outputs_of(out_0, out_1)[None],
        outputs_of(grad_0, grad_1)[None],
        attn_grad[None],
        ff_grad[None],
        gain_grad[None],
        table_grad[None],
    )


def solution(mesh):
    placed = (
        P(None, "shard", None),
        P(None, "shard", None),
        P(),
        P(None, "shard"),
        P("section", "shard", None),
        P("section", None, "shard", None),
        P("section", "shard"),
        P("section", "shard", None),
    )
    return jax.shard_map(
        per_device,
        mesh=mesh,
        in_specs=placed,
        out_specs=(
            P("section", None, "shard", None),
            P("section", None, "shard", None),
            P("section", "shard", None),
            P("section", None, "shard", None),
            P("section", "shard"),
            P("section", "shard", None),
        ),
        check_vma=False,
    )
```

time: 1440 us -> 1350 us (0.938)
  starting transfers between devices: 299 us -> 248 us
  matrix products: 223 us -> 271 us
  other arithmetic: 164 us -> 125 us
  local copies, waits for them, and re-layouts: 170 us -> 136 us
  blocking collectives: 25.4 us -> 0 us
    ppermute x67 -> x44, starting transfers between devices: 142 us -> 86.7 us  [swap_cores(): return lax.ppermute(value, 'section', [(0, 1), (1, 0)])]
    all_gather x2 -> x4, waiting for transfers between devices: 0.01 us -> 34.9 us  [the longest x1 34.9 us: per_device(): lax.all_gather(tie(kept_0['normed_b'], rows_1_own)[0], 'shard', axis=0, t...]
    dynamic_update_slice x80 -> x31, local copies, waits for them, and re-layouts: 61.3 us -> 34.2 us  [store_blocks(): lax.dynamic_update_slice(buffer, value[None], (source, jnp.int32(0), jnp....]
    all_gather x1 -> x0, blocking collectives: 25.4 us -> none  [per_device(): all_ids = lax.all_gather(token_ids.reshape(-1), 'shard', axis=0, tiled=True)]
    dot_general x27 -> x47, matrix products: 66.2 us -> 91.4 us  [dot(): return jnp.dot(left_side, right_side, preferred_element_type=F32)]
    dot_general x26 -> x46, matrix products: 78.5 us -> 98.5 us  [dot_rows(): lax.dot_general(left_side, right_side, (((1,), (1,)), ((), ())), preferre...]
    concatenate x14 -> x11, other arithmetic: 23.6 us -> 5.75 us  [the longest x2 3.41 us: backward(): jnp.concatenate([grad_keys_all.reshape(-1, KW), grad_values_all.reshape(-...]
    slice x26 -> x6, local copies, waits for them, and re-layouts: 21 us -> 4.33 us  [the longest x1 1.9 us: per_device(): incoming[:, :seq, layer * rows_dev:(layer + 1) * rows_dev]]
  transfers between devices with their start and end apart: 251 -> 229, of which waited for: 93 -> 98; matrix products, arithmetic and copies ran while one was open for 36% -> 35% of each run, Pallas kernels for 0% -> 0%
where the time goes in v2:
time: 1350 us; the launch traced here: 1340 us
  waiting for transfers between devices  535 us (40%)
  matrix products  271 us (20%)
  starting transfers between devices  248 us (18%)
  local copies, waits for them, and re-layouts  136 us (10%)
  other arithmetic  125 us (9%)
  between operations  20.9 us (2%)
    ppermute x173, waiting for transfers between devices, hop(): return lax.ppermute(value, ('section', 'shard'), pairs)  462 us
    ppermute x173, starting transfers between devices, hop(): return lax.ppermute(value, ('section', 'shard'), pairs)  146 us
    dot_general x46, matrix products, dot_rows(): lax.dot_general(left_side, right_side, (((1,), (1,)), ((), ())), preferre...  98.5 us
    dot_general x47, matrix products, dot(): return jnp.dot(left_side, right_side, preferred_element_type=F32)  91.4 us
    ppermute x44, starting transfers between devices, swap_cores(): return lax.ppermute(value, 'section', [(0, 1), (1, 0)])  86.7 us
    dot_general x29, matrix products, dot_first(): lax.dot_general(left_side, right_side, (((0,), (0,)), ((), ())), preferre...  58.1 us
    all_gather x1, waiting for transfers between devices, per_device(): lax.all_gather(tie(kept_0['normed_b'], rows_1_own)[0], 'shard', axis=0, t...  34.9 us
    dynamic_update_slice x31, local copies, waits for them, and re-layouts, store_blocks(): lax.dynamic_update_slice(buffer, value[None], (source, jnp.int32(0), jnp....  34.2 us
  transfers between devices with their start and end apart: 229, of which 98 were waited for; matrix products, arithmetic and copies ran while one was open for 35% of the time, Pallas kernels for 0%

profile of v2, /device:TPU:27, one launch (start us, length us, event | category | flops | bytes accessed | tf_op | source)
XLA Modules:
  0.0 1337.2 jit_solution(9011649803824774547)
XLA Ops:
  12.4 6.0 broadcast.717.clone
  25.1 5.8 broadcast.717
  33.0 4.0 collective-permute-done.6
  54.7 11.7 collective-permute-done.11
  82.7 5.2 collective-permute-done.17
  87.9 11.9 collective-permute-done.18
  111.0 9.0 collective-permute-done.25
  120.0 11.8 collective-permute-done.26
  139.7 4.0 collective-permute-done.32
  166.1 4.2 collective-permute-start.4
  170.3 5.8 collective-permute-done.4
  187.9 4.4 fusion.36
  209.2 27.7 %collective-permute-done.38 = bf16[256,2048]{1,0:T(8,128)(2,1)S(1)} collective-permute-done((bf16[256,2048]{1,0:T(8,128)(2,1)S(1)}, bf16[256,2048]{1,0:T(8,128)(2,1)S(1)}, u32[]{:S(2)}, u32[]{:S(2)}) %collective-permute-start.38) | collective-permute-done | bytes 1048608 | tf_op jit(solution)/shard_map/ppermute | solution.py:58
  240.1 10.0 collective-permute-done.42
  251.6 12.1 collective-permute-done.46
  263.9 34.3 %collective-permute-done.41 = bf16[64,1024]{1,0:T(8,128)(2,1)S(1)} collective-permute-done((bf16[64,1024]{1,0:T(8,128)(2,1)S(1)}, bf16[64,1024]{1,0:T(8,128)(2,1)S(1)}, u32[]{:S(2)}, u32[]{:S(2)}) %collective-permute-start.41) | collective-permute-done | bytes 131104 | tf_op jit(solution)/shard_map/ppermute | solution.py:58
  302.9 5.4 collective-permute-done.45
  312.6 5.4 collective-permute-done.49
  318.0 4.1 collective-permute-done.53
  345.4 7.2 fusion.45
  356.1 5.7 collective-permute-done.59
  397.7 4.2 collective-permute-done.69
  415.0 11.1 collective-permute-start.73
  436.5 4.1 collective-permute-done.72
  454.0 4.4 fusion.20
  462.7 10.0 collective-permute-done.75
  492.0 14.7 %collective-permute-done.78 = bf16[64,1024]{1,0:T(8,128)(2,1)S(1)} collective-permute-done((bf16[64,1024]{1,0:T(8,128)(2,1)}, bf16[64,1024]{1,0:T(8,128)(2,1)S(1)}, u32[]{:S(2)}, u32[]{:S(2)}) %collective-permute-start.78) | collective-permute-done | bytes 131104 | tf_op jit(solution)/shard_map/ppermute | solution.py:58
  555.3 6.2 collective-permute-done.96
  562.7 4.7 collective-permute-done.98
  602.0 4.7 collective-permute-done.107
  609.5 12.1 collective-permute-done.108
  623.7 6.7 collective-permute-done.109
  647.6 34.9 %all-gather.7.cloned.1.call-done = bf16[1024,2048]{1,0:T(8,128)(2,1)} async-done(((bf16[64,2048]{1,0:T(8,128)(2,1)}), bf16[1024,2048]{1,0:T(8,128)(2,1)}) %all-gather.7.cloned.1.call-update) | async-done | bytes 4194320 | tf_op jit(solution)/shard_map/all_gather | solution.py:657
  695.2 8.3 collective-permute-done.116
  706.7 4.5 collective-permute-done.117
  711.2 4.2 fusion.41
  741.4 11.0 collective-permute-done.121
  753.9 9.6 collective-permute-done.120
  763.7 5.9 collective-permute-done.122
  773.0 5.4 collective-permute-done.123
  793.1 4.4 fusion.76
  824.0 7.6 collective-permute-done.128
  838.5 5.1 collective-permute-start.144
  869.7 13.6 %collective-permute-done.129 = bf16[64,1024]{1,0:T(8,128)(2,1)S(1)} collective-permute-done((bf16[64,1024]{1,0:T(8,128)(2,1)S(1)}, bf16[64,1024]{1,0:T(8,128)(2,1)S(1)}, u32[]{:S(2)}, u32[]{:S(2)}) %collective-permute-start.129) | collective-permute-done | bytes 131104 | tf_op jit(solution)/shard_map/ppermute | solution.py:58
  883.5 4.0 dynamic-slice_bitcast_fusion.8
  932.4 4.2 collective-permute-start.154
  941.5 9.3 collective-permute-done.155
  987.8 4.8 collective-permute-done.161
  1063.9 5.7 collective-permute-done.178
  1069.7 7.2 collective-permute-start.194
  1091.4 11.3 fusion.2
  1114.2 23.3 %collective-permute-done.179 = bf16[64,1024]{1,0:T(8,128)(2,1)S(1)} collective-permute-done((bf16[64,1024]{1,0:T(8,128)(2,1)S(1)}, bf16[64,1024]{1,0:T(8,128)(2,1)S(1)}, u32[]{:S(2)}, u32[]{:S(2)}) %collective-permute-start.179) | collective-permute-done | bytes 131104 | tf_op jit(solution)/shard_map/ppermute | solution.py:58
  1142.4 5.2 collective-permute-done.193
  1167.5 10.1 collective-permute-done.201
  1189.3 6.8 all-to-all-start
  1206.2 9.2 select_convert_fusion
  1215.4 20.5 %collective-permute-start.221 = (bf16[3,512,2048]{2,1,0:T(8,128)(2,1)}, bf16[3,512,2048]{2,1,0:T(8,128)(2,1)}, u32[]{:S(2)}, u32[]{:S(2)}) collective-permute-start(bf16[3,512,2048]{2,1,0:T(8,128)(2,1)} %select_convert_fusion), channel_id=1, source_target_pairs={{0,16},{16,0},{1,17},{17,1},{2,18},{18,2},{3,19},{19,3},{4,20},{20... | collective-permute-start | bytes 18874376 | tf_op jit(solution)/shard_map/ppermute | solution.py:62
  1238.7 7.4 collective-permute-done.210
  1250.8 4.3 collective-permute-done.207
  1265.0 5.0 collective-permute-done.218
  1278.9 12.2 collective-permute-done.219
  1295.0 4.1 fusion.594
  1311.4 5.8 fusion.38
  1318.8 11.5 add_bitcast_fusion
  (1726 shorter events, 751.2 us)
Async XLA Ops:
  7.2 364.6 %all-gather.5.cloned.1.call-start = ((), (), s32[]{:S(2)}) async-start(), calls=%async_computation.3 | async-start | bytes 12533760 | tf_op jit(solution)/shard_map/all_gather | solution.py:338
  21.8 122.7 %collective-permute-start.37 = (bf16[3,512,2048]{2,1,0:T(8,128)(2,1)}, bf16[3,512,2048]{2,1,0:T(8,128)(2,1)}, u32[]{:S(2)}, u32[]{:S(2)}) collective-permute-start(bf16[3,512,2048]{2,1,0:T(8,128)(2,1)} %bitcast.663), channel_id=1, source_target_pairs={{0,16},{16,0},{1,17},{17,1},{2,18},{18,2},{3,19},{19,3},{4,20},{20... | collective-permute-start | bytes 18874376 | tf_op jit(solution)/shard_map/ppermute | solution.py:62
  74.9 24.9 %collective-permute-start.18 = (bf16[360,1024]{1,0:T(8,128)(2,1)S(1)}, bf16[360,1024]{1,0:T(8,128)(2,1)S(1)}, u32[]{:S(2)}, u32[]{:S(2)}) collective-permute-start(bf16[360,1024]{1,0:T(8,128)(2,1)S(1)} %collective-permute-done.13), channel_id=1, source_target_pairs={{0,2},{1,3},{2,0},{3,1},{4,6},{5,7},{6,4},{7,5},{8,10},{9,11},{10,... | collective-permute-start | bytes 2211848 | tf_op jit(solution)/shard_map/ppermute | solution.py:58
  75.8 24.0 %collective-permute-start.19 = (bf16[360,1024]{1,0:T(8,128)(2,1)S(1)}, bf16[360,1024]{1,0:T(8,128)(2,1)S(1)}, u32[]{:S(2)}, u32[]{:S(2)}) collective-permute-start(bf16[360,1024]{1,0:T(8,128)(2,1)S(1)} %collective-permute-done.13), channel_id=1, source_target_pairs={{0,1},{1,0},{2,3},{3,2},{4,5},{5,4},{6,7},{7,6},{8,9},{9,8},{10,11... | collective-permute-start | bytes 2211848 | tf_op jit(solution)/shard_map/ppermute | solution.py:58
  76.3 23.6 %collective-permute-start.20 = (bf16[360,1024]{1,0:T(8,128)(2,1)S(1)}, bf16[360,1024]{1,0:T(8,128)(2,1)S(1)}, u32[]{:S(2)}, u32[]{:S(2)}) collective-permute-start(bf16[360,1024]{1,0:T(8,128)(2,1)S(1)} %collective-permute-done.13), channel_id=1, source_target_pairs={{0,4},{1,5},{2,6},{3,7},{4,8},{5,9},{6,10},{7,11},{8,12},{9,13},{1... | collective-permute-start | bytes 2211848 | tf_op jit(solution)/shard_map/ppermute | solution.py:58
  106.9 24.9 %collective-permute-start.26 = (bf16[360,1024]{1,0:T(8,128)(2,1)S(1)}, bf16[360,1024]{1,0:T(8,128)(2,1)S(1)}, u32[]{:S(2)}, u32[]{:S(2)}) collective-permute-start(bf16[360,1024]{1,0:T(8,128)(2,1)S(1)} %collective-permute-done.20), channel_id=1, source_target_pairs={{0,2},{1,3},{2,0},{3,1},{4,6},{5,7},{6,4},{7,5},{8,10},{9,11},{10,... | collective-permute-start | bytes 2211848 | tf_op jit(solution)/shard_map/ppermute | solution.py:58
  107.8 24.0 %collective-permute-start.27 = (bf16[360,1024]{1,0:T(8,128)(2,1)S(1)}, bf16[360,1024]{1,0:T(8,128)(2,1)S(1)}, u32[]{:S(2)}, u32[]{:S(2)}) collective-permute-start(bf16[360,1024]{1,0:T(8,128)(2,1)S(1)} %collective-permute-done.20), channel_id=1, source_target_pairs={{0,1},{1,0},{2,3},{3,2},{4,5},{5,4},{6,7},{7,6},{8,9},{9,8},{10,11... | collective-permute-start | bytes 2211848 | tf_op jit(solution)/shard_map/ppermute | solution.py:58
  154.8 259.4 %reduce-scatter.2.cloned.1.call-start = ((), (), s32[]{:S(2)}) async-start(), calls=%async_computation.2 | async-start | bytes 1114112 | tf_op jit(solution)/shard_map/reduce_scatter | solution.py:301
  205.8 31.1 %collective-permute-start.38 = (bf16[256,2048]{1,0:T(8,128)(2,1)S(1)}, bf16[256,2048]{1,0:T(8,128)(2,1)S(1)}, u32[]{:S(2)}, u32[]{:S(2)}) collective-permute-start(bf16[256,2048]{1,0:T(8,128)(2,1)S(1)} %get-tuple-element.376), channel_id=1, source_target_pairs={{0,1},{1,0},{2,3},{3,2},{4,5},{5,4},{6,7},{7,6},{8,9},{9,8},{10,11... | collective-permute-start | bytes 3145736 | tf_op jit(solution)/shard_map/ppermute | solution.py:58
  239.6 82.6 %collective-permute-start.54 = (bf16[256,2048]{1,0:T(8,128)(2,1)S(1)}, bf16[256,2048]{1,0:T(8,128)(2,1)S(1)}, u32[]{:S(2)}, u32[]{:S(2)}) collective-permute-start(bf16[256,2048]{1,0:T(8,128)(2,1)S(1)} %get-tuple-element.172), channel_id=1, source_target_pairs={{0,1},{1,0},{2,3},{3,2},{4,5},{5,4},{6,7},{7,6},{8,9},{9,8},{10,11... | collective-permute-start | bytes 3145736 | tf_op jit(solution)/shard_map/ppermute | solution.py:58
  250.0 48.4 %collective-permute-start.43 = (bf16[64,1024]{1,0:T(8,128)(2,1)S(1)}, bf16[64,1024]{1,0:T(8,128)(2,1)S(1)}, u32[]{:S(2)}, u32[]{:S(2)}) collective-permute-start(bf16[64,1024]{1,0:T(8,128)(2,1)S(1)} %collective-permute-done.42), channel_id=1, source_target_pairs={{0,2},{1,3},{2,0},{3,1},{4,6},{5,7},{6,4},{7,5},{8,10},{9,11},{10,... | collective-permute-start | bytes 393224 | tf_op jit(solution)/shard_map/ppermute | solution.py:58
  250.5 49.5 %collective-permute-start.44 = (bf16[64,1024]{1,0:T(8,128)(2,1)S(1)}, bf16[64,1024]{1,0:T(8,128)(2,1)S(1)}, u32[]{:S(2)}, u32[]{:S(2)}) collective-permute-start(bf16[64,1024]{1,0:T(8,128)(2,1)S(1)} %collective-permute-done.42), channel_id=1, source_target_pairs={{0,1},{1,0},{2,3},{3,2},{4,5},{5,4},{6,7},{7,6},{8,9},{9,8},{10,11... | collective-permute-start | bytes 393224 | tf_op jit(solution)/shard_map/ppermute | solution.py:58
  250.5 47.8 %collective-permute-start.41 = (bf16[64,1024]{1,0:T(8,128)(2,1)S(1)}, bf16[64,1024]{1,0:T(8,128)(2,1)S(1)}, u32[]{:S(2)}, u32[]{:S(2)}) collective-permute-start(bf16[64,1024]{1,0:T(8,128)(2,1)S(1)} %collective-permute-done.40), channel_id=1, source_target_pairs={{0,2},{1,3},{2,0},{3,1},{4,6},{5,7},{6,4},{7,5},{8,10},{9,11},{10,... | collective-permute-start | bytes 393224 | tf_op jit(solution)/shard_map/ppermute | solution.py:58
  263.7 45.2 %collective-permute-start.47 = (bf16[64,1024]{1,0:T(8,128)(2,1)S(1)}, bf16[64,1024]{1,0:T(8,128)(2,1)S(1)}, u32[]{:S(2)}, u32[]{:S(2)}) collective-permute-start(bf16[64,1024]{1,0:T(8,128)(2,1)S(1)} %collective-permute-done.46), channel_id=1, source_target_pairs={{0,2},{1,3},{2,0},{3,1},{4,6},{5,7},{6,4},{7,5},{8,10},{9,11},{10,... | collective-permute-start | bytes 393224 | tf_op jit(solution)/shard_map/ppermute | solution.py:58
  352.6 329.8 %all-gather.7.cloned.1.call-start = ((), (), s32[]{:S(2)}) async-start(), calls=%async_computation.4 | async-start | bytes 4456448 | tf_op jit(solution)/shard_map/all_gather | solution.py:657
  352.7 28.8 %collective-permute-start.63 = (bf16[256,2048]{1,0:T(8,128)(2,1)}, bf16[256,2048]{1,0:T(8,128)(2,1)}, u32[]{:S(2)}, u32[]{:S(2)}) collective-permute-start(bf16[256,2048]{1,0:T(8,128)(2,1)} %copy-done.148), channel_id=1, source_target_pairs={{0,16},{16,0},{1,17},{17,1},{2,18},{18,2},{3,19},{19,3},{4,20},{20... | collective-permute-start | bytes 3145736 | tf_op jit(solution)/shard_map/ppermute | solution.py:62
  352.8 34.4 %collective-permute-start.64 = (bf16[256,2048]{1,0:T(8,128)(2,1)}, bf16[256,2048]{1,0:T(8,128)(2,1)}, u32[]{:S(2)}, u32[]{:S(2)}) collective-permute-start(bf16[256,2048]{1,0:T(8,128)(2,1)} %copy-done.150), channel_id=1, source_target_pairs={{0,16},{16,0},{1,17},{17,1},{2,18},{18,2},{3,19},{19,3},{4,20},{20... | collective-permute-start | bytes 3145736 | tf_op jit(solution)/shard_map/ppermute | solution.py:62
  353.3 40.8 %collective-permute-start.65 = (bf16[256,2048]{1,0:T(8,128)(2,1)}, bf16[256,2048]{1,0:T(8,128)(2,1)}, u32[]{:S(2)}, u32[]{:S(2)}) collective-permute-start(bf16[256,2048]{1,0:T(8,128)(2,1)} %collective-permute-done.55), channel_id=1, source_target_pairs={{0,16},{16,0},{1,17},{17,1},{2,18},{18,2},{3,19},{19,3},{4,20},{20... | collective-permute-start | bytes 3145736 | tf_op jit(solution)/shard_map/ppermute | solution.py:62
  371.8 86.7 %collective-permute-start.74 = (bf16[5760,1024]{1,0:T(8,128)(2,1)}, bf16[5760,1024]{1,0:T(8,128)(2,1)}, u32[]{:S(2)}, u32[]{:S(2)}) collective-permute-start(bf16[5760,1024]{1,0:T(8,128)(2,1)} %all-gather.5.cloned.1.call-done), channel_id=1, source_target_pairs={{0,16},{16,0},{1,17},{17,1},{2,18},{18,2},{3,19},{19,3},{4,20},{20... | collective-permute-start | bytes 35389448 | tf_op jit(solution)/shard_map/ppermute | solution.py:62
  403.0 26.9 %collective-permute-start.67 = (bf16[64,2048]{1,0:T(8,128)(2,1)S(1)}, bf16[64,2048]{1,0:T(8,128)(2,1)S(1)}, u32[]{:S(2)}, u32[]{:S(2)}) collective-permute-start(bf16[64,2048]{1,0:T(8,128)(2,1)S(1)} %get-tuple-element.424), channel_id=1, source_target_pairs={{0,2},{1,3},{2,0},{3,1},{4,6},{5,7},{6,4},{7,5},{8,10},{9,11},{10,... | collective-permute-start | bytes 786440 | tf_op jit(solution)/shard_map/ppermute | solution.py:58
  415.0 28.5 %collective-permute-start.73 = (bf16[64,256]{1,0:T(8,128)(2,1)S(1)}, bf16[64,256]{1,0:T(8,128)(2,1)S(1)}, u32[]{:S(2)}, u32[]{:S(2)}) collective-permute-start(bf16[64,256]{1,0:T(8,128)(2,1)S(1)} %broadcast_select_fusion.52), channel_id=1, source_target_pairs={{0,16},{16,0},{1,17},{17,1},{2,18},{18,2},{3,19},{19,3},{4,20},{20... | collective-permute-start | bytes 98312 | tf_op jit(solution)/shard_map/ppermute | solution.py:62
  448.7 24.0 %collective-permute-start.75 = (bf16[256,2048]{1,0:T(8,128)(2,1)}, bf16[256,2048]{1,0:T(8,128)(2,1)}, u32[]{:S(2)}, u32[]{:S(2)}) collective-permute-start(bf16[256,2048]{1,0:T(8,128)(2,1)} %get-tuple-element.184), channel_id=1, source_target_pairs={{0,1},{1,0},{2,3},{3,2},{4,5},{5,4},{6,7},{7,6},{8,9},{9,8},{10,11... | collective-permute-start | bytes 3145736 | tf_op jit(solution)/shard_map/ppermute | solution.py:58
  476.6 44.0 %collective-permute-start.91 = (bf16[256,2048]{1,0:T(8,128)(2,1)S(1)}, bf16[256,2048]{1,0:T(8,128)(2,1)}, u32[]{:S(2)}, u32[]{:S(2)}) collective-permute-start(bf16[256,2048]{1,0:T(8,128)(2,1)S(1)} %get-tuple-element.186), channel_id=1, source_target_pairs={{0,1},{1,0},{2,3},{3,2},{4,5},{5,4},{6,7},{7,6},{8,9},{9,8},{10,11... | collective-permute-start | bytes 3145736 | tf_op jit(solution)/shard_map/ppermute | solution.py:58
  485.4 22.6 %collective-permute-start.80 = (bf16[64,1024]{1,0:T(8,128)(2,1)}, bf16[64,1024]{1,0:T(8,128)(2,1)S(1)}, u32[]{:S(2)}, u32[]{:S(2)}) collective-permute-start(bf16[64,1024]{1,0:T(8,128)(2,1)} %collective-permute-done.79), channel_id=1, source_target_pairs={{0,2},{1,3},{2,0},{3,1},{4,6},{5,7},{6,4},{7,5},{8,10},{9,11},{10,... | collective-permute-start | bytes 393224 | tf_op jit(solution)/shard_map/ppermute | solution.py:58
  491.7 23.1 %collective-permute-start.84 = (bf16[64,1024]{1,0:T(8,128)(2,1)S(1)}, bf16[64,1024]{1,0:T(8,128)(2,1)S(1)}, u32[]{:S(2)}, u32[]{:S(2)}) collective-permute-start(bf16[64,1024]{1,0:T(8,128)(2,1)S(1)} %collective-permute-done.83), channel_id=1, source_target_pairs={{0,2},{1,3},{2,0},{3,1},{4,6},{5,7},{6,4},{7,5},{8,10},{9,11},{10,... | collective-permute-start | bytes 393224 | tf_op jit(solution)/shard_map/ppermute | solution.py:58
  547.7 29.9 %collective-permute-start.100 = (bf16[256,2048]{1,0:T(8,128)(2,1)}, bf16[256,2048]{1,0:T(8,128)(2,1)S(1)}, u32[]{:S(2)}, u32[]{:S(2)}) collective-permute-start(bf16[256,2048]{1,0:T(8,128)(2,1)} %collective-permute-done.75), channel_id=1, source_target_pairs={{0,16},{16,0},{1,17},{17,1},{2,18},{18,2},{3,19},{19,3},{4,20},{20... | collective-permute-start | bytes 3145736 | tf_op jit(solution)/shard_map/ppermute | solution.py:62
  550.8 32.1 %collective-permute-start.101 = (bf16[256,2048]{1,0:T(8,128)(2,1)}, bf16[256,2048]{1,0:T(8,128)(2,1)S(1)}, u32[]{:S(2)}, u32[]{:S(2)}) collective-permute-start(bf16[256,2048]{1,0:T(8,128)(2,1)} %collective-permute-done.91), channel_id=1, source_target_pairs={{0,16},{16,0},{1,17},{17,1},{2,18},{18,2},{3,19},{19,3},{4,20},{20... | collective-permute-start | bytes 3145736 | tf_op jit(solution)/shard_map/ppermute | solution.py:62
  550.9 38.3 %collective-permute-start.102 = (bf16[256,2048]{1,0:T(8,128)(2,1)}, bf16[256,2048]{1,0:T(8,128)(2,1)S(1)}, u32[]{:S(2)}, u32[]{:S(2)}) collective-permute-start(bf16[256,2048]{1,0:T(8,128)(2,1)} %collective-permute-done.92), channel_id=1, source_target_pairs={{0,16},{16,0},{1,17},{17,1},{2,18},{18,2},{3,19},{19,3},{4,20},{20... | collective-permute-start | bytes 3145736 | tf_op jit(solution)/shard_map/ppermute | solution.py:62
  594.4 469.4 %all-gather.11.cloned.1.call-start = ((), (), s32[]{:S(2)}) async-start(), calls=%async_computation.6 | async-start | bytes 4456448 | tf_op jit(solution)/shard_map/all_gather | solution.py:660
  646.4 39.5 %collective-permute-start.111 = (bf16[64,2048]{1,0:T(8,128)(2,1)}, bf16[64,2048]{1,0:T(8,128)(2,1)}, u32[]{:S(2)}, u32[]{:S(2)}) collective-permute-start(bf16[64,2048]{1,0:T(8,128)(2,1)} %fusion.290), channel_id=1, source_target_pairs={{0,2},{1,3},{2,0},{3,1},{4,6},{5,7},{6,4},{7,5},{8,10},{9,11},{10,... | collective-permute-start | bytes 786440 | tf_op jit(solution)/shard_map/ppermute | solution.py:58
  646.7 36.9 %collective-permute-start.112 = (bf16[64,2048]{1,0:T(8,128)(2,1)}, bf16[64,2048]{1,0:T(8,128)(2,1)}, u32[]{:S(2)}, u32[]{:S(2)}) collective-permute-start(bf16[64,2048]{1,0:T(8,128)(2,1)} %fusion.290), channel_id=1, source_target_pairs={{0,4},{1,5},{2,6},{3,7},{4,8},{5,9},{6,10},{7,11},{8,12},{9,13},{1... | collective-permute-start | bytes 786440 | tf_op jit(solution)/shard_map/ppermute | solution.py:58
  682.5 381.4 %all-gather.9.cloned.1.call-start = ((), (), s32[]{:S(2)}) async-start(), calls=%async_computation.5 | async-start | bytes 1114112 | tf_op jit(solution)/shard_map/all_gather | solution.py:677
  732.8 45.8 %collective-permute-start.127 = (bf16[256,2048]{1,0:T(8,128)(2,1)}, bf16[256,2048]{1,0:T(8,128)(2,1)S(1)}, u32[]{:S(2)}, u32[]{:S(2)}) collective-permute-start(bf16[256,2048]{1,0:T(8,128)(2,1)} %convolution_convert_fusion.12), channel_id=1, source_target_pairs={{0,16},{16,0},{1,17},{17,1},{2,18},{18,2},{3,19},{19,3},{4,20},{20... | collective-permute-start | bytes 3145736 | tf_op jit(solution)/shard_map/ppermute | solution.py:62
  736.4 44.0 %collective-permute-start.126 = (bf16[256,2048]{1,0:T(8,128)(2,1)S(1)}, bf16[256,2048]{1,0:T(8,128)(2,1)S(1)}, u32[]{:S(2)}, u32[]{:S(2)}) collective-permute-start(bf16[256,2048]{1,0:T(8,128)(2,1)S(1)} %convolution_convert_fusion.14), channel_id=1, source_target_pairs={{0,16},{16,0},{1,17},{17,1},{2,18},{18,2},{3,19},{19,3},{4,20},{20... | collective-permute-start | bytes 3145736 | tf_op jit(solution)/shard_map/ppermute | solution.py:62
  737.6 44.5 %collective-permute-start.125 = (bf16[256,2048]{1,0:T(8,128)(2,1)S(1)}, bf16[256,2048]{1,0:T(8,128)(2,1)S(1)}, u32[]{:S(2)}, u32[]{:S(2)}) collective-permute-start(bf16[256,2048]{1,0:T(8,128)(2,1)S(1)} %convolution_convert_fusion.16), channel_id=1, source_target_pairs={{0,16},{16,0},{1,17},{17,1},{2,18},{18,2},{3,19},{19,3},{4,20},{20... | collective-permute-start | bytes 3145736 | tf_op jit(solution)/shard_map/ppermute | solution.py:62
  740.1 23.5 %collective-permute-start.120 = (bf16[64,2048]{1,0:T(8,128)(2,1)S(1)}, bf16[64,2048]{1,0:T(8,128)(2,1)S(1)}, u32[]{:S(2)}, u32[]{:S(2)}) collective-permute-start(bf16[64,2048]{1,0:T(8,128)(2,1)S(1)} %get-tuple-element.411), channel_id=1, source_target_pairs={{0,2},{1,3},{2,0},{3,1},{4,6},{5,7},{6,4},{7,5},{8,10},{9,11},{10,... | collective-permute-start | bytes 786440 | tf_op jit(solution)/shard_map/ppermute | solution.py:58
  838.5 24.7 %collective-permute-start.144 = (bf16[64,2624]{1,0:T(8,128)(2,1)S(1)}, bf16[64,2624]{1,0:T(8,128)(2,1)S(1)}, u32[]{:S(2)}, u32[]{:S(2)}) collective-permute-start(bf16[64,2624]{1,0:T(8,128)(2,1)S(1)} %concatenate.256), channel_id=1, source_target_pairs={{0,16},{16,0},{1,17},{17,1},{2,18},{18,2},{3,19},{19,3},{4,20},{20... | collective-permute-start | bytes 1007624 | tf_op jit(solution)/shard_map/ppermute | solution.py:62
  858.1 25.3 %collective-permute-start.146 = (bf16[256,2048]{1,0:T(8,128)(2,1)S(1)}, bf16[256,2048]{1,0:T(8,128)(2,1)S(1)}, u32[]{:S(2)}, u32[]{:S(2)}) collective-permute-start(bf16[256,2048]{1,0:T(8,128)(2,1)S(1)} %copy-done.119), channel_id=1, source_target_pairs={{0,1},{1,0},{2,3},{3,2},{4,5},{5,4},{6,7},{7,6},{8,9},{9,8},{10,11... | collective-permute-start | bytes 3145736 | tf_op jit(solution)/shard_map/ppermute | solution.py:58
  858.7 24.6 %collective-permute-start.129 = (bf16[64,1024]{1,0:T(8,128)(2,1)S(1)}, bf16[64,1024]{1,0:T(8,128)(2,1)S(1)}, u32[]{:S(2)}, u32[]{:S(2)}) collective-permute-start(bf16[64,1024]{1,0:T(8,128)(2,1)S(1)} %copy-done.230), channel_id=1, source_target_pairs={{0,2},{1,3},{2,0},{3,1},{4,6},{5,7},{6,4},{7,5},{8,10},{9,11},{10,... | collective-permute-start | bytes 393224 | tf_op jit(solution)/shard_map/ppermute | solution.py:58
  887.5 26.8 %collective-permute-start.148 = (bf16[184,1024]{1,0:T(8,128)(2,1)}, bf16[184,1024]{1,0:T(8,128)(2,1)S(1)}, u32[]{:S(2)}, u32[]{:S(2)}) collective-permute-start(bf16[184,1024]{1,0:T(8,128)(2,1)} %get-tuple-element.366), channel_id=1, source_target_pairs={{0,2},{1,3},{2,0},{3,1},{4,6},{5,7},{6,4},{7,5},{8,10},{9,11},{10,... | collective-permute-start | bytes 1130504 | tf_op jit(solution)/shard_map/ppermute | solution.py:58
  888.1 28.7 %collective-permute-start.147 = (bf16[256,2048]{1,0:T(8,128)(2,1)}, bf16[256,2048]{1,0:T(8,128)(2,1)}, u32[]{:S(2)}, u32[]{:S(2)}) collective-permute-start(bf16[256,2048]{1,0:T(8,128)(2,1)} %fusion.54), channel_id=1, source_target_pairs={{0,1},{1,0},{2,3},{3,2},{4,5},{5,4},{6,7},{7,6},{8,9},{9,8},{10,11... | collective-permute-start | bytes 3145736 | tf_op jit(solution)/shard_map/ppermute | solution.py:58
  891.6 59.2 %collective-permute-start.156 = (bf16[184,1024]{1,0:T(8,128)(2,1)}, bf16[184,1024]{1,0:T(8,128)(2,1)}, u32[]{:S(2)}, u32[]{:S(2)}) collective-permute-start(bf16[184,1024]{1,0:T(8,128)(2,1)} %get-tuple-element.365), channel_id=1, source_target_pairs={{0,2},{1,3},{2,0},{3,1},{4,6},{5,7},{6,4},{7,5},{8,10},{9,11},{10,... | collective-permute-start | bytes 1130504 | tf_op jit(solution)/shard_map/ppermute | solution.py:58
  892.2 58.6 %collective-permute-start.157 = (bf16[184,1024]{1,0:T(8,128)(2,1)}, bf16[184,1024]{1,0:T(8,128)(2,1)}, u32[]{:S(2)}, u32[]{:S(2)}) collective-permute-start(bf16[184,1024]{1,0:T(8,128)(2,1)} %get-tuple-element.364), channel_id=1, source_target_pairs={{0,2},{1,3},{2,0},{3,1},{4,6},{5,7},{6,4},{7,5},{8,10},{9,11},{10,... | collective-permute-start | bytes 1130504 | tf_op jit(solution)/shard_map/ppermute | solution.py:58
  912.7 103.4 %collective-permute-start.169 = (bf16[184,1024]{1,0:T(8,128)(2,1)}, bf16[184,1024]{1,0:T(8,128)(2,1)}, u32[]{:S(2)}, u32[]{:S(2)}) collective-permute-start(bf16[184,1024]{1,0:T(8,128)(2,1)} %get-tuple-element.363), channel_id=1, source_target_pairs={{0,2},{1,3},{2,0},{3,1},{4,6},{5,7},{6,4},{7,5},{8,10},{9,11},{10,... | collective-permute-start | bytes 1130504 | tf_op jit(solution)/shard_map/ppermute | solution.py:58
  975.6 28.3 %collective-permute-start.168 = (bf16[256,2048]{1,0:T(8,128)(2,1)S(1)}, bf16[256,2048]{1,0:T(8,128)(2,1)S(1)}, u32[]{:S(2)}, u32[]{:S(2)}) collective-permute-start(bf16[256,2048]{1,0:T(8,128)(2,1)S(1)} %copy-done.123), channel_id=1, source_target_pairs={{0,16},{16,0},{1,17},{17,1},{2,18},{18,2},{3,19},{19,3},{4,20},{20... | collective-permute-start | bytes 3145736 | tf_op jit(solution)/shard_map/ppermute | solution.py:62
  979.0 32.7 %collective-permute-start.167 = (bf16[256,2048]{1,0:T(8,128)(2,1)S(1)}, bf16[256,2048]{1,0:T(8,128)(2,1)S(1)}, u32[]{:S(2)}, u32[]{:S(2)}) collective-permute-start(bf16[256,2048]{1,0:T(8,128)(2,1)S(1)} %convolution_convert_fusion.8), channel_id=1, source_target_pairs={{0,16},{16,0},{1,17},{17,1},{2,18},{18,2},{3,19},{19,3},{4,20},{20... | collective-permute-start | bytes 3145736 | tf_op jit(solution)/shard_map/ppermute | solution.py:62
  1013.9 49.9 %collective-permute-start.174 = (bf16[184,1024]{1,0:T(8,128)(2,1)}, bf16[184,1024]{1,0:T(8,128)(2,1)}, u32[]{:S(2)}, u32[]{:S(2)}) collective-permute-start(bf16[184,1024]{1,0:T(8,128)(2,1)} %get-tuple-element.361), channel_id=1, source_target_pairs={{0,2},{1,3},{2,0},{3,1},{4,6},{5,7},{6,4},{7,5},{8,10},{9,11},{10,... | collective-permute-start | bytes 1130504 | tf_op jit(solution)/shard_map/ppermute | solution.py:58
  1016.2 47.6 %collective-permute-start.175 = (bf16[184,1024]{1,0:T(8,128)(2,1)}, bf16[184,1024]{1,0:T(8,128)(2,1)}, u32[]{:S(2)}, u32[]{:S(2)}) collective-permute-start(bf16[184,1024]{1,0:T(8,128)(2,1)} %get-tuple-element.360), channel_id=1, source_target_pairs={{0,2},{1,3},{2,0},{3,1},{4,6},{5,7},{6,4},{7,5},{8,10},{9,11},{10,... | collective-permute-start | bytes 1130504 | tf_op jit(solution)/shard_map/ppermute | solution.py:58
  1040.8 23.1 %collective-permute-start.176 = (bf16[184,1024]{1,0:T(8,128)(2,1)}, bf16[184,1024]{1,0:T(8,128)(2,1)}, u32[]{:S(2)}, u32[]{:S(2)}) collective-permute-start(bf16[184,1024]{1,0:T(8,128)(2,1)} %get-tuple-element.368), channel_id=1, source_target_pairs={{0,1},{1,0},{2,3},{3,2},{4,5},{5,4},{6,7},{7,6},{8,9},{9,8},{10,11... | collective-permute-start | bytes 1130504 | tf_op jit(solution)/shard_map/ppermute | solution.py:58
  1041.6 22.3 %collective-permute-start.177 = (bf16[184,1024]{1,0:T(8,128)(2,1)}, bf16[184,1024]{1,0:T(8,128)(2,1)}, u32[]{:S(2)}, u32[]{:S(2)}) collective-permute-start(bf16[184,1024]{1,0:T(8,128)(2,1)} %get-tuple-element.367), channel_id=1, source_target_pairs={{0,12},{1,13},{2,14},{3,15},{4,0},{5,1},{6,2},{7,3},{8,4},{9,5},{1... | collective-permute-start | bytes 1130504 | tf_op jit(solution)/shard_map/ppermute | solution.py:58
  1046.8 22.8 %collective-permute-start.178 = (bf16[256,2048]{1,0:T(8,128)(2,1)}, bf16[256,2048]{1,0:T(8,128)(2,1)}, u32[]{:S(2)}, u32[]{:S(2)}) collective-permute-start(bf16[256,2048]{1,0:T(8,128)(2,1)} %fusion.57), channel_id=1, source_target_pairs={{0,1},{1,0},{2,3},{3,2},{4,5},{5,4},{6,7},{7,6},{8,9},{9,8},{10,11... | collective-permute-start | bytes 3145736 | tf_op jit(solution)/shard_map/ppermute | solution.py:58
  1069.7 41.3 %collective-permute-start.194 = (bf16[64,2624]{1,0:T(8,128)(2,1)S(1)}, bf16[64,2624]{1,0:T(8,128)(2,1)S(1)}, u32[]{:S(2)}, u32[]{:S(2)}) collective-permute-start(bf16[64,2624]{1,0:T(8,128)(2,1)S(1)} %concatenate.267), channel_id=1, source_target_pairs={{0,16},{16,0},{1,17},{17,1},{2,18},{18,2},{3,19},{19,3},{4,20},{20... | collective-permute-start | bytes 1007624 | tf_op jit(solution)/shard_map/ppermute | solution.py:62
  1087.0 24.7 %collective-permute-start.195 = (bf16[4,64,1024]{2,1,0:T(8,128)(2,1)S(1)}, bf16[4,64,1024]{2,1,0:T(8,128)(2,1)S(1)}, u32[]{:S(2)}, u32[]{:S(2)}) collective-permute-start(bf16[4,64,1024]{2,1,0:T(8,128)(2,1)S(1)} %get-tuple-element.429), channel_id=1, source_target_pairs={{0,16},{16,0},{1,17},{17,1},{2,18},{18,2},{3,19},{19,3},{4,20},{20... | collective-permute-start | bytes 1572872 | tf_op jit(solution)/shard_map/ppermute | solution.py:62
  1106.5 41.2 %collective-permute-start.196 = (bf16[184,1024]{1,0:T(8,128)(2,1)S(1)}, bf16[184,1024]{1,0:T(8,128)(2,1)S(1)}, u32[]{:S(2)}, u32[]{:S(2)}) collective-permute-start(bf16[184,1024]{1,0:T(8,128)(2,1)S(1)} %copy-done.176), channel_id=1, source_target_pairs={{0,2},{1,3},{2,0},{3,1},{4,6},{5,7},{6,4},{7,5},{8,10},{9,11},{10,... | collective-permute-start | bytes 1130504 | tf_op jit(solution)/shard_map/ppermute | solution.py:58
  1107.4 40.3 %collective-permute-start.199 = (bf16[256,2048]{1,0:T(8,128)(2,1)S(1)}, bf16[256,2048]{1,0:T(8,128)(2,1)S(1)}, u32[]{:S(2)}, u32[]{:S(2)}) collective-permute-start(bf16[256,2048]{1,0:T(8,128)(2,1)S(1)} %copy-done.118), channel_id=1, source_target_pairs={{0,1},{1,0},{2,3},{3,2},{4,5},{5,4},{6,7},{7,6},{8,9},{9,8},{10,11... | collective-permute-start | bytes 3145736 | tf_op jit(solution)/shard_map/ppermute | solution.py:58
  1110.0 37.7 %collective-permute-start.197 = (bf16[184,1024]{1,0:T(8,128)(2,1)S(1)}, bf16[184,1024]{1,0:T(8,128)(2,1)S(1)}, u32[]{:S(2)}, u32[]{:S(2)}) collective-permute-start(bf16[184,1024]{1,0:T(8,128)(2,1)S(1)} %get-tuple-element.358), channel_id=1, source_target_pairs={{0,1},{1,0},{2,3},{3,2},{4,5},{5,4},{6,7},{7,6},{8,9},{9,8},{10,11... | collective-permute-start | bytes 1130504 | tf_op jit(solution)/shard_map/ppermute | solution.py:58
  1111.0 26.5 %collective-permute-start.179 = (bf16[64,1024]{1,0:T(8,128)(2,1)S(1)}, bf16[64,1024]{1,0:T(8,128)(2,1)S(1)}, u32[]{:S(2)}, u32[]{:S(2)}) collective-permute-start(bf16[64,1024]{1,0:T(8,128)(2,1)S(1)} %get-tuple-element.379), channel_id=1, source_target_pairs={{0,2},{1,3},{2,0},{3,1},{4,6},{5,7},{6,4},{7,5},{8,10},{9,11},{10,... | collective-permute-start | bytes 393224 | tf_op jit(solution)/shard_map/ppermute | solution.py:58
  1111.7 28.3 %collective-permute-start.181 = (bf16[64,1024]{1,0:T(8,128)(2,1)S(1)}, bf16[64,1024]{1,0:T(8,128)(2,1)S(1)}, u32[]{:S(2)}, u32[]{:S(2)}) collective-permute-start(bf16[64,1024]{1,0:T(8,128)(2,1)S(1)} %get-tuple-element.387), channel_id=1, source_target_pairs={{0,1},{1,0},{2,3},{3,2},{4,5},{5,4},{6,7},{7,6},{8,9},{9,8},{10,11... | collective-permute-start | bytes 393224 | tf_op jit(solution)/shard_map/ppermute | solution.py:58
  1154.3 23.3 %collective-permute-start.202 = (bf16[256,2048]{1,0:T(8,128)(2,1)}, bf16[256,2048]{1,0:T(8,128)(2,1)}, u32[]{:S(2)}, u32[]{:S(2)}) collective-permute-start(bf16[256,2048]{1,0:T(8,128)(2,1)} %fusion.63), channel_id=1, source_target_pairs={{0,1},{1,0},{2,3},{3,2},{4,5},{5,4},{6,7},{7,6},{8,9},{9,8},{10,11... | collective-permute-start | bytes 3145736 | tf_op jit(solution)/shard_map/ppermute | solution.py:58
  1189.3 103.8 %all-to-all-start = ((bf16[16,72,720]{2,1,0:T(8,128)(2,1)}), bf16[16,72,720]{2,1,0:T(8,128)(2,1)}, u32[]{:S(2)}, u32[]{:S(2)}) async-start(bf16[16,72,720]{2,1,0:T(8,128)(2,1)} %copy.212), calls=%async_computation.1 | async-start | bytes 3538944 | tf_op jit(solution)/shard_map/all_to_all | solution.py:706
  1196.1 39.8 %collective-permute-start.213 = (bf16[184,1024]{1,0:T(8,128)(2,1)}, bf16[184,1024]{1,0:T(8,128)(2,1)S(1)}, u32[]{:S(2)}, u32[]{:S(2)}) collective-permute-start(bf16[184,1024]{1,0:T(8,128)(2,1)} %get-tuple-element.347), channel_id=1, source_target_pairs={{0,2},{1,3},{2,0},{3,1},{4,6},{5,7},{6,4},{7,5},{8,10},{9,11},{10,... | collective-permute-start | bytes 1130504 | tf_op jit(solution)/shard_map/ppermute | solution.py:58
  1203.4 32.6 %collective-permute-start.215 = (bf16[184,1024]{1,0:T(8,128)(2,1)S(1)}, bf16[184,1024]{1,0:T(8,128)(2,1)S(1)}, u32[]{:S(2)}, u32[]{:S(2)}) collective-permute-start(bf16[184,1024]{1,0:T(8,128)(2,1)S(1)} %get-tuple-element.354), channel_id=1, source_target_pairs={{0,1},{1,0},{2,3},{3,2},{4,5},{5,4},{6,7},{7,6},{8,9},{9,8},{10,11... | collective-permute-start | bytes 1130504 | tf_op jit(solution)/shard_map/ppermute | solution.py:58
  1215.4 101.8 %collective-permute-start.221 = (bf16[3,512,2048]{2,1,0:T(8,128)(2,1)}, bf16[3,512,2048]{2,1,0:T(8,128)(2,1)}, u32[]{:S(2)}, u32[]{:S(2)}) collective-permute-start(bf16[3,512,2048]{2,1,0:T(8,128)(2,1)} %select_convert_fusion), channel_id=1, source_target_pairs={{0,16},{16,0},{1,17},{17,1},{2,18},{18,2},{3,19},{19,3},{4,20},{20... | collective-permute-start | bytes 18874376 | tf_op jit(solution)/shard_map/ppermute | solution.py:62
  1274.1 29.0 %collective-permute-start.200 = (bf16[64,2048]{1,0:T(8,128)(2,1)}, bf16[64,2048]{1,0:T(8,128)(2,1)}, u32[]{:S(2)}, u32[]{:S(2)}) collective-permute-start(bf16[64,2048]{1,0:T(8,128)(2,1)} %get-tuple-element.320), channel_id=1, source_target_pairs={{0,16},{16,0},{1,17},{17,1},{2,18},{18,2},{3,19},{19,3},{4,20},{20... | collective-permute-start | bytes 786440 | tf_op jit(solution)/shard_map/ppermute | solution.py:62
  (538 other events, 6187.6 us)
Sparse Core Ops, SparseCore 0:
  155.0 189.9 all-gather.4
  352.8 61.4 reduce-scatter.1
  594.5 87.8 all-gather.6
  685.4 96.1 all-gather.10
  914.4 55.2 all-gather.8

commit v3 on v2

--- a/solution.py
+++ b/solution.py
@@ -98,10 +98,12 @@
     return found
 
 
-def scatter_steps(terms, n, orders, sums):
+def scatter_steps(terms, n, orders, sums, beside=None):
     totals = dict(terms)
-    for edges in reversed(tree(n, orders)):
+    for number, edges in enumerate(reversed(tree(n, orders))):
         sent = [hop(totals[offset].astype(BF), n, dims, -1) for offset, _, dims in edges]
+        if number == 1 and beside is not None:
+            sent = beside(sent)
         sent, _ = yield sent
         for (_, parent, _), value in zip(edges, sent):
             totals[parent] = totals[parent].astype(F32) + value.astype(F32)
@@ -298,15 +300,10 @@
         (all_ids - me * vocab_dev)[:, None] == jnp.arange(vocab_dev, dtype=jnp.int32)[None, :]
     ).astype(BF)
     looked_up = dot(one_hot, table[0]).astype(BF)
-    looked_up = lax.psum_scatter(looked_up, "shard", scatter_dimension=0, tiled=True)
-    looked_up = looked_up.reshape(2, seq, PLD)
-    side_theirs = swap_cores(pick(looked_up[1], looked_up[0]))
-    side_inputs = [
-        value.astype(F32) for value in by_layer(pick(looked_up[0], looked_up[1]), side_theirs)
-    ]
 
     own_half, other_half = halves(attn_weight[0], core)
     attn_blocks = by_layer(own_half, swap_cores(other_half))
+    rows_1_own = lax.all_gather(attn_blocks[1], "shard", axis=0, tiled=True)
     ff_own = by_layer(ff_weight[0], swap_cores(ff_weight[0]))
     ff_half = [lax.dynamic_slice_in_dim(own, core * half_units, half_units, 1) for own in ff_own]
     buffers = [jnp.zeros((n, rows_dev, HALF), BF), jnp.zeros((n, rows_dev, HALF), BF)]
@@ -324,20 +321,27 @@
 
     fresh = {(0, 0, 0): attn_blocks[0]}
     held = dict(fresh)
-    for edges in tree(n, ALL_CHIPS):
+    for number, edges in enumerate(tree(n, ALL_CHIPS)):
         arriving = {offset: hop(held[parent], n, dims, 1) for offset, parent, dims in edges}
         buffers = store_blocks(buffers, fresh)
+        if number == 1:
+            arriving, looked_up = tie(arriving, looked_up)
+        if number == 2:
+            arriving, ff_own = tie(arriving, ff_own)
+        if number == 3:
+            arriving, ff_half = tie(arriving, ff_half)
         fresh, held, buffers = tie(arriving, held, buffers)
         held.update(fresh)
-    last_block = fresh[max(fresh)]
     buffers = store_blocks(buffers, fresh)
     rows_0 = [buffer.reshape(n * rows_dev, HALF) for buffer in buffers]
-    next_block, last_block, ff_own, ff_half, _ = tie(
-        attn_blocks[1], last_block, ff_own, ff_half, looked_up
-    )
-    rows_1_own = lax.all_gather(next_block, "shard", axis=0, tiled=True)
     rows_1 = [rows_1_own, swap_cores(rows_1_own)]
     attn_rows = (rows_0, rows_1)
+    looked_up = lax.psum_scatter(looked_up, "shard", scatter_dimension=0, tiled=True)
+    looked_up = looked_up.reshape(2, seq, PLD)
+    side_theirs = swap_cores(pick(looked_up[1], looked_up[0]))
+    side_inputs = [
+        value.astype(F32) for value in by_layer(pick(looked_up[0], looked_up[1]), side_theirs)
+    ]
 
     positions = me * seq + jnp.arange(seq, dtype=jnp.int32)
     cosine_part, sine_part = rope_tables(positions)
@@ -381,6 +385,8 @@
         projected_kv = rows_product(normed_b, rows, QW, QW + 2 * KW, core)
         local = key_value_split(projected_kv, key_gain).astype(BF)
         (local,) = background.stage(local)
+        if layer == 0:
+            background.add(near_units(0, local, near))
         found = gather_tree(local, n, ALL_CHIPS)
         projected_q = rows_product(normed_b, rows, 0, QW, core)
         queries_b = query_split(projected_q, query_gain).astype(BF)
@@ -424,6 +430,8 @@
         hidden_ff_b = [gated_gelu(g, u).astype(BF) for g, u in zip(gate, up)]
         down_out = plane_scatter(sum(dot(h, part) for h, part in zip(hidden_ff_b, weights[2])))
         (down_out,) = background.stage(down_out)
+        if layer == 0:
+            background.add(near_units(1, down_out, near_1))
         settled = add_branch(joined, down_out, gain_rows[4])
         settled_b = settled.astype(BF)
         side_gate = rows_product(settled_b, rows, IN_ROWS, OUT_START, core)
@@ -474,7 +482,7 @@
     first = (rows_dev // 2 + 7) // 8 * 8
     upper_rows = n // 2 * rows_dev
 
-    def early_rows(term, result):
+    def early_rows(term, result, beside=None, finish=None):
         shaped = term.reshape(n // 2, rows_dev, HALF)
         upper = me >= n // 2
         pieces = {}
@@ -483,8 +491,10 @@
             place = (target % (n // 2), jnp.where(target >= n // 2, 0, rows_dev - first), 0)
             pieces[offset] = lax.dynamic_slice(shaped, place, (1, first, HALF))[0]
         sums = []
-        yield from scatter_steps(pieces, n, ALL_CHIPS, sums)
+        yield from scatter_steps(pieces, n, ALL_CHIPS, sums, beside)
         mine = sums[0].astype(BF)
+        if finish is not None:
+            mine = finish(mine)
         sent = lax.ppermute(mine, "shard", [(i, i + n // 2) for i in range(n // 2)])
         (sent,), _ = yield [sent]
         whole = jnp.concatenate([mine, sent[2 * first - rows_dev :]], axis=0).astype(F32)
@@ -650,25 +660,19 @@
         return grad_hidden_b, late, ff_base, gain_vec
 
     near_0, near_1 = [], []
-    background.add(near_units(0, last_block, near_0))
     out_0, kept_0 = forward(0, hidden_b, near_0)
-    background.add(near_units(1, out_0, near_1))
     out_1, kept_1 = forward(1, out_0, near_1)
-    normed_all_0 = lax.all_gather(
-        tie(kept_0["normed_b"], rows_1_own)[0], "shard", axis=0, tiled=True
-    )
-    normed_all_1 = lax.all_gather(
-        tie(kept_1["normed_b"], normed_all_0)[0], "shard", axis=0, tiled=True
-    )
+    normed_all_0 = lax.all_gather(kept_0["normed_b"], "shard", axis=0, tiled=True)
     top = pick(cotangent[0], cotangent[1])
     passed_0, passed_1, early_0, early_1, sides = [], [], [], [], []
     due_1 = [sides, normed_all_0, lambda work: work]
     grad_1, late_1, ff_base_1, gain_vec_1 = backward(1, kept_1, top, passed_1, early_1, due_1)
     normed_all_0 = due_1[1]
-
-    def table_grads(work):
-        side_all, normed_all = work
-        return dot_first(one_hot, side_all), normed_all
+    grad_1, normed_b = tie(grad_1, kept_1["normed_b"])
+    normed_all_1 = lax.all_gather(normed_b, "shard", axis=0, tiled=True)
+
+    def table_product(side_all):
+        return dot_first(one_hot, side_all)
 
     def gather_sides():
         keep = pick(sides[1], sides[0])
@@ -676,7 +680,7 @@
         two = jnp.concatenate([pick(keep, other), pick(other, keep)], axis=0)
         return lax.all_gather(two, "shard", axis=0, tiled=True)
 
-    due_0 = [sides, None, table_grads]
+    due_0 = [sides, None, lambda work: (table_product(work[0]), work[1])]
     due_0_start = lambda: (gather_sides(), normed_all_1)
     due_0[1] = due_0_start
     grad_0, late_0, ff_base_0, gain_vec_0 = backward(0, kept_0, grad_1, passed_0, early_0, due_0)
@@ -700,42 +704,57 @@
         ],
         axis=1,
     )
-    (outgoing, ff_base_0, ff_base_1, early_0[0]) = background.stage(
-        outgoing, ff_base_0, ff_base_1, early_0[0]
-    )
     incoming = lax.all_to_all(outgoing, "shard", 0, 0, tiled=True)
-    late_sums = [
-        dot_first(
-            incoming[:, :seq, layer * rows_dev : (layer + 1) * rows_dev].reshape(
-                n * seq, rows_dev
-            ),
-            normed_all,
-        )
-        for layer, normed_all in enumerate((normed_all_0, normed_all_1))
-    ]
-    run(early_rows(early_0.pop(), early_0))
     background.drain()
+
+    def whole_ff(base, passed):
+        passed = jnp.concatenate([part[None] for part in passed], axis=0)
+        zeros = jnp.zeros((3, units - half_units, D), BF)
+        placed = pick(
+            jnp.concatenate([passed, zeros], axis=1), jnp.concatenate([zeros, passed], axis=1)
+        )
+        return base.astype(F32) + placed.astype(F32)
+
+    def finish_ff(base_0, passed_0, base_1, passed_1):
+        whole_0, whole_1 = whole_ff(base_0, passed_0), whole_ff(base_1, passed_1)
+        other = swap_cores(pick(whole_1, whole_0).astype(BF)).astype(F32)
+        return pick(whole_0, whole_1) + other
+
+    def late_rows(arrived):
+        sums = [
+            dot_first(
+                arrived[:, :seq, layer * rows_dev : (layer + 1) * rows_dev].reshape(
+                    n * seq, rows_dev
+                ),
+                normed_all,
+            )
+            for layer, normed_all in enumerate((normed_all_0, normed_all_1))
+        ]
+        return pick(sums[0], sums[1]) + swap_cores(pick(sums[1], sums[0]).astype(BF)).astype(F32)
+
+    ready = []
+
+    def beside(sent):
+        sent, parts = tie(sent, (ff_base_0, passed_0, ff_base_1, passed_1))
+        ready.append(finish_ff(*parts))
+        return sent
+
+    def finish(mine):
+        ready.append(late_rows(incoming))
+        mine, ready[:] = tie(mine, list(ready))
+        return mine
+
+    run(early_rows(early_0.pop(), early_0, beside, finish))
+    ff_grad, late_grad = ready
     early_keep = pick(early_0[0], early_1[0])
     early_other = swap_cores(pick(early_1[0], early_0[0]))
     attn_grad = (
-        pick(late_sums[0], late_sums[1])
-        + swap_cores(pick(late_sums[1], late_sums[0]).astype(BF)).astype(F32)
+        late_grad
         + rejoin(early_keep, early_other, core)
     )
     gain_sums = jnp.sum(incoming[:, seq:].astype(F32), axis=0).reshape(-1)
     gain_sums = (gain_sums[:gains_dev], gain_sums[gains_dev : 2 * gains_dev])
     gain_grad = pick(gain_sums[0], gain_sums[1]) + swap_cores(pick(gain_sums[1], gain_sums[0]))
-
-    def whole_ff(base, passed):
-        passed = jnp.stack(passed)
-        zeros = jnp.zeros((3, units - half_units, D), BF)
-        placed = pick(
-            jnp.concatenate([passed, zeros], axis=1), jnp.concatenate([zeros, passed], axis=1)
-        )
-        return base.astype(F32) + placed.astype(F32)
-
-    whole_0, whole_1 = whole_ff(ff_base_0, passed_0), whole_ff(ff_base_1, passed_1)
-    ff_grad = pick(whole_0, whole_1) + swap_cores(pick(whole_1, whole_0).astype(BF)).astype(F32)
 
     def outputs_of(value_0, value_1):
         keep = pick(value_0, value_1)

time: 1350 us -> 1310 us (0.970)
  waiting for transfers between devices: 535 us -> 495 us
  starting transfers between devices: 248 us -> 264 us
    all_gather x3, waiting for transfers between devices: 34.9 us -> 0.02 us  [the longest x1 0.01 us: per_device(): lax.all_gather(kept_0['normed_b'], 'shard', axis=0, tiled=True)]
    ppermute x44, starting transfers between devices: 86.7 us -> 101 us  [swap_cores(): return lax.ppermute(value, 'section', [(0, 1), (1, 0)])]
    add x0 -> x2, other arithmetic: none -> 13.7 us  [the longest x1 11.4 us: finish_ff(): return pick(whole_0, whole_1) + other]
    unnamed x832 -> x804, local copies, waits for them, and re-layouts: 26.5 us -> 30.3 us
  transfers between devices with their start and end apart: 229 -> 229, of which waited for: 98 -> 95; matrix products, arithmetic and copies ran while one was open for 35% -> 35% of each run, Pallas kernels for 0% -> 0%
where the time goes in v3:
time: 1310 us; the launch traced here: 1300 us
  waiting for transfers between devices  495 us (38%)
  matrix products  266 us (20%)
  starting transfers between devices  264 us (20%)
  local copies, waits for them, and re-layouts  130 us (10%)
  other arithmetic  119 us (9%)
  between operations  21.6 us (2%)
    ppermute x173, waiting for transfers between devices, hop(): return lax.ppermute(value, ('section', 'shard'), pairs)  468 us
    ppermute x173, starting transfers between devices, hop(): return lax.ppermute(value, ('section', 'shard'), pairs)  151 us
    ppermute x44, starting transfers between devices, swap_cores(): return lax.ppermute(value, 'section', [(0, 1), (1, 0)])  101 us
    dot_general x46, matrix products, dot_rows(): lax.dot_general(left_side, right_side, (((1,), (1,)), ((), ())), preferre...  94.1 us
    dot_general x47, matrix products, dot(): return jnp.dot(left_side, right_side, preferred_element_type=F32)  89.4 us
    dot_general x29, matrix products, dot_first(): lax.dot_general(left_side, right_side, (((0,), (0,)), ((), ())), preferre...  56.4 us
    dynamic_update_slice x31, local copies, waits for them, and re-layouts, store_blocks(): lax.dynamic_update_slice(buffer, value[None], (source, jnp.int32(0), jnp....  33.1 us
    unnamed x804, local copies, waits for them, and re-layouts  30.3 us
  transfers between devices with their start and end apart: 229, of which 95 were waited for; matrix products, arithmetic and copies ran while one was open for 35% of the time, Pallas kernels for 0%

profile of v3, /device:TPU:27, one launch (start us, length us, event | category | flops | bytes accessed | tf_op | source)
XLA Modules:
  0.0 1295.4 jit_solution(13611858403531892649)
XLA Ops:
  21.6 4.0 collective-permute-done.4
  25.7 6.0 broadcast.717.clone
  40.7 7.2 fusion.45
  48.7 6.1 broadcast.717
  59.3 5.1 collective-permute-done.8
  68.0 8.8 collective-permute-done.10
  76.8 16.2 %collective-permute-start.14 = (bf16[360,1024]{1,0:T(8,128)(2,1)}, bf16[360,1024]{1,0:T(8,128)(2,1)S(1)}, u32[]{:S(2)}, u32[]{:S(2)}) collective-permute-start(bf16[360,1024]{1,0:T(8,128)(2,1)} %collective-permute-done.6), channel_id=1, source_target_pairs={{0,16},{16,0},{1,17},{17,1},{2,18},{18,2},{3,19},{19,3},{4,20},{20... | collective-permute-start | bytes 2211848 | tf_op jit(solution)/shard_map/ppermute | solution.py:62
  95.0 7.3 collective-permute-done.11
  129.6 24.0 %collective-permute-done.18 = bf16[360,1024]{1,0:T(8,128)(2,1)S(1)} collective-permute-done((bf16[360,1024]{1,0:T(8,128)(2,1)S(1)}, bf16[360,1024]{1,0:T(8,128)(2,1)S(1)}, u32[]{:S(2)}, u32[]{:S(2)}) %collective-permute-start.18) | collective-permute-done | bytes 737312 | tf_op jit(solution)/shard_map/ppermute | solution.py:58
  153.6 6.0 collective-permute-start.27
  160.0 6.9 collective-permute-start.29
  172.2 36.8 %collective-permute-done.26 = bf16[360,1024]{1,0:T(8,128)(2,1)S(1)} collective-permute-done((bf16[360,1024]{1,0:T(8,128)(2,1)S(1)}, bf16[360,1024]{1,0:T(8,128)(2,1)S(1)}, u32[]{:S(2)}, u32[]{:S(2)}) %collective-permute-start.26) | collective-permute-done | bytes 737312 | tf_op jit(solution)/shard_map/ppermute | solution.py:58
  258.1 17.0 %collective-permute-done.40 = bf16[64,1024]{1,0:T(8,128)(2,1)S(1)} collective-permute-done((bf16[64,1024]{1,0:T(8,128)(2,1)}, bf16[64,1024]{1,0:T(8,128)(2,1)S(1)}, u32[]{:S(2)}, u32[]{:S(2)}) %collective-permute-start.40) | collective-permute-done | bytes 131104 | tf_op jit(solution)/shard_map/ppermute | solution.py:58
  282.7 4.3 collective-permute-done.51
  310.4 5.4 collective-permute-done.54
  317.9 4.5 collective-permute-done.56
  342.0 4.8 collective-permute-done.61
  346.9 5.0 collective-permute-done.62
  373.3 8.0 collective-permute-done.69
  423.2 7.0 collective-permute-done.75
  452.9 6.1 collective-permute-done.78
  467.8 4.5 collective-permute-done.89
  472.5 4.4 collective-permute-done.90
  496.7 7.3 collective-permute-start.100
  505.6 5.9 collective-permute-done.96
  514.2 6.0 collective-permute-done.98
  520.3 7.9 collective-permute-done.99
  553.9 4.3 collective-permute-done.107
  560.9 5.2 collective-permute-done.108
  566.5 6.7 collective-permute-done.109
  610.0 6.2 collective-permute-done.117
  616.2 4.2 fusion.41
  637.9 22.0 %collective-permute-start.127 = (bf16[256,2048]{1,0:T(8,128)(2,1)}, bf16[256,2048]{1,0:T(8,128)(2,1)S(1)}, u32[]{:S(2)}, u32[]{:S(2)}) collective-permute-start(bf16[256,2048]{1,0:T(8,128)(2,1)} %convolution_convert_fusion.12), channel_id=1, source_target_pairs={{0,16},{16,0},{1,17},{17,1},{2,18},{18,2},{3,19},{19,3},{4,20},{20... | collective-permute-start | bytes 3145736 | tf_op jit(solution)/shard_map/ppermute | solution.py:62
  665.6 9.2 collective-permute-done.121
  676.2 4.2 collective-permute-done.120
  680.8 4.7 collective-permute-done.122
  709.0 4.4 fusion.76
  742.1 7.4 collective-permute-done.128
  756.4 5.0 collective-permute-start.144
  788.4 13.1 %collective-permute-done.129 = bf16[64,1024]{1,0:T(8,128)(2,1)S(1)} collective-permute-done((bf16[64,1024]{1,0:T(8,128)(2,1)S(1)}, bf16[64,1024]{1,0:T(8,128)(2,1)S(1)}, u32[]{:S(2)}, u32[]{:S(2)}) %collective-permute-start.129) | collective-permute-done | bytes 131104 | tf_op jit(solution)/shard_map/ppermute | solution.py:58
  834.1 21.9 %collective-permute-done.147 = bf16[256,2048]{1,0:T(8,128)(2,1)} collective-permute-done((bf16[256,2048]{1,0:T(8,128)(2,1)}, bf16[256,2048]{1,0:T(8,128)(2,1)}, u32[]{:S(2)}, u32[]{:S(2)}) %collective-permute-start.147) | collective-permute-done | bytes 1048608 | tf_op jit(solution)/shard_map/ppermute | solution.py:58
  861.2 5.8 collective-permute-done.150
  871.4 6.7 collective-permute-done.152
  888.5 11.7 collective-permute-done.155
  931.0 5.6 collective-permute-done.162
  937.8 10.0 collective-permute-done.161
  953.1 7.2 collective-permute-done.160
  961.3 4.8 collective-permute-done.164
  968.0 4.2 collective-permute-done.159
  1028.6 7.2 collective-permute-start.194
  1052.0 11.3 fusion.2
  1074.6 24.9 %collective-permute-done.179 = bf16[64,1024]{1,0:T(8,128)(2,1)S(1)} collective-permute-done((bf16[64,1024]{1,0:T(8,128)(2,1)S(1)}, bf16[64,1024]{1,0:T(8,128)(2,1)S(1)}, u32[]{:S(2)}, u32[]{:S(2)}) %collective-permute-start.179) | collective-permute-done | bytes 131104 | tf_op jit(solution)/shard_map/ppermute | solution.py:58
  1103.0 6.2 collective-permute-done.193
  1126.4 22.3 %collective-permute-done.210 = bf16[184,1024]{1,0:T(8,128)(2,1)S(1)} collective-permute-done((bf16[184,1024]{1,0:T(8,128)(2,1)S(1)}, bf16[184,1024]{1,0:T(8,128)(2,1)S(1)}, u32[]{:S(2)}, u32[]{:S(2)}) %collective-permute-start.210) | collective-permute-done | bytes 376864 | tf_op jit(solution)/shard_map/ppermute | solution.py:58
  1159.5 6.3 all-to-all-start
  1173.1 10.3 select_convert_fusion
  1186.4 6.3 collective-permute-done.202
  1192.7 4.0 collective-permute-done.205
  1209.1 3.9 collective-permute-done.214
  1217.0 4.1 fusion.593
  1231.0 4.3 collective-permute-done.201
  1237.4 4.0 collective-permute-done.216
  1247.2 11.4 convert_add_fusion
  1262.5 15.9 %collective-permute-done.219 = bf16[184,1024]{1,0:T(8,128)(2,1)S(1)} collective-permute-done((bf16[184,1024]{1,0:T(8,128)(2,1)S(1)}, bf16[184,1024]{1,0:T(8,128)(2,1)S(1)}, u32[]{:S(2)}, u32[]{:S(2)}) %collective-permute-start.219) | collective-permute-done | bytes 376864 | tf_op jit(solution)/shard_map/ppermute | solution.py:498
  (1701 shorter events, 724.5 us)
Async XLA Ops:
  7.2 327.8 %all-gather.5.cloned.1.call-start = ((), (), s32[]{:S(2)}) async-start(), calls=%async_computation.3 | async-start | bytes 12533760 | tf_op jit(solution)/shard_map/all_gather | solution.py:306
  10.5 114.1 %collective-permute-start.21 = (bf16[3,512,2048]{2,1,0:T(8,128)(2,1)}, bf16[3,512,2048]{2,1,0:T(8,128)(2,1)}, u32[]{:S(2)}, u32[]{:S(2)}) collective-permute-start(bf16[3,512,2048]{2,1,0:T(8,128)(2,1)} %bitcast.635), channel_id=1, source_target_pairs={{0,16},{16,0},{1,17},{17,1},{2,18},{18,2},{3,19},{19,3},{4,20},{20... | collective-permute-start | bytes 18874376 | tf_op jit(solution)/shard_map/ppermute | solution.py:62
  39.6 24.9 %collective-permute-start.8 = (bf16[360,1024]{1,0:T(8,128)(2,1)}, bf16[360,1024]{1,0:T(8,128)(2,1)}, u32[]{:S(2)}, u32[]{:S(2)}) collective-permute-start(bf16[360,1024]{1,0:T(8,128)(2,1)} %get-tuple-element.381), channel_id=1, source_target_pairs={{0,4},{1,5},{2,6},{3,7},{4,8},{5,9},{6,10},{7,11},{8,12},{9,13},{1... | collective-permute-start | bytes 2211848 | tf_op jit(solution)/shard_map/ppermute | solution.py:58
  40.6 352.0 %reduce-scatter.2.cloned.1.call-start = ((), (), s32[]{:S(2)}) async-start(), calls=%async_computation.2 | async-start | bytes 1114112 | tf_op jit(solution)/shard_map/reduce_scatter | solution.py:339
  67.4 34.9 %collective-permute-start.11 = (bf16[360,1024]{1,0:T(8,128)(2,1)}, bf16[360,1024]{1,0:T(8,128)(2,1)S(1)}, u32[]{:S(2)}, u32[]{:S(2)}) collective-permute-start(bf16[360,1024]{1,0:T(8,128)(2,1)} %collective-permute-done.8), channel_id=1, source_target_pairs={{0,2},{1,3},{2,0},{3,1},{4,6},{5,7},{6,4},{7,5},{8,10},{9,11},{10,... | collective-permute-start | bytes 2211848 | tf_op jit(solution)/shard_map/ppermute | solution.py:58
  67.6 39.6 %collective-permute-start.12 = (bf16[360,1024]{1,0:T(8,128)(2,1)}, bf16[360,1024]{1,0:T(8,128)(2,1)S(1)}, u32[]{:S(2)}, u32[]{:S(2)}) collective-permute-start(bf16[360,1024]{1,0:T(8,128)(2,1)} %collective-permute-done.8), channel_id=1, source_target_pairs={{0,1},{1,0},{2,3},{3,2},{4,5},{5,4},{6,7},{7,6},{8,9},{9,8},{10,11... | collective-permute-start | bytes 2211848 | tf_op jit(solution)/shard_map/ppermute | solution.py:58
  67.7 41.6 %collective-permute-start.13 = (bf16[360,1024]{1,0:T(8,128)(2,1)}, bf16[360,1024]{1,0:T(8,128)(2,1)S(1)}, u32[]{:S(2)}, u32[]{:S(2)}) collective-permute-start(bf16[360,1024]{1,0:T(8,128)(2,1)} %collective-permute-done.8), channel_id=1, source_target_pairs={{0,4},{1,5},{2,6},{3,7},{4,8},{5,9},{6,10},{7,11},{8,12},{9,13},{1... | collective-permute-start | bytes 2211848 | tf_op jit(solution)/shard_map/ppermute | solution.py:58
  76.8 32.5 %collective-permute-start.14 = (bf16[360,1024]{1,0:T(8,128)(2,1)}, bf16[360,1024]{1,0:T(8,128)(2,1)S(1)}, u32[]{:S(2)}, u32[]{:S(2)}) collective-permute-start(bf16[360,1024]{1,0:T(8,128)(2,1)} %collective-permute-done.6), channel_id=1, source_target_pairs={{0,16},{16,0},{1,17},{17,1},{2,18},{18,2},{3,19},{19,3},{4,20},{20... | collective-permute-start | bytes 2211848 | tf_op jit(solution)/shard_map/ppermute | solution.py:62
  119.1 34.5 %collective-permute-start.18 = (bf16[360,1024]{1,0:T(8,128)(2,1)S(1)}, bf16[360,1024]{1,0:T(8,128)(2,1)S(1)}, u32[]{:S(2)}, u32[]{:S(2)}) collective-permute-start(bf16[360,1024]{1,0:T(8,128)(2,1)S(1)} %collective-permute-done.13), channel_id=1, source_target_pairs={{0,2},{1,3},{2,0},{3,1},{4,6},{5,7},{6,4},{7,5},{8,10},{9,11},{10,... | collective-permute-start | bytes 2211848 | tf_op jit(solution)/shard_map/ppermute | solution.py:58
  120.2 33.5 %collective-permute-start.19 = (bf16[360,1024]{1,0:T(8,128)(2,1)S(1)}, bf16[360,1024]{1,0:T(8,128)(2,1)S(1)}, u32[]{:S(2)}, u32[]{:S(2)}) collective-permute-start(bf16[360,1024]{1,0:T(8,128)(2,1)S(1)} %collective-permute-done.13), channel_id=1, source_target_pairs={{0,1},{1,0},{2,3},{3,2},{4,5},{5,4},{6,7},{7,6},{8,9},{9,8},{10,11... | collective-permute-start | bytes 2211848 | tf_op jit(solution)/shard_map/ppermute | solution.py:58
  123.7 30.0 %collective-permute-start.20 = (bf16[360,1024]{1,0:T(8,128)(2,1)S(1)}, bf16[360,1024]{1,0:T(8,128)(2,1)S(1)}, u32[]{:S(2)}, u32[]{:S(2)}) collective-permute-start(bf16[360,1024]{1,0:T(8,128)(2,1)S(1)} %collective-permute-done.13), channel_id=1, source_target_pairs={{0,4},{1,5},{2,6},{3,7},{4,8},{5,9},{6,10},{7,11},{8,12},{9,13},{1... | collective-permute-start | bytes 2211848 | tf_op jit(solution)/shard_map/ppermute | solution.py:58
  153.6 58.4 %collective-permute-start.27 = (bf16[360,1024]{1,0:T(8,128)(2,1)S(1)}, bf16[360,1024]{1,0:T(8,128)(2,1)S(1)}, u32[]{:S(2)}, u32[]{:S(2)}) collective-permute-start(bf16[360,1024]{1,0:T(8,128)(2,1)S(1)} %collective-permute-done.20), channel_id=1, source_target_pairs={{0,2},{1,3},{2,0},{3,1},{4,6},{5,7},{6,4},{7,5},{8,10},{9,11},{10,... | collective-permute-start | bytes 2211848 | tf_op jit(solution)/shard_map/ppermute | solution.py:58
  159.6 52.4 %collective-permute-start.28 = (bf16[360,1024]{1,0:T(8,128)(2,1)S(1)}, bf16[360,1024]{1,0:T(8,128)(2,1)S(1)}, u32[]{:S(2)}, u32[]{:S(2)}) collective-permute-start(bf16[360,1024]{1,0:T(8,128)(2,1)S(1)} %collective-permute-done.20), channel_id=1, source_target_pairs={{0,1},{1,0},{2,3},{3,2},{4,5},{5,4},{6,7},{7,6},{8,9},{9,8},{10,11... | collective-permute-start | bytes 2211848 | tf_op jit(solution)/shard_map/ppermute | solution.py:58
  160.0 52.0 %collective-permute-start.29 = (bf16[360,1024]{1,0:T(8,128)(2,1)S(1)}, bf16[360,1024]{1,0:T(8,128)(2,1)S(1)}, u32[]{:S(2)}, u32[]{:S(2)}) collective-permute-start(bf16[360,1024]{1,0:T(8,128)(2,1)S(1)} %collective-permute-done.17), channel_id=1, source_target_pairs={{0,16},{16,0},{1,17},{17,1},{2,18},{18,2},{3,19},{19,3},{4,20},{20... | collective-permute-start | bytes 2211848 | tf_op jit(solution)/shard_map/ppermute | solution.py:62
  167.0 46.1 %collective-permute-start.30 = (bf16[360,1024]{1,0:T(8,128)(2,1)S(1)}, bf16[360,1024]{1,0:T(8,128)(2,1)S(1)}, u32[]{:S(2)}, u32[]{:S(2)}) collective-permute-start(bf16[360,1024]{1,0:T(8,128)(2,1)S(1)} %collective-permute-done.18), channel_id=1, source_target_pairs={{0,16},{16,0},{1,17},{17,1},{2,18},{18,2},{3,19},{19,3},{4,20},{20... | collective-permute-start | bytes 2211848 | tf_op jit(solution)/shard_map/ppermute | solution.py:62
  167.0 42.1 %collective-permute-start.26 = (bf16[360,1024]{1,0:T(8,128)(2,1)S(1)}, bf16[360,1024]{1,0:T(8,128)(2,1)S(1)}, u32[]{:S(2)}, u32[]{:S(2)}) collective-permute-start(bf16[360,1024]{1,0:T(8,128)(2,1)S(1)} %collective-permute-done.19), channel_id=1, source_target_pairs={{0,2},{1,3},{2,0},{3,1},{4,6},{5,7},{6,4},{7,5},{8,10},{9,11},{10,... | collective-permute-start | bytes 2211848 | tf_op jit(solution)/shard_map/ppermute | solution.py:58
  244.3 46.8 %collective-permute-start.53 = (bf16[256,2048]{1,0:T(8,128)(2,1)}, bf16[256,2048]{1,0:T(8,128)(2,1)}, u32[]{:S(2)}, u32[]{:S(2)}) collective-permute-start(bf16[256,2048]{1,0:T(8,128)(2,1)} %get-tuple-element.202), channel_id=1, source_target_pairs={{0,1},{1,0},{2,3},{3,2},{4,5},{5,4},{6,7},{7,6},{8,9},{9,8},{10,11... | collective-permute-start | bytes 3145736 | tf_op jit(solution)/shard_map/ppermute | solution.py:58
  252.2 23.8 %collective-permute-start.42 = (bf16[64,1024]{1,0:T(8,128)(2,1)S(1)}, bf16[64,1024]{1,0:T(8,128)(2,1)S(1)}, u32[]{:S(2)}, u32[]{:S(2)}) collective-permute-start(bf16[64,1024]{1,0:T(8,128)(2,1)S(1)} %collective-permute-done.41), channel_id=1, source_target_pairs={{0,2},{1,3},{2,0},{3,1},{4,6},{5,7},{6,4},{7,5},{8,10},{9,11},{10,... | collective-permute-start | bytes 393224 | tf_op jit(solution)/shard_map/ppermute | solution.py:58
  253.7 22.8 %collective-permute-start.43 = (bf16[64,1024]{1,0:T(8,128)(2,1)S(1)}, bf16[64,1024]{1,0:T(8,128)(2,1)S(1)}, u32[]{:S(2)}, u32[]{:S(2)}) collective-permute-start(bf16[64,1024]{1,0:T(8,128)(2,1)S(1)} %collective-permute-done.41), channel_id=1, source_target_pairs={{0,1},{1,0},{2,3},{3,2},{4,5},{5,4},{6,7},{7,6},{8,9},{9,8},{10,11... | collective-permute-start | bytes 393224 | tf_op jit(solution)/shard_map/ppermute | solution.py:58
  257.9 24.8 %collective-permute-start.46 = (bf16[64,1024]{1,0:T(8,128)(2,1)S(1)}, bf16[64,1024]{1,0:T(8,128)(2,1)S(1)}, u32[]{:S(2)}, u32[]{:S(2)}) collective-permute-start(bf16[64,1024]{1,0:T(8,128)(2,1)S(1)} %collective-permute-done.45), channel_id=1, source_target_pairs={{0,2},{1,3},{2,0},{3,1},{4,6},{5,7},{6,4},{7,5},{8,10},{9,11},{10,... | collective-permute-start | bytes 393224 | tf_op jit(solution)/shard_map/ppermute | solution.py:58
  291.1 24.7 %collective-permute-start.54 = (bf16[256,2048]{1,0:T(8,128)(2,1)}, bf16[256,2048]{1,0:T(8,128)(2,1)}, u32[]{:S(2)}, u32[]{:S(2)}) collective-permute-start(bf16[256,2048]{1,0:T(8,128)(2,1)} %get-tuple-element.206), channel_id=1, source_target_pairs={{0,1},{1,0},{2,3},{3,2},{4,5},{5,4},{6,7},{7,6},{8,9},{9,8},{10,11... | collective-permute-start | bytes 3145736 | tf_op jit(solution)/shard_map/ppermute | solution.py:58
  316.2 425.9 %all-gather.7.cloned.1.call-start = ((), (), s32[]{:S(2)}) async-start(), calls=%async_computation.4 | async-start | bytes 4456448 | tf_op jit(solution)/shard_map/all_gather | solution.py:665
  316.3 42.1 %collective-permute-start.63 = (bf16[256,2048]{1,0:T(8,128)(2,1)}, bf16[256,2048]{1,0:T(8,128)(2,1)}, u32[]{:S(2)}, u32[]{:S(2)}) collective-permute-start(bf16[256,2048]{1,0:T(8,128)(2,1)} %collective-permute-done.53), channel_id=1, source_target_pairs={{0,16},{16,0},{1,17},{17,1},{2,18},{18,2},{3,19},{19,3},{4,20},{20... | collective-permute-start | bytes 3145736 | tf_op jit(solution)/shard_map/ppermute | solution.py:62
  317.5 34.3 %collective-permute-start.62 = (bf16[256,2048]{1,0:T(8,128)(2,1)}, bf16[256,2048]{1,0:T(8,128)(2,1)}, u32[]{:S(2)}, u32[]{:S(2)}) collective-permute-start(bf16[256,2048]{1,0:T(8,128)(2,1)} %get-tuple-element.208), channel_id=1, source_target_pairs={{0,1},{1,0},{2,3},{3,2},{4,5},{5,4},{6,7},{7,6},{8,9},{9,8},{10,11... | collective-permute-start | bytes 3145736 | tf_op jit(solution)/shard_map/ppermute | solution.py:58
  335.0 81.2 %collective-permute-start.74 = (bf16[5760,1024]{1,0:T(8,128)(2,1)}, bf16[5760,1024]{1,0:T(8,128)(2,1)}, u32[]{:S(2)}, u32[]{:S(2)}) collective-permute-start(bf16[5760,1024]{1,0:T(8,128)(2,1)} %all-gather.5.cloned.1.call-done), channel_id=1, source_target_pairs={{0,16},{16,0},{1,17},{17,1},{2,18},{18,2},{3,19},{19,3},{4,20},{20... | collective-permute-start | bytes 35389448 | tf_op jit(solution)/shard_map/ppermute | solution.py:62
  339.0 25.0 %collective-permute-start.64 = (bf16[256,2048]{1,0:T(8,128)(2,1)}, bf16[256,2048]{1,0:T(8,128)(2,1)S(1)}, u32[]{:S(2)}, u32[]{:S(2)}) collective-permute-start(bf16[256,2048]{1,0:T(8,128)(2,1)} %collective-permute-done.54), channel_id=1, source_target_pairs={{0,16},{16,0},{1,17},{17,1},{2,18},{18,2},{3,19},{19,3},{4,20},{20... | collective-permute-start | bytes 3145736 | tf_op jit(solution)/shard_map/ppermute | solution.py:62
  431.3 45.6 %collective-permute-start.91 = (bf16[256,2048]{1,0:T(8,128)(2,1)S(1)}, bf16[256,2048]{1,0:T(8,128)(2,1)}, u32[]{:S(2)}, u32[]{:S(2)}) collective-permute-start(bf16[256,2048]{1,0:T(8,128)(2,1)S(1)} %get-tuple-element.218), channel_id=1, source_target_pairs={{0,1},{1,0},{2,3},{3,2},{4,5},{5,4},{6,7},{7,6},{8,9},{9,8},{10,11... | collective-permute-start | bytes 3145736 | tf_op jit(solution)/shard_map/ppermute | solution.py:58
  496.7 36.5 %collective-permute-start.100 = (bf16[256,2048]{1,0:T(8,128)(2,1)}, bf16[256,2048]{1,0:T(8,128)(2,1)S(1)}, u32[]{:S(2)}, u32[]{:S(2)}) collective-permute-start(bf16[256,2048]{1,0:T(8,128)(2,1)} %collective-permute-done.75), channel_id=1, source_target_pairs={{0,16},{16,0},{1,17},{17,1},{2,18},{18,2},{3,19},{19,3},{4,20},{20... | collective-permute-start | bytes 3145736 | tf_op jit(solution)/shard_map/ppermute | solution.py:62
  504.0 34.4 %collective-permute-start.101 = (bf16[256,2048]{1,0:T(8,128)(2,1)}, bf16[256,2048]{1,0:T(8,128)(2,1)S(1)}, u32[]{:S(2)}, u32[]{:S(2)}) collective-permute-start(bf16[256,2048]{1,0:T(8,128)(2,1)} %collective-permute-done.91), channel_id=1, source_target_pairs={{0,16},{16,0},{1,17},{17,1},{2,18},{18,2},{3,19},{19,3},{4,20},{20... | collective-permute-start | bytes 3145736 | tf_op jit(solution)/shard_map/ppermute | solution.py:62
  504.1 40.6 %collective-permute-start.102 = (bf16[256,2048]{1,0:T(8,128)(2,1)}, bf16[256,2048]{1,0:T(8,128)(2,1)S(1)}, u32[]{:S(2)}, u32[]{:S(2)}) collective-permute-start(bf16[256,2048]{1,0:T(8,128)(2,1)} %collective-permute-done.92), channel_id=1, source_target_pairs={{0,16},{16,0},{1,17},{17,1},{2,18},{18,2},{3,19},{19,3},{4,20},{20... | collective-permute-start | bytes 3145736 | tf_op jit(solution)/shard_map/ppermute | solution.py:62
  589.0 438.6 %all-gather.9.cloned.1.call-start = ((), (), s32[]{:S(2)}) async-start(), calls=%async_computation.5 | async-start | bytes 1114112 | tf_op jit(solution)/shard_map/all_gather | solution.py:681
  637.9 57.5 %collective-permute-start.127 = (bf16[256,2048]{1,0:T(8,128)(2,1)}, bf16[256,2048]{1,0:T(8,128)(2,1)S(1)}, u32[]{:S(2)}, u32[]{:S(2)}) collective-permute-start(bf16[256,2048]{1,0:T(8,128)(2,1)} %convolution_convert_fusion.12), channel_id=1, source_target_pairs={{0,16},{16,0},{1,17},{17,1},{2,18},{18,2},{3,19},{19,3},{4,20},{20... | collective-permute-start | bytes 3145736 | tf_op jit(solution)/shard_map/ppermute | solution.py:62
  660.6 36.6 %collective-permute-start.126 = (bf16[256,2048]{1,0:T(8,128)(2,1)S(1)}, bf16[256,2048]{1,0:T(8,128)(2,1)S(1)}, u32[]{:S(2)}, u32[]{:S(2)}) collective-permute-start(bf16[256,2048]{1,0:T(8,128)(2,1)S(1)} %convolution_convert_fusion.14), channel_id=1, source_target_pairs={{0,16},{16,0},{1,17},{17,1},{2,18},{18,2},{3,19},{19,3},{4,20},{20... | collective-permute-start | bytes 3145736 | tf_op jit(solution)/shard_map/ppermute | solution.py:62
  661.8 37.1 %collective-permute-start.125 = (bf16[256,2048]{1,0:T(8,128)(2,1)S(1)}, bf16[256,2048]{1,0:T(8,128)(2,1)S(1)}, u32[]{:S(2)}, u32[]{:S(2)}) collective-permute-start(bf16[256,2048]{1,0:T(8,128)(2,1)S(1)} %convolution_convert_fusion.16), channel_id=1, source_target_pairs={{0,16},{16,0},{1,17},{17,1},{2,18},{18,2},{3,19},{19,3},{4,20},{20... | collective-permute-start | bytes 3145736 | tf_op jit(solution)/shard_map/ppermute | solution.py:62
  727.4 22.1 %collective-permute-start.128 = (bf16[256,2048]{1,0:T(8,128)(2,1)}, bf16[256,2048]{1,0:T(8,128)(2,1)}, u32[]{:S(2)}, u32[]{:S(2)}) collective-permute-start(bf16[256,2048]{1,0:T(8,128)(2,1)} %fusion.48), channel_id=1, source_target_pairs={{0,1},{1,0},{2,3},{3,2},{4,5},{5,4},{6,7},{7,6},{8,9},{9,8},{10,11... | collective-permute-start | bytes 3145736 | tf_op jit(solution)/shard_map/ppermute | solution.py:58
  756.4 25.5 %collective-permute-start.144 = (bf16[64,2624]{1,0:T(8,128)(2,1)S(1)}, bf16[64,2624]{1,0:T(8,128)(2,1)S(1)}, u32[]{:S(2)}, u32[]{:S(2)}) collective-permute-start(bf16[64,2624]{1,0:T(8,128)(2,1)S(1)} %concatenate.262), channel_id=1, source_target_pairs={{0,16},{16,0},{1,17},{17,1},{2,18},{18,2},{3,19},{19,3},{4,20},{20... | collective-permute-start | bytes 1007624 | tf_op jit(solution)/shard_map/ppermute | solution.py:62
  776.1 25.5 %collective-permute-start.146 = (bf16[256,2048]{1,0:T(8,128)(2,1)S(1)}, bf16[256,2048]{1,0:T(8,128)(2,1)S(1)}, u32[]{:S(2)}, u32[]{:S(2)}) collective-permute-start(bf16[256,2048]{1,0:T(8,128)(2,1)S(1)} %copy-done.113), channel_id=1, source_target_pairs={{0,1},{1,0},{2,3},{3,2},{4,5},{5,4},{6,7},{7,6},{8,9},{9,8},{10,11... | collective-permute-start | bytes 3145736 | tf_op jit(solution)/shard_map/ppermute | solution.py:58
  777.2 24.3 %collective-permute-start.129 = (bf16[64,1024]{1,0:T(8,128)(2,1)S(1)}, bf16[64,1024]{1,0:T(8,128)(2,1)S(1)}, u32[]{:S(2)}, u32[]{:S(2)}) collective-permute-start(bf16[64,1024]{1,0:T(8,128)(2,1)S(1)} %copy-done.218), channel_id=1, source_target_pairs={{0,2},{1,3},{2,0},{3,1},{4,6},{5,7},{6,4},{7,5},{8,10},{9,11},{10,... | collective-permute-start | bytes 393224 | tf_op jit(solution)/shard_map/ppermute | solution.py:58
  819.0 209.5 %all-gather.11.cloned.1.call-start = ((), (), s32[]{:S(2)}) async-start(), calls=%async_computation.6 | async-start | bytes 4456448 | tf_op jit(solution)/shard_map/all_gather | solution.py:672
  824.4 31.6 %collective-permute-start.147 = (bf16[256,2048]{1,0:T(8,128)(2,1)}, bf16[256,2048]{1,0:T(8,128)(2,1)}, u32[]{:S(2)}, u32[]{:S(2)}) collective-permute-start(bf16[256,2048]{1,0:T(8,128)(2,1)} %fusion.54), channel_id=1, source_target_pairs={{0,1},{1,0},{2,3},{3,2},{4,5},{5,4},{6,7},{7,6},{8,9},{9,8},{10,11... | collective-permute-start | bytes 3145736 | tf_op jit(solution)/shard_map/ppermute | solution.py:58
  825.6 74.7 %collective-permute-start.156 = (bf16[184,1024]{1,0:T(8,128)(2,1)}, bf16[184,1024]{1,0:T(8,128)(2,1)}, u32[]{:S(2)}, u32[]{:S(2)}) collective-permute-start(bf16[184,1024]{1,0:T(8,128)(2,1)} %get-tuple-element.404), channel_id=1, source_target_pairs={{0,2},{1,3},{2,0},{3,1},{4,6},{5,7},{6,4},{7,5},{8,10},{9,11},{10,... | collective-permute-start | bytes 1130504 | tf_op jit(solution)/shard_map/ppermute | solution.py:58
  825.9 74.4 %collective-permute-start.157 = (bf16[184,1024]{1,0:T(8,128)(2,1)}, bf16[184,1024]{1,0:T(8,128)(2,1)}, u32[]{:S(2)}, u32[]{:S(2)}) collective-permute-start(bf16[184,1024]{1,0:T(8,128)(2,1)} %get-tuple-element.403), channel_id=1, source_target_pairs={{0,2},{1,3},{2,0},{3,1},{4,6},{5,7},{6,4},{7,5},{8,10},{9,11},{10,... | collective-permute-start | bytes 1130504 | tf_op jit(solution)/shard_map/ppermute | solution.py:58
  827.0 151.6 %collective-permute-start.169 = (bf16[184,1024]{1,0:T(8,128)(2,1)}, bf16[184,1024]{1,0:T(8,128)(2,1)}, u32[]{:S(2)}, u32[]{:S(2)}) collective-permute-start(bf16[184,1024]{1,0:T(8,128)(2,1)} %get-tuple-element.402), channel_id=1, source_target_pairs={{0,2},{1,3},{2,0},{3,1},{4,6},{5,7},{6,4},{7,5},{8,10},{9,11},{10,... | collective-permute-start | bytes 1130504 | tf_op jit(solution)/shard_map/ppermute | solution.py:58
  924.6 41.6 %collective-permute-start.168 = (bf16[256,2048]{1,0:T(8,128)(2,1)S(1)}, bf16[256,2048]{1,0:T(8,128)(2,1)S(1)}, u32[]{:S(2)}, u32[]{:S(2)}) collective-permute-start(bf16[256,2048]{1,0:T(8,128)(2,1)S(1)} %copy-done.121), channel_id=1, source_target_pairs={{0,16},{16,0},{1,17},{17,1},{2,18},{18,2},{3,19},{19,3},{4,20},{20... | collective-permute-start | bytes 3145736 | tf_op jit(solution)/shard_map/ppermute | solution.py:62
  925.4 49.4 %collective-permute-start.167 = (bf16[256,2048]{1,0:T(8,128)(2,1)S(1)}, bf16[256,2048]{1,0:T(8,128)(2,1)S(1)}, u32[]{:S(2)}, u32[]{:S(2)}) collective-permute-start(bf16[256,2048]{1,0:T(8,128)(2,1)S(1)} %convolution_convert_fusion.8), channel_id=1, source_target_pairs={{0,16},{16,0},{1,17},{17,1},{2,18},{18,2},{3,19},{19,3},{4,20},{20... | collective-permute-start | bytes 3145736 | tf_op jit(solution)/shard_map/ppermute | solution.py:62
  976.8 50.8 %collective-permute-start.174 = (bf16[184,1024]{1,0:T(8,128)(2,1)}, bf16[184,1024]{1,0:T(8,128)(2,1)}, u32[]{:S(2)}, u32[]{:S(2)}) collective-permute-start(bf16[184,1024]{1,0:T(8,128)(2,1)} %get-tuple-element.400), channel_id=1, source_target_pairs={{0,2},{1,3},{2,0},{3,1},{4,6},{5,7},{6,4},{7,5},{8,10},{9,11},{10,... | collective-permute-start | bytes 1130504 | tf_op jit(solution)/shard_map/ppermute | solution.py:58
  978.6 49.0 %collective-permute-start.175 = (bf16[184,1024]{1,0:T(8,128)(2,1)}, bf16[184,1024]{1,0:T(8,128)(2,1)}, u32[]{:S(2)}, u32[]{:S(2)}) collective-permute-start(bf16[184,1024]{1,0:T(8,128)(2,1)} %get-tuple-element.399), channel_id=1, source_target_pairs={{0,2},{1,3},{2,0},{3,1},{4,6},{5,7},{6,4},{7,5},{8,10},{9,11},{10,... | collective-permute-start | bytes 1130504 | tf_op jit(solution)/shard_map/ppermute | solution.py:58
  985.9 41.7 %collective-permute-start.176 = (bf16[184,1024]{1,0:T(8,128)(2,1)}, bf16[184,1024]{1,0:T(8,128)(2,1)}, u32[]{:S(2)}, u32[]{:S(2)}) collective-permute-start(bf16[184,1024]{1,0:T(8,128)(2,1)} %get-tuple-element.407), channel_id=1, source_target_pairs={{0,1},{1,0},{2,3},{3,2},{4,5},{5,4},{6,7},{7,6},{8,9},{9,8},{10,11... | collective-permute-start | bytes 1130504 | tf_op jit(solution)/shard_map/ppermute | solution.py:58
  987.6 40.1 %collective-permute-start.177 = (bf16[184,1024]{1,0:T(8,128)(2,1)}, bf16[184,1024]{1,0:T(8,128)(2,1)}, u32[]{:S(2)}, u32[]{:S(2)}) collective-permute-start(bf16[184,1024]{1,0:T(8,128)(2,1)} %get-tuple-element.406), channel_id=1, source_target_pairs={{0,12},{1,13},{2,14},{3,15},{4,0},{5,1},{6,2},{7,3},{8,4},{9,5},{1... | collective-permute-start | bytes 1130504 | tf_op jit(solution)/shard_map/ppermute | solution.py:58
  1028.6 43.7 %collective-permute-start.194 = (bf16[64,2624]{1,0:T(8,128)(2,1)S(1)}, bf16[64,2624]{1,0:T(8,128)(2,1)S(1)}, u32[]{:S(2)}, u32[]{:S(2)}) collective-permute-start(bf16[64,2624]{1,0:T(8,128)(2,1)S(1)} %concatenate.273), channel_id=1, source_target_pairs={{0,16},{16,0},{1,17},{17,1},{2,18},{18,2},{3,19},{19,3},{4,20},{20... | collective-permute-start | bytes 1007624 | tf_op jit(solution)/shard_map/ppermute | solution.py:62
  1046.0 26.7 %collective-permute-start.195 = (bf16[4,64,1024]{2,1,0:T(8,128)(2,1)S(1)}, bf16[4,64,1024]{2,1,0:T(8,128)(2,1)S(1)}, u32[]{:S(2)}, u32[]{:S(2)}) collective-permute-start(bf16[4,64,1024]{2,1,0:T(8,128)(2,1)S(1)} %get-tuple-element.468), channel_id=1, source_target_pairs={{0,16},{16,0},{1,17},{17,1},{2,18},{18,2},{3,19},{19,3},{4,20},{20... | collective-permute-start | bytes 1572872 | tf_op jit(solution)/shard_map/ppermute | solution.py:62
  1069.7 39.5 %collective-permute-start.196 = (bf16[184,1024]{1,0:T(8,128)(2,1)S(1)}, bf16[184,1024]{1,0:T(8,128)(2,1)S(1)}, u32[]{:S(2)}, u32[]{:S(2)}) collective-permute-start(bf16[184,1024]{1,0:T(8,128)(2,1)S(1)} %copy-done.172), channel_id=1, source_target_pairs={{0,2},{1,3},{2,0},{3,1},{4,6},{5,7},{6,4},{7,5},{8,10},{9,11},{10,... | collective-permute-start | bytes 1130504 | tf_op jit(solution)/shard_map/ppermute | solution.py:58
  1069.9 39.4 %collective-permute-start.199 = (bf16[256,2048]{1,0:T(8,128)(2,1)S(1)}, bf16[256,2048]{1,0:T(8,128)(2,1)S(1)}, u32[]{:S(2)}, u32[]{:S(2)}) collective-permute-start(bf16[256,2048]{1,0:T(8,128)(2,1)S(1)} %copy-done.112), channel_id=1, source_target_pairs={{0,1},{1,0},{2,3},{3,2},{4,5},{5,4},{6,7},{7,6},{8,9},{9,8},{10,11... | collective-permute-start | bytes 3145736 | tf_op jit(solution)/shard_map/ppermute | solution.py:58
  1071.3 38.0 %collective-permute-start.197 = (bf16[184,1024]{1,0:T(8,128)(2,1)S(1)}, bf16[184,1024]{1,0:T(8,128)(2,1)S(1)}, u32[]{:S(2)}, u32[]{:S(2)}) collective-permute-start(bf16[184,1024]{1,0:T(8,128)(2,1)S(1)} %get-tuple-element.397), channel_id=1, source_target_pairs={{0,1},{1,0},{2,3},{3,2},{4,5},{5,4},{6,7},{7,6},{8,9},{9,8},{10,11... | collective-permute-start | bytes 1130504 | tf_op jit(solution)/shard_map/ppermute | solution.py:58
  1072.3 27.2 %collective-permute-start.179 = (bf16[64,1024]{1,0:T(8,128)(2,1)S(1)}, bf16[64,1024]{1,0:T(8,128)(2,1)S(1)}, u32[]{:S(2)}, u32[]{:S(2)}) collective-permute-start(bf16[64,1024]{1,0:T(8,128)(2,1)S(1)} %get-tuple-element.418), channel_id=1, source_target_pairs={{0,2},{1,3},{2,0},{3,1},{4,6},{5,7},{6,4},{7,5},{8,10},{9,11},{10,... | collective-permute-start | bytes 393224 | tf_op jit(solution)/shard_map/ppermute | solution.py:58
  1072.7 29.5 %collective-permute-start.181 = (bf16[64,1024]{1,0:T(8,128)(2,1)S(1)}, bf16[64,1024]{1,0:T(8,128)(2,1)S(1)}, u32[]{:S(2)}, u32[]{:S(2)}) collective-permute-start(bf16[64,1024]{1,0:T(8,128)(2,1)S(1)} %get-tuple-element.426), channel_id=1, source_target_pairs={{0,1},{1,0},{2,3},{3,2},{4,5},{5,4},{6,7},{7,6},{8,9},{9,8},{10,11... | collective-permute-start | bytes 393224 | tf_op jit(solution)/shard_map/ppermute | solution.py:58
  1118.4 49.1 %collective-permute-start.212 = (bf16[256,2048]{1,0:T(8,128)(2,1)}, bf16[256,2048]{1,0:T(8,128)(2,1)}, u32[]{:S(2)}, u32[]{:S(2)}) collective-permute-start(bf16[256,2048]{1,0:T(8,128)(2,1)} %fusion.63), channel_id=1, source_target_pairs={{0,1},{1,0},{2,3},{3,2},{4,5},{5,4},{6,7},{7,6},{8,9},{9,8},{10,11... | collective-permute-start | bytes 3145736 | tf_op jit(solution)/shard_map/ppermute | solution.py:58
  1123.9 24.8 %collective-permute-start.210 = (bf16[184,1024]{1,0:T(8,128)(2,1)S(1)}, bf16[184,1024]{1,0:T(8,128)(2,1)S(1)}, u32[]{:S(2)}, u32[]{:S(2)}) collective-permute-start(bf16[184,1024]{1,0:T(8,128)(2,1)S(1)} %get-tuple-element.385), channel_id=1, source_target_pairs={{0,2},{1,3},{2,0},{3,1},{4,6},{5,7},{6,4},{7,5},{8,10},{9,11},{10,... | collective-permute-start | bytes 1130504 | tf_op jit(solution)/shard_map/ppermute | solution.py:58
  1124.0 41.9 %collective-permute-start.208 = (bf16[184,1024]{1,0:T(8,128)(2,1)}, bf16[184,1024]{1,0:T(8,128)(2,1)}, u32[]{:S(2)}, u32[]{:S(2)}) collective-permute-start(bf16[184,1024]{1,0:T(8,128)(2,1)} %get-tuple-element.387), channel_id=1, source_target_pairs={{0,2},{1,3},{2,0},{3,1},{4,6},{5,7},{6,4},{7,5},{8,10},{9,11},{10,... | collective-permute-start | bytes 1130504 | tf_op jit(solution)/shard_map/ppermute | solution.py:58
  1125.4 42.1 %collective-permute-start.209 = (bf16[184,1024]{1,0:T(8,128)(2,1)}, bf16[184,1024]{1,0:T(8,128)(2,1)}, u32[]{:S(2)}, u32[]{:S(2)}) collective-permute-start(bf16[184,1024]{1,0:T(8,128)(2,1)} %get-tuple-element.386), channel_id=1, source_target_pairs={{0,2},{1,3},{2,0},{3,1},{4,6},{5,7},{6,4},{7,5},{8,10},{9,11},{10,... | collective-permute-start | bytes 1130504 | tf_op jit(solution)/shard_map/ppermute | solution.py:58
  1159.5 55.5 %all-to-all-start = ((bf16[16,72,720]{2,1,0:T(8,128)(2,1)}), bf16[16,72,720]{2,1,0:T(8,128)(2,1)}, u32[]{:S(2)}, u32[]{:S(2)}) async-start(bf16[16,72,720]{2,1,0:T(8,128)(2,1)} %copy.212), calls=%async_computation.1 | async-start | bytes 3538944 | tf_op jit(solution)/shard_map/all_to_all | solution.py:707
  1183.4 61.6 %collective-permute-start.217 = (bf16[3,512,2048]{2,1,0:T(8,128)(2,1)}, bf16[3,512,2048]{2,1,0:T(8,128)(2,1)}, u32[]{:S(2)}, u32[]{:S(2)}) collective-permute-start(bf16[3,512,2048]{2,1,0:T(8,128)(2,1)} %select_convert_fusion), channel_id=1, source_target_pairs={{0,16},{16,0},{1,17},{17,1},{2,18},{18,2},{3,19},{19,3},{4,20},{20... | collective-permute-start | bytes 18874376 | tf_op jit(solution)/shard_map/ppermute | solution.py:62
  1204.8 21.3 %collective-permute-start.204 = (bf16[184,1024]{1,0:T(8,128)(2,1)S(1)}, bf16[184,1024]{1,0:T(8,128)(2,1)S(1)}, u32[]{:S(2)}, u32[]{:S(2)}) collective-permute-start(bf16[184,1024]{1,0:T(8,128)(2,1)S(1)} %copy-done.181), channel_id=1, source_target_pairs={{0,2},{1,3},{2,0},{3,1},{4,6},{5,7},{6,4},{7,5},{8,10},{9,11},{10,... | collective-permute-start | bytes 1130504 | tf_op jit(solution)/shard_map/ppermute | solution.py:58
  1235.3 27.2 %collective-permute-start.220 = (bf16[184,1024]{1,0:T(8,128)(2,1)S(1)}, bf16[184,1024]{1,0:T(8,128)(2,1)S(1)}, u32[]{:S(2)}, u32[]{:S(2)}) collective-permute-start(bf16[184,1024]{1,0:T(8,128)(2,1)S(1)} %fusion.207), channel_id=1, source_target_pairs={{0,8},{1,9},{2,10},{3,11},{4,12},{5,13},{6,14},{7,15},{16,24},{17,... | collective-permute-start | bytes 1130504 | tf_op jit(solution)/shard_map/ppermute | solution.py:498
  (524 other events, 7145.6 us)
Sparse Core Ops, SparseCore 0:
  40.8 190.4 all-gather.4
  316.3 64.1 reduce-scatter.1
  589.1 98.6 all-gather.6
  819.2 56.1 all-gather.8
  878.4 93.9 all-gather.10

commit v4 on v3

--- a/solution.py
+++ b/solution.py
@@ -98,12 +98,17 @@
     return found
 
 
-def scatter_steps(terms, n, orders, sums, beside=None):
+def scatter_steps(terms, n, orders, sums, finish=None, pieces=(), landed=None):
     totals = dict(terms)
-    for number, edges in enumerate(reversed(tree(n, orders))):
-        sent = [hop(totals[offset].astype(BF), n, dims, -1) for offset, _, dims in edges]
-        if number == 1 and beside is not None:
-            sent = beside(sent)
+    levels = tree(n, orders)
+    for number, edges in enumerate(reversed(levels)):
+        sent = [totals[offset].astype(BF) for offset, _, _ in edges]
+        if finish is not None and edges is levels[0]:
+            sent = finish(sent)
+        if number < len(pieces):
+            sent, piece = tie(sent, pieces[number])
+            landed.append(hop(piece, n, (2, 2), -1))
+        sent = [hop(value, n, dims, -1) for value, (_, _, dims) in zip(sent, edges)]
         sent, _ = yield sent
         for (_, parent, _), value in zip(edges, sent):
             totals[parent] = totals[parent].astype(F32) + value.astype(F32)
@@ -482,7 +487,7 @@
     first = (rows_dev // 2 + 7) // 8 * 8
     upper_rows = n // 2 * rows_dev
 
-    def early_rows(term, result, beside=None, finish=None):
+    def early_rows(term, result, finish=None, riding=(), landed=None):
         shaped = term.reshape(n // 2, rows_dev, HALF)
         upper = me >= n // 2
         pieces = {}
@@ -491,14 +496,14 @@
             place = (target % (n // 2), jnp.where(target >= n // 2, 0, rows_dev - first), 0)
             pieces[offset] = lax.dynamic_slice(shaped, place, (1, first, HALF))[0]
         sums = []
-        yield from scatter_steps(pieces, n, ALL_CHIPS, sums, beside)
+        yield from scatter_steps(pieces, n, ALL_CHIPS, sums, finish, riding, landed)
         mine = sums[0].astype(BF)
-        if finish is not None:
-            mine = finish(mine)
         sent = lax.ppermute(mine, "shard", [(i, i + n // 2) for i in range(n // 2)])
         (sent,), _ = yield [sent]
         whole = jnp.concatenate([mine, sent[2 * first - rows_dev :]], axis=0).astype(F32)
         result.append(jnp.where(upper, whole, 0.0))
+
+    last_base, last_pieces = [], []
 
     def backward(layer, kept, grad_out_b, passed, early, due):
         rows = attn_rows[layer]
@@ -552,18 +557,21 @@
         ]
         grad_prenorm, pair_sums, ff_base = background.stage(grad_prenorm, pair_sums, ff_base)
 
-        def pass_back():
+        def pass_back(groups):
             anchor = None
-            for which in range(3):
+            for group in groups:
                 carried = None
                 for steps in range(side - 1, 0, -1):
-                    term = after(pair_sums[which][steps - 1], anchor)
+                    terms = [after(pair_sums[which][steps - 1], anchor) for which in group]
                     if carried is not None:
-                        term = (term.astype(F32) + carried.astype(F32)).astype(BF)
-                    (carried,), anchor = yield [hop(term, n, (2, 2), -1)]
-                passed.append(carried)
-
-        background.add(pass_back())
+                        terms = [
+                            (term.astype(F32) + part.astype(F32)).astype(BF)
+                            for term, part in zip(terms, carried)
+                        ]
+                    carried, anchor = yield [hop(term, n, (2, 2), -1) for term in terms]
+                passed.extend(carried)
+
+        background.add(pass_back(((0, 1),) if layer == 0 else ((0,), (1,), (2,))))
         join_pull = jax.vjp(
             join_piece,
             kept["hidden_in"],
@@ -610,7 +618,11 @@
             (kept["gated_b"], grad_projected_b),
         )
         work = due[1]() if callable(due[1]) else due[1]
-        grad_key_value, early_pairs, work = background.stage(grad_key_value, early_pairs, work)
+        grad_key_value, early_pairs, work, ff_base = background.stage(
+            grad_key_value, early_pairs, work, ff_base
+        )
+        if layer == 0:
+            ff_other = swap_cores(pick(last_base[0], ff_base))
         early_term = early_products(early_pairs)
         due[1] = due[2](work)
         terms = {o: grad_key_value[i * seq : (i + 1) * seq] for i, o in enumerate(key_offsets)}
@@ -628,13 +640,22 @@
             + back_product(grad_q_b, rows, 0, QW, core)
             + back_product(grad_z_b, rows, QW + 2 * KW, IN_ROWS, core)
         )
-        grad_local, grad_normed, early_term, due[1] = background.stage(
-            grad_local, grad_normed, early_term, due[1]
-        )
-        if layer == 1:
+        if layer == 0:
+            grad_local, grad_normed, early_term, due[1], pair_sums[2] = tie(
+                grad_local, grad_normed, early_term, due[1], pair_sums[2]
+            )
+            if side == 2:
+                last_pieces.extend(jnp.split(pair_sums[2][0], 4, axis=0))
+            else:
+                background.add(pass_back(((2,),)))
+            ff_base = pick(ff_base, last_base[0]).astype(F32) + ff_other.astype(F32)
+            early.append(early_term)
+        else:
+            grad_local, grad_normed, early_term, due[1] = background.stage(
+                grad_local, grad_normed, early_term, due[1]
+            )
             background.add(early_rows(early_term, early))
-        else:
-            early.append(early_term)
+            last_base.append(ff_base)
         grad_projected_kv, grad_key_gain = jax.vjp(
             key_value_split, kept["projected_kv"], key_gain
         )[1](grad_local)
@@ -666,7 +687,7 @@
     top = pick(cotangent[0], cotangent[1])
     passed_0, passed_1, early_0, early_1, sides = [], [], [], [], []
     due_1 = [sides, normed_all_0, lambda work: work]
-    grad_1, late_1, ff_base_1, gain_vec_1 = backward(1, kept_1, top, passed_1, early_1, due_1)
+    grad_1, late_1, _, gain_vec_1 = backward(1, kept_1, top, passed_1, early_1, due_1)
     normed_all_0 = due_1[1]
     grad_1, normed_b = tie(grad_1, kept_1["normed_b"])
     normed_all_1 = lax.all_gather(normed_b, "shard", axis=0, tiled=True)
@@ -683,7 +704,7 @@
     due_0 = [sides, None, lambda work: (table_product(work[0]), work[1])]
     due_0_start = lambda: (gather_sides(), normed_all_1)
     due_0[1] = due_0_start
-    grad_0, late_0, ff_base_0, gain_vec_0 = backward(0, kept_0, grad_1, passed_0, early_0, due_0)
+    grad_0, late_0, ff_base, gain_vec_0 = backward(0, kept_0, grad_1, passed_0, early_0, due_0)
     table_grad, normed_all_1 = due_0[1]
 
     def to_owners(late):
@@ -707,18 +728,14 @@
     incoming = lax.all_to_all(outgoing, "shard", 0, 0, tiled=True)
     background.drain()
 
-    def whole_ff(base, passed):
-        passed = jnp.concatenate([part[None] for part in passed], axis=0)
-        zeros = jnp.zeros((3, units - half_units, D), BF)
-        placed = pick(
-            jnp.concatenate([passed, zeros], axis=1), jnp.concatenate([zeros, passed], axis=1)
-        )
-        return base.astype(F32) + placed.astype(F32)
-
-    def finish_ff(base_0, passed_0, base_1, passed_1):
-        whole_0, whole_1 = whole_ff(base_0, passed_0), whole_ff(base_1, passed_1)
-        other = swap_cores(pick(whole_1, whole_0).astype(BF)).astype(F32)
-        return pick(whole_0, whole_1) + other
+    def finish_ff():
+        passed = [
+            jnp.concatenate([part[None] for part in parts], axis=0)
+            for parts in (passed_0, passed_1)
+        ]
+        mine, theirs = pick(*passed), swap_cores(pick(passed[1], passed[0]))
+        halves_in_order = jnp.concatenate([pick(mine, theirs), pick(theirs, mine)], axis=1)
+        return ff_base + halves_in_order.astype(F32)
 
     def late_rows(arrived):
         sums = [
@@ -732,19 +749,16 @@
         ]
         return pick(sums[0], sums[1]) + swap_cores(pick(sums[1], sums[0]).astype(BF)).astype(F32)
 
-    ready = []
-
-    def beside(sent):
-        sent, parts = tie(sent, (ff_base_0, passed_0, ff_base_1, passed_1))
-        ready.append(finish_ff(*parts))
+    ready, landed = [], []
+
+    def finish(sent):
+        if landed:
+            passed_0.append(jnp.concatenate(landed, axis=0))
+        ready.extend([finish_ff(), late_rows(incoming)])
+        sent, ready[:] = tie(sent, list(ready))
         return sent
 
-    def finish(mine):
-        ready.append(late_rows(incoming))
-        mine, ready[:] = tie(mine, list(ready))
-        return mine
-
-    run(early_rows(early_0.pop(), early_0, beside, finish))
+    run(early_rows(early_0.pop(), early_0, finish, last_pieces, landed))
     ff_grad, late_grad = ready
     early_keep = pick(early_0[0], early_1[0])
     early_other = swap_cores(pick(early_1[0], early_0[0]))

time: 1310 us -> 1310 us (level)
  waiting for transfers between devices: 495 us -> 475 us
    ppermute x173 -> x176, waiting for transfers between devices: 468 us -> 438 us  [hop(): return lax.ppermute(value, ('section', 'shard'), pairs)]
    select_n x11 -> x14, other arithmetic: 8.55 us -> 21.9 us  [pick(): return jnp.where(core == 0, for_0, for_1)]
    ppermute x44 -> x45, starting transfers between devices: 101 us -> 108 us  [swap_cores(): return lax.ppermute(value, 'section', [(0, 1), (1, 0)])]
    ppermute x173 -> x176, starting transfers between devices: 151 us -> 157 us  [hop(): return lax.ppermute(value, ('section', 'shard'), pairs)]
    convert_element_type x29 -> x28, other arithmetic: 31.3 us -> 26.4 us  [scatter_steps(): sent = [totals[offset].astype(BF) for offset, _, _ in edges]]
    unnamed x804 -> x812, local copies, waits for them, and re-layouts: 30.3 us -> 29.9 us
  transfers between devices with their start and end apart: 229 -> 233, of which waited for: 95 -> 91; matrix products, arithmetic and copies ran while one was open for 35% -> 35% of each run, Pallas kernels for 0% -> 0%
where the time goes in v4:
time: 1310 us; the launch traced here: 1300 us
  waiting for transfers between devices  475 us (36%)
  starting transfers between devices  277 us (21%)
  matrix products  268 us (20%)
  local copies, waits for them, and re-layouts  132 us (10%)
  other arithmetic  123 us (9%)
  between operations  21.6 us (2%)
    ppermute x176, waiting for transfers between devices, hop(): return lax.ppermute(value, ('section', 'shard'), pairs)  438 us
    ppermute x176, starting transfers between devices, hop(): return lax.ppermute(value, ('section', 'shard'), pairs)  157 us
    ppermute x45, starting transfers between devices, swap_cores(): return lax.ppermute(value, 'section', [(0, 1), (1, 0)])  108 us
    dot_general x46, matrix products, dot_rows(): lax.dot_general(left_side, right_side, (((1,), (1,)), ((), ())), preferre...  93.4 us
    dot_general x47, matrix products, dot(): return jnp.dot(left_side, right_side, preferred_element_type=F32)  92.5 us
    dot_general x29, matrix products, dot_first(): lax.dot_general(left_side, right_side, (((0,), (0,)), ((), ())), preferre...  56 us
    dynamic_update_slice x31, local copies, waits for them, and re-layouts, store_blocks(): lax.dynamic_update_slice(buffer, value[None], (source, jnp.int32(0), jnp....  35.3 us
    unnamed x812, local copies, waits for them, and re-layouts  29.9 us
  transfers between devices with their start and end apart: 233, of which 91 were waited for; matrix products, arithmetic and copies ran while one was open for 35% of the time, Pallas kernels for 0%

profile of v4, /device:TPU:27, one launch (start us, length us, event | category | flops | bytes accessed | tf_op | source)
XLA Modules:
  0.0 1297.2 jit_solution(2634174993430041190)
XLA Ops:
  25.7 6.0 broadcast.708.clone
  40.7 7.2 fusion.45
  48.7 6.1 broadcast.708
  59.3 5.1 collective-permute-done.8
  67.9 8.9 collective-permute-done.10
  76.8 16.3 %collective-permute-start.14 = (bf16[360,1024]{1,0:T(8,128)(2,1)}, bf16[360,1024]{1,0:T(8,128)(2,1)S(1)}, u32[]{:S(2)}, u32[]{:S(2)}) collective-permute-start(bf16[360,1024]{1,0:T(8,128)(2,1)} %collective-permute-done.6), channel_id=1, source_target_pairs={{0,16},{16,0},{1,17},{17,1},{2,18},{18,2},{3,19},{19,3},{4,20},{20... | collective-permute-start | bytes 2211848 | tf_op jit(solution)/shard_map/ppermute | solution.py:62
  95.2 7.1 collective-permute-done.11
  131.9 27.8 %collective-permute-done.18 = bf16[360,1024]{1,0:T(8,128)(2,1)S(1)} collective-permute-done((bf16[360,1024]{1,0:T(8,128)(2,1)S(1)}, bf16[360,1024]{1,0:T(8,128)(2,1)S(1)}, u32[]{:S(2)}, u32[]{:S(2)}) %collective-permute-start.18) | collective-permute-done | bytes 737312 | tf_op jit(solution)/shard_map/ppermute | solution.py:58
  160.9 9.1 collective-permute-start.27
  177.2 34.2 %collective-permute-done.26 = bf16[360,1024]{1,0:T(8,128)(2,1)S(1)} collective-permute-done((bf16[360,1024]{1,0:T(8,128)(2,1)S(1)}, bf16[360,1024]{1,0:T(8,128)(2,1)S(1)}, u32[]{:S(2)}, u32[]{:S(2)}) %collective-permute-start.26) | collective-permute-done | bytes 737312 | tf_op jit(solution)/shard_map/ppermute | solution.py:58
  260.7 16.6 %collective-permute-done.40 = bf16[64,1024]{1,0:T(8,128)(2,1)S(1)} collective-permute-done((bf16[64,1024]{1,0:T(8,128)(2,1)}, bf16[64,1024]{1,0:T(8,128)(2,1)S(1)}, u32[]{:S(2)}, u32[]{:S(2)}) %collective-permute-start.40) | collective-permute-done | bytes 131104 | tf_op jit(solution)/shard_map/ppermute | solution.py:58
  284.9 4.1 collective-permute-done.51
  312.3 5.4 collective-permute-done.54
  319.9 4.4 collective-permute-done.56
  332.9 4.1 collective-permute-start.60
  343.9 4.7 collective-permute-done.61
  348.6 5.2 collective-permute-done.62
  375.3 8.0 collective-permute-done.69
  426.4 5.8 collective-permute-done.75
  455.4 5.7 collective-permute-done.78
  500.8 6.9 collective-permute-start.100
  508.6 5.4 collective-permute-done.96
  517.9 5.1 collective-permute-done.98
  524.7 6.7 collective-permute-done.99
  557.1 4.3 collective-permute-done.107
  563.7 4.9 collective-permute-done.108
  570.0 5.7 collective-permute-done.109
  608.6 4.1 collective-permute-done.116
  612.7 7.3 collective-permute-done.117
  620.1 4.2 fusion.41
  642.0 20.3 %collective-permute-start.127 = (bf16[256,2048]{1,0:T(8,128)(2,1)}, bf16[256,2048]{1,0:T(8,128)(2,1)S(1)}, u32[]{:S(2)}, u32[]{:S(2)}) collective-permute-start(bf16[256,2048]{1,0:T(8,128)(2,1)} %convolution_convert_fusion.12), channel_id=1, source_target_pairs={{0,16},{16,0},{1,17},{17,1},{2,18},{18,2},{3,19},{19,3},{4,20},{20... | collective-permute-start | bytes 3145736 | tf_op jit(solution)/shard_map/ppermute | solution.py:62
  668.0 11.0 collective-permute-done.121
  680.5 4.3 collective-permute-done.120
  685.1 5.0 collective-permute-done.122
  696.1 4.6 collective-permute-done.123
  749.2 6.9 collective-permute-done.128
  763.0 4.5 collective-permute-start.144
  795.5 12.1 collective-permute-done.129
  841.1 19.4 %collective-permute-done.147 = bf16[256,2048]{1,0:T(8,128)(2,1)S(1)} collective-permute-done((bf16[256,2048]{1,0:T(8,128)(2,1)}, bf16[256,2048]{1,0:T(8,128)(2,1)S(1)}, u32[]{:S(2)}, u32[]{:S(2)}) %collective-permute-start.147) | collective-permute-done | bytes 1048608 | tf_op jit(solution)/shard_map/ppermute | solution.py:58
  865.8 6.3 collective-permute-done.150
  876.3 6.1 collective-permute-done.152
  883.4 4.1 collective-permute-start.154
  893.3 11.4 collective-permute-done.155
  935.3 6.4 collective-permute-done.162
  942.6 10.4 collective-permute-done.161
  957.2 7.5 collective-permute-done.160
  1025.5 4.6 broadcast_select_fusion.24
  1033.4 6.5 collective-permute-done.179
  1047.7 12.1 collective-permute-start.195
  1075.1 11.3 fusion.2
  1108.9 5.6 collective-permute-done.198
  1124.5 7.1 all-to-all-start
  1136.7 6.1 broadcast_select_fusion
  1142.9 5.4 collective-permute-start.210
  1149.5 8.2 collective-permute-done.203
  1159.2 5.3 collective-permute-done.205
  1167.8 5.3 collective-permute-done.213
  1173.1 9.7 collective-permute-done.214
  1186.7 4.8 collective-permute-start.215
  1196.1 4.1 fusion.594
  1223.4 10.2 convert_add_fusion
  1248.4 5.6 collective-permute-start.197
  1254.0 18.2 %collective-permute-done.224 = bf16[184,1024]{1,0:T(8,128)(2,1)S(1)} collective-permute-done((bf16[184,1024]{1,0:T(8,128)(2,1)S(1)}, bf16[184,1024]{1,0:T(8,128)(2,1)S(1)}, u32[]{:S(2)}, u32[]{:S(2)}) %collective-permute-start.224) | collective-permute-done | bytes 376864 | tf_op jit(solution)/shard_map/ppermute | solution.py:501
  1272.2 8.0 collective-permute-done.220
  (1718 shorter events, 750.6 us)
Async XLA Ops:
  7.2 329.8 %all-gather.5.cloned.1.call-start = ((), (), s32[]{:S(2)}) async-start(), calls=%async_computation.3 | async-start | bytes 12533760 | tf_op jit(solution)/shard_map/all_gather | solution.py:311
  10.5 116.2 %collective-permute-start.21 = (bf16[3,512,2048]{2,1,0:T(8,128)(2,1)}, bf16[3,512,2048]{2,1,0:T(8,128)(2,1)}, u32[]{:S(2)}, u32[]{:S(2)}) collective-permute-start(bf16[3,512,2048]{2,1,0:T(8,128)(2,1)} %bitcast.648), channel_id=1, source_target_pairs={{0,16},{16,0},{1,17},{17,1},{2,18},{18,2},{3,19},{19,3},{4,20},{20... | collective-permute-start | bytes 18874376 | tf_op jit(solution)/shard_map/ppermute | solution.py:62
  39.5 24.9 %collective-permute-start.8 = (bf16[360,1024]{1,0:T(8,128)(2,1)}, bf16[360,1024]{1,0:T(8,128)(2,1)}, u32[]{:S(2)}, u32[]{:S(2)}) collective-permute-start(bf16[360,1024]{1,0:T(8,128)(2,1)} %get-tuple-element.391), channel_id=1, source_target_pairs={{0,4},{1,5},{2,6},{3,7},{4,8},{5,9},{6,10},{7,11},{8,12},{9,13},{1... | collective-permute-start | bytes 2211848 | tf_op jit(solution)/shard_map/ppermute | solution.py:58
  40.6 353.4 %reduce-scatter.2.cloned.1.call-start = ((), (), s32[]{:S(2)}) async-start(), calls=%async_computation.2 | async-start | bytes 1114112 | tf_op jit(solution)/shard_map/reduce_scatter | solution.py:344
  67.4 34.9 %collective-permute-start.11 = (bf16[360,1024]{1,0:T(8,128)(2,1)}, bf16[360,1024]{1,0:T(8,128)(2,1)}, u32[]{:S(2)}, u32[]{:S(2)}) collective-permute-start(bf16[360,1024]{1,0:T(8,128)(2,1)} %collective-permute-done.8), channel_id=1, source_target_pairs={{0,2},{1,3},{2,0},{3,1},{4,6},{5,7},{6,4},{7,5},{8,10},{9,11},{10,... | collective-permute-start | bytes 2211848 | tf_op jit(solution)/shard_map/ppermute | solution.py:58
  67.6 39.7 %collective-permute-start.12 = (bf16[360,1024]{1,0:T(8,128)(2,1)}, bf16[360,1024]{1,0:T(8,128)(2,1)S(1)}, u32[]{:S(2)}, u32[]{:S(2)}) collective-permute-start(bf16[360,1024]{1,0:T(8,128)(2,1)} %collective-permute-done.8), channel_id=1, source_target_pairs={{0,1},{1,0},{2,3},{3,2},{4,5},{5,4},{6,7},{7,6},{8,9},{9,8},{10,11... | collective-permute-start | bytes 2211848 | tf_op jit(solution)/shard_map/ppermute | solution.py:58
  67.7 41.7 %collective-permute-start.13 = (bf16[360,1024]{1,0:T(8,128)(2,1)}, bf16[360,1024]{1,0:T(8,128)(2,1)S(1)}, u32[]{:S(2)}, u32[]{:S(2)}) collective-permute-start(bf16[360,1024]{1,0:T(8,128)(2,1)} %collective-permute-done.8), channel_id=1, source_target_pairs={{0,4},{1,5},{2,6},{3,7},{4,8},{5,9},{6,10},{7,11},{8,12},{9,13},{1... | collective-permute-start | bytes 2211848 | tf_op jit(solution)/shard_map/ppermute | solution.py:58
  76.8 32.5 %collective-permute-start.14 = (bf16[360,1024]{1,0:T(8,128)(2,1)}, bf16[360,1024]{1,0:T(8,128)(2,1)S(1)}, u32[]{:S(2)}, u32[]{:S(2)}) collective-permute-start(bf16[360,1024]{1,0:T(8,128)(2,1)} %collective-permute-done.6), channel_id=1, source_target_pairs={{0,16},{16,0},{1,17},{17,1},{2,18},{18,2},{3,19},{19,3},{4,20},{20... | collective-permute-start | bytes 2211848 | tf_op jit(solution)/shard_map/ppermute | solution.py:62
  121.5 38.2 %collective-permute-start.18 = (bf16[360,1024]{1,0:T(8,128)(2,1)S(1)}, bf16[360,1024]{1,0:T(8,128)(2,1)S(1)}, u32[]{:S(2)}, u32[]{:S(2)}) collective-permute-start(bf16[360,1024]{1,0:T(8,128)(2,1)S(1)} %collective-permute-done.13), channel_id=1, source_target_pairs={{0,2},{1,3},{2,0},{3,1},{4,6},{5,7},{6,4},{7,5},{8,10},{9,11},{10,... | collective-permute-start | bytes 2211848 | tf_op jit(solution)/shard_map/ppermute | solution.py:58
  122.4 37.3 %collective-permute-start.19 = (bf16[360,1024]{1,0:T(8,128)(2,1)S(1)}, bf16[360,1024]{1,0:T(8,128)(2,1)S(1)}, u32[]{:S(2)}, u32[]{:S(2)}) collective-permute-start(bf16[360,1024]{1,0:T(8,128)(2,1)S(1)} %collective-permute-done.13), channel_id=1, source_target_pairs={{0,1},{1,0},{2,3},{3,2},{4,5},{5,4},{6,7},{7,6},{8,9},{9,8},{10,11... | collective-permute-start | bytes 2211848 | tf_op jit(solution)/shard_map/ppermute | solution.py:58
  125.8 35.1 %collective-permute-start.20 = (bf16[360,1024]{1,0:T(8,128)(2,1)S(1)}, bf16[360,1024]{1,0:T(8,128)(2,1)S(1)}, u32[]{:S(2)}, u32[]{:S(2)}) collective-permute-start(bf16[360,1024]{1,0:T(8,128)(2,1)S(1)} %collective-permute-done.13), channel_id=1, source_target_pairs={{0,4},{1,5},{2,6},{3,7},{4,8},{5,9},{6,10},{7,11},{8,12},{9,13},{1... | collective-permute-start | bytes 2211848 | tf_op jit(solution)/shard_map/ppermute | solution.py:58
  160.9 53.4 %collective-permute-start.27 = (bf16[360,1024]{1,0:T(8,128)(2,1)S(1)}, bf16[360,1024]{1,0:T(8,128)(2,1)S(1)}, u32[]{:S(2)}, u32[]{:S(2)}) collective-permute-start(bf16[360,1024]{1,0:T(8,128)(2,1)S(1)} %collective-permute-done.20), channel_id=1, source_target_pairs={{0,2},{1,3},{2,0},{3,1},{4,6},{5,7},{6,4},{7,5},{8,10},{9,11},{10,... | collective-permute-start | bytes 2211848 | tf_op jit(solution)/shard_map/ppermute | solution.py:58
  170.0 44.3 %collective-permute-start.28 = (bf16[360,1024]{1,0:T(8,128)(2,1)S(1)}, bf16[360,1024]{1,0:T(8,128)(2,1)S(1)}, u32[]{:S(2)}, u32[]{:S(2)}) collective-permute-start(bf16[360,1024]{1,0:T(8,128)(2,1)S(1)} %collective-permute-done.20), channel_id=1, source_target_pairs={{0,1},{1,0},{2,3},{3,2},{4,5},{5,4},{6,7},{7,6},{8,9},{9,8},{10,11... | collective-permute-start | bytes 2211848 | tf_op jit(solution)/shard_map/ppermute | solution.py:58
  170.0 44.3 %collective-permute-start.29 = (bf16[360,1024]{1,0:T(8,128)(2,1)S(1)}, bf16[360,1024]{1,0:T(8,128)(2,1)S(1)}, u32[]{:S(2)}, u32[]{:S(2)}) collective-permute-start(bf16[360,1024]{1,0:T(8,128)(2,1)S(1)} %collective-permute-done.17), channel_id=1, source_target_pairs={{0,16},{16,0},{1,17},{17,1},{2,18},{18,2},{3,19},{19,3},{4,20},{20... | collective-permute-start | bytes 2211848 | tf_op jit(solution)/shard_map/ppermute | solution.py:62
  172.0 43.3 %collective-permute-start.30 = (bf16[360,1024]{1,0:T(8,128)(2,1)S(1)}, bf16[360,1024]{1,0:T(8,128)(2,1)S(1)}, u32[]{:S(2)}, u32[]{:S(2)}) collective-permute-start(bf16[360,1024]{1,0:T(8,128)(2,1)S(1)} %collective-permute-done.18), channel_id=1, source_target_pairs={{0,16},{16,0},{1,17},{17,1},{2,18},{18,2},{3,19},{19,3},{4,20},{20... | collective-permute-start | bytes 2211848 | tf_op jit(solution)/shard_map/ppermute | solution.py:62
  172.0 39.5 %collective-permute-start.26 = (bf16[360,1024]{1,0:T(8,128)(2,1)S(1)}, bf16[360,1024]{1,0:T(8,128)(2,1)S(1)}, u32[]{:S(2)}, u32[]{:S(2)}) collective-permute-start(bf16[360,1024]{1,0:T(8,128)(2,1)S(1)} %collective-permute-done.19), channel_id=1, source_target_pairs={{0,2},{1,3},{2,0},{3,1},{4,6},{5,7},{6,4},{7,5},{8,10},{9,11},{10,... | collective-permute-start | bytes 2211848 | tf_op jit(solution)/shard_map/ppermute | solution.py:58
  246.3 46.7 %collective-permute-start.53 = (bf16[256,2048]{1,0:T(8,128)(2,1)}, bf16[256,2048]{1,0:T(8,128)(2,1)}, u32[]{:S(2)}, u32[]{:S(2)}) collective-permute-start(bf16[256,2048]{1,0:T(8,128)(2,1)} %get-tuple-element.207), channel_id=1, source_target_pairs={{0,1},{1,0},{2,3},{3,2},{4,5},{5,4},{6,7},{7,6},{8,9},{9,8},{10,11... | collective-permute-start | bytes 3145736 | tf_op jit(solution)/shard_map/ppermute | solution.py:58
  254.8 23.3 %collective-permute-start.42 = (bf16[64,1024]{1,0:T(8,128)(2,1)S(1)}, bf16[64,1024]{1,0:T(8,128)(2,1)S(1)}, u32[]{:S(2)}, u32[]{:S(2)}) collective-permute-start(bf16[64,1024]{1,0:T(8,128)(2,1)S(1)} %collective-permute-done.41), channel_id=1, source_target_pairs={{0,2},{1,3},{2,0},{3,1},{4,6},{5,7},{6,4},{7,5},{8,10},{9,11},{10,... | collective-permute-start | bytes 393224 | tf_op jit(solution)/shard_map/ppermute | solution.py:58
  256.3 22.3 %collective-permute-start.43 = (bf16[64,1024]{1,0:T(8,128)(2,1)S(1)}, bf16[64,1024]{1,0:T(8,128)(2,1)S(1)}, u32[]{:S(2)}, u32[]{:S(2)}) collective-permute-start(bf16[64,1024]{1,0:T(8,128)(2,1)S(1)} %collective-permute-done.41), channel_id=1, source_target_pairs={{0,1},{1,0},{2,3},{3,2},{4,5},{5,4},{6,7},{7,6},{8,9},{9,8},{10,11... | collective-permute-start | bytes 393224 | tf_op jit(solution)/shard_map/ppermute | solution.py:58
  260.5 24.4 %collective-permute-start.46 = (bf16[64,1024]{1,0:T(8,128)(2,1)S(1)}, bf16[64,1024]{1,0:T(8,128)(2,1)S(1)}, u32[]{:S(2)}, u32[]{:S(2)}) collective-permute-start(bf16[64,1024]{1,0:T(8,128)(2,1)S(1)} %collective-permute-done.45), channel_id=1, source_target_pairs={{0,2},{1,3},{2,0},{3,1},{4,6},{5,7},{6,4},{7,5},{8,10},{9,11},{10,... | collective-permute-start | bytes 393224 | tf_op jit(solution)/shard_map/ppermute | solution.py:58
  293.1 24.6 %collective-permute-start.54 = (bf16[256,2048]{1,0:T(8,128)(2,1)}, bf16[256,2048]{1,0:T(8,128)(2,1)}, u32[]{:S(2)}, u32[]{:S(2)}) collective-permute-start(bf16[256,2048]{1,0:T(8,128)(2,1)} %get-tuple-element.211), channel_id=1, source_target_pairs={{0,1},{1,0},{2,3},{3,2},{4,5},{5,4},{6,7},{7,6},{8,9},{9,8},{10,11... | collective-permute-start | bytes 3145736 | tf_op jit(solution)/shard_map/ppermute | solution.py:58
  318.2 431.0 %all-gather.7.cloned.1.call-start = ((), (), s32[]{:S(2)}) async-start(), calls=%async_computation.4 | async-start | bytes 4456448 | tf_op jit(solution)/shard_map/all_gather | solution.py:686
  318.3 42.0 %collective-permute-start.63 = (bf16[256,2048]{1,0:T(8,128)(2,1)}, bf16[256,2048]{1,0:T(8,128)(2,1)}, u32[]{:S(2)}, u32[]{:S(2)}) collective-permute-start(bf16[256,2048]{1,0:T(8,128)(2,1)} %collective-permute-done.53), channel_id=1, source_target_pairs={{0,16},{16,0},{1,17},{17,1},{2,18},{18,2},{3,19},{19,3},{4,20},{20... | collective-permute-start | bytes 3145736 | tf_op jit(solution)/shard_map/ppermute | solution.py:62
  319.5 34.3 %collective-permute-start.62 = (bf16[256,2048]{1,0:T(8,128)(2,1)}, bf16[256,2048]{1,0:T(8,128)(2,1)}, u32[]{:S(2)}, u32[]{:S(2)}) collective-permute-start(bf16[256,2048]{1,0:T(8,128)(2,1)} %get-tuple-element.213), channel_id=1, source_target_pairs={{0,1},{1,0},{2,3},{3,2},{4,5},{5,4},{6,7},{7,6},{8,9},{9,8},{10,11... | collective-permute-start | bytes 3145736 | tf_op jit(solution)/shard_map/ppermute | solution.py:58
  337.0 81.4 %collective-permute-start.74 = (bf16[5760,1024]{1,0:T(8,128)(2,1)}, bf16[5760,1024]{1,0:T(8,128)(2,1)}, u32[]{:S(2)}, u32[]{:S(2)}) collective-permute-start(bf16[5760,1024]{1,0:T(8,128)(2,1)} %all-gather.5.cloned.1.call-done), channel_id=1, source_target_pairs={{0,16},{16,0},{1,17},{17,1},{2,18},{18,2},{3,19},{19,3},{4,20},{20... | collective-permute-start | bytes 35389448 | tf_op jit(solution)/shard_map/ppermute | solution.py:62
  341.0 25.0 %collective-permute-start.64 = (bf16[256,2048]{1,0:T(8,128)(2,1)}, bf16[256,2048]{1,0:T(8,128)(2,1)S(1)}, u32[]{:S(2)}, u32[]{:S(2)}) collective-permute-start(bf16[256,2048]{1,0:T(8,128)(2,1)} %collective-permute-done.54), channel_id=1, source_target_pairs={{0,16},{16,0},{1,17},{17,1},{2,18},{18,2},{3,19},{19,3},{4,20},{20... | collective-permute-start | bytes 3145736 | tf_op jit(solution)/shard_map/ppermute | solution.py:62
  433.1 43.7 %collective-permute-start.91 = (bf16[256,2048]{1,0:T(8,128)(2,1)S(1)}, bf16[256,2048]{1,0:T(8,128)(2,1)}, u32[]{:S(2)}, u32[]{:S(2)}) collective-permute-start(bf16[256,2048]{1,0:T(8,128)(2,1)S(1)} %get-tuple-element.223), channel_id=1, source_target_pairs={{0,1},{1,0},{2,3},{3,2},{4,5},{5,4},{6,7},{7,6},{8,9},{9,8},{10,11... | collective-permute-start | bytes 3145736 | tf_op jit(solution)/shard_map/ppermute | solution.py:58
  500.8 35.5 %collective-permute-start.100 = (bf16[256,2048]{1,0:T(8,128)(2,1)}, bf16[256,2048]{1,0:T(8,128)(2,1)S(1)}, u32[]{:S(2)}, u32[]{:S(2)}) collective-permute-start(bf16[256,2048]{1,0:T(8,128)(2,1)} %collective-permute-done.75), channel_id=1, source_target_pairs={{0,16},{16,0},{1,17},{17,1},{2,18},{18,2},{3,19},{19,3},{4,20},{20... | collective-permute-start | bytes 3145736 | tf_op jit(solution)/shard_map/ppermute | solution.py:62
  507.7 33.9 %collective-permute-start.101 = (bf16[256,2048]{1,0:T(8,128)(2,1)}, bf16[256,2048]{1,0:T(8,128)(2,1)S(1)}, u32[]{:S(2)}, u32[]{:S(2)}) collective-permute-start(bf16[256,2048]{1,0:T(8,128)(2,1)} %collective-permute-done.91), channel_id=1, source_target_pairs={{0,16},{16,0},{1,17},{17,1},{2,18},{18,2},{3,19},{19,3},{4,20},{20... | collective-permute-start | bytes 3145736 | tf_op jit(solution)/shard_map/ppermute | solution.py:62
  507.8 40.1 %collective-permute-start.102 = (bf16[256,2048]{1,0:T(8,128)(2,1)}, bf16[256,2048]{1,0:T(8,128)(2,1)S(1)}, u32[]{:S(2)}, u32[]{:S(2)}) collective-permute-start(bf16[256,2048]{1,0:T(8,128)(2,1)} %collective-permute-done.92), channel_id=1, source_target_pairs={{0,16},{16,0},{1,17},{17,1},{2,18},{18,2},{3,19},{19,3},{4,20},{20... | collective-permute-start | bytes 3145736 | tf_op jit(solution)/shard_map/ppermute | solution.py:62
  593.2 436.9 %all-gather.9.cloned.1.call-start = ((), (), s32[]{:S(2)}) async-start(), calls=%async_computation.5 | async-start | bytes 1114112 | tf_op jit(solution)/shard_map/all_gather | solution.py:702
  642.0 58.9 %collective-permute-start.127 = (bf16[256,2048]{1,0:T(8,128)(2,1)}, bf16[256,2048]{1,0:T(8,128)(2,1)S(1)}, u32[]{:S(2)}, u32[]{:S(2)}) collective-permute-start(bf16[256,2048]{1,0:T(8,128)(2,1)} %convolution_convert_fusion.12), channel_id=1, source_target_pairs={{0,16},{16,0},{1,17},{17,1},{2,18},{18,2},{3,19},{19,3},{4,20},{20... | collective-permute-start | bytes 3145736 | tf_op jit(solution)/shard_map/ppermute | solution.py:62
  663.0 39.6 %collective-permute-start.126 = (bf16[256,2048]{1,0:T(8,128)(2,1)S(1)}, bf16[256,2048]{1,0:T(8,128)(2,1)S(1)}, u32[]{:S(2)}, u32[]{:S(2)}) collective-permute-start(bf16[256,2048]{1,0:T(8,128)(2,1)S(1)} %convolution_convert_fusion.14), channel_id=1, source_target_pairs={{0,16},{16,0},{1,17},{17,1},{2,18},{18,2},{3,19},{19,3},{4,20},{20... | collective-permute-start | bytes 3145736 | tf_op jit(solution)/shard_map/ppermute | solution.py:62
  664.2 40.2 %collective-permute-start.125 = (bf16[256,2048]{1,0:T(8,128)(2,1)S(1)}, bf16[256,2048]{1,0:T(8,128)(2,1)S(1)}, u32[]{:S(2)}, u32[]{:S(2)}) collective-permute-start(bf16[256,2048]{1,0:T(8,128)(2,1)S(1)} %convolution_convert_fusion.16), channel_id=1, source_target_pairs={{0,16},{16,0},{1,17},{17,1},{2,18},{18,2},{3,19},{19,3},{4,20},{20... | collective-permute-start | bytes 3145736 | tf_op jit(solution)/shard_map/ppermute | solution.py:62
  733.5 22.7 %collective-permute-start.128 = (bf16[256,2048]{1,0:T(8,128)(2,1)}, bf16[256,2048]{1,0:T(8,128)(2,1)}, u32[]{:S(2)}, u32[]{:S(2)}) collective-permute-start(bf16[256,2048]{1,0:T(8,128)(2,1)} %fusion.48), channel_id=1, source_target_pairs={{0,1},{1,0},{2,3},{3,2},{4,5},{5,4},{6,7},{7,6},{8,9},{9,8},{10,11... | collective-permute-start | bytes 3145736 | tf_op jit(solution)/shard_map/ppermute | solution.py:58
  763.0 25.9 %collective-permute-start.144 = (bf16[64,2624]{1,0:T(8,128)(2,1)S(1)}, bf16[64,2624]{1,0:T(8,128)(2,1)S(1)}, u32[]{:S(2)}, u32[]{:S(2)}) collective-permute-start(bf16[64,2624]{1,0:T(8,128)(2,1)S(1)} %concatenate.256), channel_id=1, source_target_pairs={{0,16},{16,0},{1,17},{17,1},{2,18},{18,2},{3,19},{19,3},{4,20},{20... | collective-permute-start | bytes 1007624 | tf_op jit(solution)/shard_map/ppermute | solution.py:62
  782.2 26.4 %collective-permute-start.146 = (bf16[256,2048]{1,0:T(8,128)(2,1)S(1)}, bf16[256,2048]{1,0:T(8,128)(2,1)}, u32[]{:S(2)}, u32[]{:S(2)}) collective-permute-start(bf16[256,2048]{1,0:T(8,128)(2,1)S(1)} %copy-done.106), channel_id=1, source_target_pairs={{0,1},{1,0},{2,3},{3,2},{4,5},{5,4},{6,7},{7,6},{8,9},{9,8},{10,11... | collective-permute-start | bytes 3145736 | tf_op jit(solution)/shard_map/ppermute | solution.py:58
  782.3 25.3 %collective-permute-start.129 = (bf16[64,1024]{1,0:T(8,128)(2,1)S(1)}, bf16[64,1024]{1,0:T(8,128)(2,1)S(1)}, u32[]{:S(2)}, u32[]{:S(2)}) collective-permute-start(bf16[64,1024]{1,0:T(8,128)(2,1)S(1)} %copy-done.218), channel_id=1, source_target_pairs={{0,2},{1,3},{2,0},{3,1},{4,6},{5,7},{6,4},{7,5},{8,10},{9,11},{10,... | collective-permute-start | bytes 393224 | tf_op jit(solution)/shard_map/ppermute | solution.py:58
  824.0 215.9 %all-gather.11.cloned.1.call-start = ((), (), s32[]{:S(2)}) async-start(), calls=%async_computation.6 | async-start | bytes 4456448 | tf_op jit(solution)/shard_map/all_gather | solution.py:693
  829.0 31.5 %collective-permute-start.147 = (bf16[256,2048]{1,0:T(8,128)(2,1)}, bf16[256,2048]{1,0:T(8,128)(2,1)S(1)}, u32[]{:S(2)}, u32[]{:S(2)}) collective-permute-start(bf16[256,2048]{1,0:T(8,128)(2,1)} %fusion.54), channel_id=1, source_target_pairs={{0,1},{1,0},{2,3},{3,2},{4,5},{5,4},{6,7},{7,6},{8,9},{9,8},{10,11... | collective-permute-start | bytes 3145736 | tf_op jit(solution)/shard_map/ppermute | solution.py:58
  830.4 74.4 %collective-permute-start.156 = (bf16[184,1024]{1,0:T(8,128)(2,1)}, bf16[184,1024]{1,0:T(8,128)(2,1)}, u32[]{:S(2)}, u32[]{:S(2)}) collective-permute-start(bf16[184,1024]{1,0:T(8,128)(2,1)} %get-tuple-element.402), channel_id=1, source_target_pairs={{0,2},{1,3},{2,0},{3,1},{4,6},{5,7},{6,4},{7,5},{8,10},{9,11},{10,... | collective-permute-start | bytes 1130504 | tf_op jit(solution)/shard_map/ppermute | solution.py:58
  830.5 74.3 %collective-permute-start.157 = (bf16[184,1024]{1,0:T(8,128)(2,1)}, bf16[184,1024]{1,0:T(8,128)(2,1)}, u32[]{:S(2)}, u32[]{:S(2)}) collective-permute-start(bf16[184,1024]{1,0:T(8,128)(2,1)} %get-tuple-element.401), channel_id=1, source_target_pairs={{0,2},{1,3},{2,0},{3,1},{4,6},{5,7},{6,4},{7,5},{8,10},{9,11},{10,... | collective-permute-start | bytes 1130504 | tf_op jit(solution)/shard_map/ppermute | solution.py:58
  831.9 149.5 %collective-permute-start.169 = (bf16[184,1024]{1,0:T(8,128)(2,1)}, bf16[184,1024]{1,0:T(8,128)(2,1)}, u32[]{:S(2)}, u32[]{:S(2)}) collective-permute-start(bf16[184,1024]{1,0:T(8,128)(2,1)} %get-tuple-element.400), channel_id=1, source_target_pairs={{0,2},{1,3},{2,0},{3,1},{4,6},{5,7},{6,4},{7,5},{8,10},{9,11},{10,... | collective-permute-start | bytes 1130504 | tf_op jit(solution)/shard_map/ppermute | solution.py:58
  928.8 39.1 %collective-permute-start.168 = (bf16[256,2048]{1,0:T(8,128)(2,1)S(1)}, bf16[256,2048]{1,0:T(8,128)(2,1)S(1)}, u32[]{:S(2)}, u32[]{:S(2)}) collective-permute-start(bf16[256,2048]{1,0:T(8,128)(2,1)S(1)} %copy-done.116), channel_id=1, source_target_pairs={{0,16},{16,0},{1,17},{17,1},{2,18},{18,2},{3,19},{19,3},{4,20},{20... | collective-permute-start | bytes 3145736 | tf_op jit(solution)/shard_map/ppermute | solution.py:62
  929.6 47.7 %collective-permute-start.167 = (bf16[256,2048]{1,0:T(8,128)(2,1)S(1)}, bf16[256,2048]{1,0:T(8,128)(2,1)S(1)}, u32[]{:S(2)}, u32[]{:S(2)}) collective-permute-start(bf16[256,2048]{1,0:T(8,128)(2,1)S(1)} %convolution_convert_fusion.8), channel_id=1, source_target_pairs={{0,16},{16,0},{1,17},{17,1},{2,18},{18,2},{3,19},{19,3},{4,20},{20... | collective-permute-start | bytes 3145736 | tf_op jit(solution)/shard_map/ppermute | solution.py:62
  979.1 45.2 %collective-permute-start.174 = (bf16[184,1024]{1,0:T(8,128)(2,1)}, bf16[184,1024]{1,0:T(8,128)(2,1)}, u32[]{:S(2)}, u32[]{:S(2)}) collective-permute-start(bf16[184,1024]{1,0:T(8,128)(2,1)} %get-tuple-element.398), channel_id=1, source_target_pairs={{0,2},{1,3},{2,0},{3,1},{4,6},{5,7},{6,4},{7,5},{8,10},{9,11},{10,... | collective-permute-start | bytes 1130504 | tf_op jit(solution)/shard_map/ppermute | solution.py:58
  981.4 48.7 %collective-permute-start.175 = (bf16[184,1024]{1,0:T(8,128)(2,1)}, bf16[184,1024]{1,0:T(8,128)(2,1)}, u32[]{:S(2)}, u32[]{:S(2)}) collective-permute-start(bf16[184,1024]{1,0:T(8,128)(2,1)} %get-tuple-element.397), channel_id=1, source_target_pairs={{0,2},{1,3},{2,0},{3,1},{4,6},{5,7},{6,4},{7,5},{8,10},{9,11},{10,... | collective-permute-start | bytes 1130504 | tf_op jit(solution)/shard_map/ppermute | solution.py:58
  989.0 41.1 %collective-permute-start.176 = (bf16[184,1024]{1,0:T(8,128)(2,1)}, bf16[184,1024]{1,0:T(8,128)(2,1)}, u32[]{:S(2)}, u32[]{:S(2)}) collective-permute-start(bf16[184,1024]{1,0:T(8,128)(2,1)} %get-tuple-element.421), channel_id=1, source_target_pairs={{0,1},{1,0},{2,3},{3,2},{4,5},{5,4},{6,7},{7,6},{8,9},{9,8},{10,11... | collective-permute-start | bytes 1130504 | tf_op jit(solution)/shard_map/ppermute | solution.py:58
  999.9 33.5 %collective-permute-start.178 = (bf16[256,2048]{1,0:T(8,128)(2,1)}, bf16[256,2048]{1,0:T(8,128)(2,1)}, u32[]{:S(2)}, u32[]{:S(2)}) collective-permute-start(bf16[256,2048]{1,0:T(8,128)(2,1)} %fusion.57), channel_id=1, source_target_pairs={{0,1},{1,0},{2,3},{3,2},{4,5},{5,4},{6,7},{7,6},{8,9},{9,8},{10,11... | collective-permute-start | bytes 3145736 | tf_op jit(solution)/shard_map/ppermute | solution.py:58
  1000.3 39.6 %collective-permute-start.179 = (bf16[256,2048]{1,0:T(8,128)(2,1)}, bf16[256,2048]{1,0:T(8,128)(2,1)}, u32[]{:S(2)}, u32[]{:S(2)}) collective-permute-start(bf16[256,2048]{1,0:T(8,128)(2,1)} %fusion.60), channel_id=1, source_target_pairs={{0,1},{1,0},{2,3},{3,2},{4,5},{5,4},{6,7},{7,6},{8,9},{9,8},{10,11... | collective-permute-start | bytes 3145736 | tf_op jit(solution)/shard_map/ppermute | solution.py:58
  1047.7 42.5 %collective-permute-start.195 = (bf16[64,2624]{1,0:T(8,128)(2,1)S(1)}, bf16[64,2624]{1,0:T(8,128)(2,1)S(1)}, u32[]{:S(2)}, u32[]{:S(2)}) collective-permute-start(bf16[64,2624]{1,0:T(8,128)(2,1)S(1)} %concatenate.267), channel_id=1, source_target_pairs={{0,16},{16,0},{1,17},{17,1},{2,18},{18,2},{3,19},{19,3},{4,20},{20... | collective-permute-start | bytes 1007624 | tf_op jit(solution)/shard_map/ppermute | solution.py:62
  1068.4 21.9 %collective-permute-start.196 = (bf16[4,64,1024]{2,1,0:T(8,128)(2,1)S(1)}, bf16[4,64,1024]{2,1,0:T(8,128)(2,1)S(1)}, u32[]{:S(2)}, u32[]{:S(2)}) collective-permute-start(bf16[4,64,1024]{2,1,0:T(8,128)(2,1)S(1)} %get-tuple-element.486), channel_id=1, source_target_pairs={{0,16},{16,0},{1,17},{17,1},{2,18},{18,2},{3,19},{19,3},{4,20},{20... | collective-permute-start | bytes 1572872 | tf_op jit(solution)/shard_map/ppermute | solution.py:62
  1124.5 69.6 %all-to-all-start = ((bf16[16,72,720]{2,1,0:T(8,128)(2,1)}), bf16[16,72,720]{2,1,0:T(8,128)(2,1)}, u32[]{:S(2)}, u32[]{:S(2)}) async-start(bf16[16,72,720]{2,1,0:T(8,128)(2,1)} %copy.212), calls=%async_computation.1 | async-start | bytes 3538944 | tf_op jit(solution)/shard_map/all_to_all | solution.py:728
  1133.9 23.8 %collective-permute-start.203 = (bf16[184,1024]{1,0:T(8,128)(2,1)S(1)}, bf16[184,1024]{1,0:T(8,128)(2,1)S(1)}, u32[]{:S(2)}, u32[]{:S(2)}) collective-permute-start(bf16[184,1024]{1,0:T(8,128)(2,1)S(1)} %copy-done.172), channel_id=1, source_target_pairs={{0,2},{1,3},{2,0},{3,1},{4,6},{5,7},{6,4},{7,5},{8,10},{9,11},{10,... | collective-permute-start | bytes 1130504 | tf_op jit(solution)/shard_map/ppermute | solution.py:58
  1135.1 23.6 %collective-permute-start.204 = (bf16[184,1024]{1,0:T(8,128)(2,1)S(1)}, bf16[184,1024]{1,0:T(8,128)(2,1)S(1)}, u32[]{:S(2)}, u32[]{:S(2)}) collective-permute-start(bf16[184,1024]{1,0:T(8,128)(2,1)S(1)} %get-tuple-element.305), channel_id=1, source_target_pairs={{0,1},{1,0},{2,3},{3,2},{4,5},{5,4},{6,7},{7,6},{8,9},{9,8},{10,11... | collective-permute-start | bytes 1130504 | tf_op jit(solution)/shard_map/ppermute | solution.py:58
  1136.3 28.2 %collective-permute-start.205 = (bf16[184,1024]{1,0:T(8,128)(2,1)S(1)}, bf16[184,1024]{1,0:T(8,128)(2,1)S(1)}, u32[]{:S(2)}, u32[]{:S(2)}) collective-permute-start(bf16[184,1024]{1,0:T(8,128)(2,1)S(1)} %get-tuple-element.306), channel_id=1, source_target_pairs={{0,12},{1,13},{2,14},{3,15},{4,0},{5,1},{6,2},{7,3},{8,4},{9,5},{1... | collective-permute-start | bytes 1130504 | tf_op jit(solution)/shard_map/ppermute | solution.py:58
  1142.9 80.4 %collective-permute-start.210 = (bf16[3,512,2048]{2,1,0:T(8,128)(2,1)}, bf16[3,512,2048]{2,1,0:T(8,128)(2,1)}, u32[]{:S(2)}, u32[]{:S(2)}) collective-permute-start(bf16[3,512,2048]{2,1,0:T(8,128)(2,1)} %broadcast_select_fusion), channel_id=1, source_target_pairs={{0,16},{16,0},{1,17},{17,1},{2,18},{18,2},{3,19},{19,3},{4,20},{20... | collective-permute-start | bytes 18874376 | tf_op jit(solution)/shard_map/ppermute | solution.py:62
  1186.7 28.8 %collective-permute-start.215 = (bf16[3,256,2048]{2,1,0:T(8,128)(2,1)}, bf16[3,256,2048]{2,1,0:T(8,128)(2,1)}, u32[]{:S(2)}, u32[]{:S(2)}) collective-permute-start(bf16[3,256,2048]{2,1,0:T(8,128)(2,1)} %broadcast_select_fusion.5), channel_id=1, source_target_pairs={{0,16},{16,0},{1,17},{17,1},{2,18},{18,2},{3,19},{19,3},{4,20},{20... | collective-permute-start | bytes 9437192 | tf_op jit(solution)/shard_map/ppermute | solution.py:62
  1209.0 26.5 %collective-permute-start.221 = (bf16[184,1024]{1,0:T(8,128)(2,1)S(1)}, bf16[184,1024]{1,0:T(8,128)(2,1)S(1)}, u32[]{:S(2)}, u32[]{:S(2)}) collective-permute-start(bf16[184,1024]{1,0:T(8,128)(2,1)S(1)} %copy-done.167), channel_id=1, source_target_pairs={{0,2},{1,3},{2,0},{3,1},{4,6},{5,7},{6,4},{7,5},{8,10},{9,11},{10,... | collective-permute-start | bytes 1130504 | tf_op jit(solution)/shard_map/ppermute | solution.py:58
  1213.8 23.7 %collective-permute-start.222 = (bf16[184,1024]{1,0:T(8,128)(2,1)S(1)}, bf16[184,1024]{1,0:T(8,128)(2,1)S(1)}, u32[]{:S(2)}, u32[]{:S(2)}) collective-permute-start(bf16[184,1024]{1,0:T(8,128)(2,1)S(1)} %get-tuple-element.404), channel_id=1, source_target_pairs={{0,1},{1,0},{2,3},{3,2},{4,5},{5,4},{6,7},{7,6},{8,9},{9,8},{10,11... | collective-permute-start | bytes 1130504 | tf_op jit(solution)/shard_map/ppermute | solution.py:58
  1215.6 21.9 %collective-permute-start.223 = (bf16[184,1024]{1,0:T(8,128)(2,1)S(1)}, bf16[184,1024]{1,0:T(8,128)(2,1)S(1)}, u32[]{:S(2)}, u32[]{:S(2)}) collective-permute-start(bf16[184,1024]{1,0:T(8,128)(2,1)S(1)} %get-tuple-element.405), channel_id=1, source_target_pairs={{0,12},{1,13},{2,14},{3,15},{4,0},{5,1},{6,2},{7,3},{8,4},{9,5},{1... | collective-permute-start | bytes 1130504 | tf_op jit(solution)/shard_map/ppermute | solution.py:58
  1238.7 33.5 %collective-permute-start.224 = (bf16[184,1024]{1,0:T(8,128)(2,1)S(1)}, bf16[184,1024]{1,0:T(8,128)(2,1)S(1)}, u32[]{:S(2)}, u32[]{:S(2)}) collective-permute-start(bf16[184,1024]{1,0:T(8,128)(2,1)S(1)} %fusion.211), channel_id=1, source_target_pairs={{0,8},{1,9},{2,10},{3,11},{4,12},{5,13},{6,14},{7,15},{16,24},{17,... | collective-permute-start | bytes 1130504 | tf_op jit(solution)/shard_map/ppermute | solution.py:501
  1246.8 33.5 %collective-permute-start.220 = (bf16[184,1024]{1,0:T(8,128)(2,1)S(1)}, bf16[184,1024]{1,0:T(8,128)(2,1)S(1)}, u32[]{:S(2)}, u32[]{:S(2)}) collective-permute-start(bf16[184,1024]{1,0:T(8,128)(2,1)S(1)} %fusion.214), channel_id=1, source_target_pairs={{0,8},{1,9},{2,10},{3,11},{4,12},{5,13},{6,14},{7,15},{16,24},{17,... | collective-permute-start | bytes 1130504 | tf_op jit(solution)/shard_map/ppermute | solution.py:501
  1248.4 34.6 %collective-permute-start.197 = (bf16[64,2048]{1,0:T(8,128)(2,1)S(1)}, bf16[64,2048]{1,0:T(8,128)(2,1)S(1)}, u32[]{:S(2)}, u32[]{:S(2)}) collective-permute-start(bf16[64,2048]{1,0:T(8,128)(2,1)S(1)} %get-tuple-element.370), channel_id=1, source_target_pairs={{0,16},{16,0},{1,17},{17,1},{2,18},{18,2},{3,19},{19,3},{4,20},{20... | collective-permute-start | bytes 786440 | tf_op jit(solution)/shard_map/ppermute | solution.py:62
  (532 other events, 7146.6 us)
Sparse Core Ops, SparseCore 0:
  40.7 189.2 all-gather.4
  318.3 64.3 reduce-scatter.1
  593.3 101.9 all-gather.6
  824.1 55.8 all-gather.8
  883.0 94.9 all-gather.10

commit v5 on v3

--- a/solution.py
+++ b/solution.py
@@ -521,7 +521,7 @@
             add_branch, kept["joined"], kept["down_out"], gain_rows[4]
         )[1](grad_settled)
         due[0].append(grad_side.astype(BF))
-        (grad_down_b,) = background.stage(grad_down.astype(BF))
+        grad_down_b = grad_down.astype(BF)
         grad_down_all = plane_gather(grad_down_b)
         (grad_down_all,) = background.stage(grad_down_all)
         grad_hidden_ff = [dot_rows(grad_down_all, part) for part in weights[2]]

time: 1310 us -> 1300 us (level)
  waiting for transfers between devices: 495 us -> 461 us
  local copies, waits for them, and re-layouts: 130 us -> 148 us
    ppermute x173, waiting for transfers between devices: 468 us -> 437 us  [hop(): return lax.ppermute(value, ('section', 'shard'), pairs)]
    unnamed x804 -> x800, local copies, waits for them, and re-layouts: 30.3 us -> 47.6 us
    ppermute x173, starting transfers between devices: 151 us -> 138 us  [hop(): return lax.ppermute(value, ('section', 'shard'), pairs)]
  transfers between devices with their start and end apart: 229 -> 229, of which waited for: 95 -> 94; matrix products, arithmetic and copies ran while one was open for 35% -> 37% of each run, Pallas kernels for 0% -> 0%
where the time goes in v5:
time: 1300 us; the launch traced here: 1280 us
  waiting for transfers between devices  461 us (35%)
  matrix products  276 us (21%)
  starting transfers between devices  253 us (19%)
  local copies, waits for them, and re-layouts  148 us (11%)
  other arithmetic  125 us (10%)
  between operations  20.7 us (2%)
    ppermute x173, waiting for transfers between devices, hop(): return lax.ppermute(value, ('section', 'shard'), pairs)  437 us
    ppermute x173, starting transfers between devices, hop(): return lax.ppermute(value, ('section', 'shard'), pairs)  138 us
    ppermute x44, starting transfers between devices, swap_cores(): return lax.ppermute(value, 'section', [(0, 1), (1, 0)])  102 us
    dot_general x47, matrix products, dot(): return jnp.dot(left_side, right_side, preferred_element_type=F32)  98 us
    dot_general x46, matrix products, dot_rows(): lax.dot_general(left_side, right_side, (((1,), (1,)), ((), ())), preferre...  95.3 us
    dot_general x29, matrix products, dot_first(): lax.dot_general(left_side, right_side, (((0,), (0,)), ((), ())), preferre...  60.7 us
    unnamed x800, local copies, waits for them, and re-layouts  47.6 us
    dynamic_update_slice x31, local copies, waits for them, and re-layouts, store_blocks(): lax.dynamic_update_slice(buffer, value[None], (source, jnp.int32(0), jnp....  33.1 us
  transfers between devices with their start and end apart: 229, of which 94 were waited for; matrix products, arithmetic and copies ran while one was open for 37% of the time, Pallas kernels for 0%

profile of v5, /device:TPU:27, one launch (start us, length us, event | category | flops | bytes accessed | tf_op | source)
XLA Modules:
  0.0 1283.2 jit_solution(3340186162326491199)
XLA Ops:
  21.5 4.0 collective-permute-done.4
  25.6 6.0 broadcast.717.clone
  33.2 4.8 collective-permute-start.9
  40.7 7.2 fusion.45
  48.7 5.9 broadcast.717
  60.4 6.3 collective-permute-done.8
  70.2 8.8 collective-permute-done.10
  79.0 19.1 %collective-permute-start.14 = (bf16[360,1024]{1,0:T(8,128)(2,1)}, bf16[360,1024]{1,0:T(8,128)(2,1)S(1)}, u32[]{:S(2)}, u32[]{:S(2)}) collective-permute-start(bf16[360,1024]{1,0:T(8,128)(2,1)} %collective-permute-done.6), channel_id=1, source_target_pairs={{0,16},{16,0},{1,17},{17,1},{2,18},{18,2},{3,19},{19,3},{4,20},{20... | collective-permute-start | bytes 2211848 | tf_op jit(solution)/shard_map/ppermute | solution.py:62
  100.1 7.5 collective-permute-done.11
  125.0 3.8 broadcast_select_fusion
  128.9 4.9 collective-permute-done.17
  133.8 23.2 %collective-permute-done.18 = bf16[360,1024]{1,0:T(8,128)(2,1)S(1)} collective-permute-done((bf16[360,1024]{1,0:T(8,128)(2,1)S(1)}, bf16[360,1024]{1,0:T(8,128)(2,1)S(1)}, u32[]{:S(2)}, u32[]{:S(2)}) %collective-permute-start.18) | collective-permute-done | bytes 737312 | tf_op jit(solution)/shard_map/ppermute | solution.py:58
  166.8 45.3 %collective-permute-done.26 = bf16[360,1024]{1,0:T(8,128)(2,1)S(1)} collective-permute-done((bf16[360,1024]{1,0:T(8,128)(2,1)S(1)}, bf16[360,1024]{1,0:T(8,128)(2,1)S(1)}, u32[]{:S(2)}, u32[]{:S(2)}) %collective-permute-start.26) | collective-permute-done | bytes 737312 | tf_op jit(solution)/shard_map/ppermute | solution.py:58
  259.6 16.0 %collective-permute-done.40 = bf16[64,1024]{1,0:T(8,128)(2,1)S(1)} collective-permute-done((bf16[64,1024]{1,0:T(8,128)(2,1)S(1)}, bf16[64,1024]{1,0:T(8,128)(2,1)S(1)}, u32[]{:S(2)}, u32[]{:S(2)}) %collective-permute-start.40) | collective-permute-done | bytes 131104 | tf_op jit(solution)/shard_map/ppermute | solution.py:58
  308.1 6.1 collective-permute-done.54
  332.3 4.0 collective-permute-start.74
  340.5 5.0 collective-permute-done.61
  345.5 7.4 collective-permute-done.62
  373.3 7.8 collective-permute-done.69
  424.5 4.4 collective-permute-done.75
  452.9 5.3 collective-permute-done.78
  498.0 7.4 collective-permute-start.100
  506.5 5.2 collective-permute-done.96
  515.5 4.8 collective-permute-done.98
  522.0 6.7 collective-permute-done.99
  548.7 3.8 collective-permute-done.106
  555.3 4.4 collective-permute-done.107
  561.0 6.2 collective-permute-done.108
  568.3 6.1 collective-permute-done.109
  612.3 4.0 collective-permute-done.117
  617.1 4.4 fusion.41
  647.0 19.6 %collective-permute-start.127 = (bf16[256,2048]{1,0:T(8,128)(2,1)}, bf16[256,2048]{1,0:T(8,128)(2,1)S(1)}, u32[]{:S(2)}, u32[]{:S(2)}) collective-permute-start(bf16[256,2048]{1,0:T(8,128)(2,1)} %convolution_convert_fusion.12), channel_id=1, source_target_pairs={{0,16},{16,0},{1,17},{17,1},{2,18},{18,2},{3,19},{19,3},{4,20},{20... | collective-permute-start | bytes 3145736 | tf_op jit(solution)/shard_map/ppermute | solution.py:62
  672.2 5.3 collective-permute-done.121
  678.9 4.0 collective-permute-done.120
  684.0 4.6 collective-permute-done.122
  692.8 4.3 collective-permute-done.123
  711.7 4.4 fusion.76
  741.5 3.9 broadcast_select_fusion.27
  745.3 7.1 collective-permute-done.128
  759.3 5.2 collective-permute-start.144
  790.8 13.4 %collective-permute-done.129 = bf16[64,1024]{1,0:T(8,128)(2,1)S(1)} collective-permute-done((bf16[64,1024]{1,0:T(8,128)(2,1)S(1)}, bf16[64,1024]{1,0:T(8,128)(2,1)S(1)}, u32[]{:S(2)}, u32[]{:S(2)}) %collective-permute-start.129) | collective-permute-done | bytes 131104 | tf_op jit(solution)/shard_map/ppermute | solution.py:58
  852.2 4.8 collective-permute-done.152
  858.4 4.2 collective-permute-done.153
  864.4 4.5 fusion.44
  903.3 4.6 collective-permute-done.159
  913.9 9.4 collective-permute-done.160
  928.4 7.7 collective-permute-done.161
  938.0 11.2 collective-permute-done.156
  957.9 9.3 collective-permute-done.168
  1007.1 9.0 collective-permute-done.174
  1033.2 11.3 fusion.2
  1058.0 23.0 %collective-permute-done.175 = bf16[64,1024]{1,0:T(8,128)(2,1)S(1)} collective-permute-done((bf16[64,1024]{1,0:T(8,128)(2,1)S(1)}, bf16[64,1024]{1,0:T(8,128)(2,1)S(1)}, u32[]{:S(2)}, u32[]{:S(2)}) %collective-permute-start.175) | collective-permute-done | bytes 131104 | tf_op jit(solution)/shard_map/ppermute | solution.py:58
  1089.4 4.3 collective-permute-done.195
  1110.8 24.4 %collective-permute-done.207 = bf16[184,1024]{1,0:T(8,128)(2,1)S(1)} collective-permute-done((bf16[184,1024]{1,0:T(8,128)(2,1)S(1)}, bf16[184,1024]{1,0:T(8,128)(2,1)S(1)}, u32[]{:S(2)}, u32[]{:S(2)}) %collective-permute-start.207) | collective-permute-done | bytes 376864 | tf_op jit(solution)/shard_map/ppermute | solution.py:58
  1143.0 7.9 all-to-all-start
  1158.5 10.3 select_convert_fusion
  1172.4 5.0 collective-permute-done.199
  1177.5 4.1 collective-permute-done.202
  1193.0 4.1 collective-permute-done.211
  1201.3 4.1 fusion.595
  1218.7 4.2 collective-permute-done.198
  1231.5 11.4 convert_add_fusion
  1244.5 7.7 collective-permute-start.197
  1252.3 13.8 %collective-permute-done.216 = bf16[184,1024]{1,0:T(8,128)(2,1)S(1)} collective-permute-done((bf16[184,1024]{1,0:T(8,128)(2,1)S(1)}, bf16[184,1024]{1,0:T(8,128)(2,1)S(1)}, u32[]{:S(2)}, u32[]{:S(2)}) %collective-permute-start.216) | collective-permute-done | bytes 376864 | tf_op jit(solution)/shard_map/ppermute | solution.py:498
  (1696 shorter events, 734.6 us)
Async XLA Ops:
  7.2 325.1 %all-gather.5.cloned.1.call-start = ((), (), s32[]{:S(2)}) async-start(), calls=%async_computation.3 | async-start | bytes 12533760 | tf_op jit(solution)/shard_map/all_gather | solution.py:306
  10.5 114.5 %collective-permute-start.21 = (bf16[3,512,2048]{2,1,0:T(8,128)(2,1)}, bf16[3,512,2048]{2,1,0:T(8,128)(2,1)}, u32[]{:S(2)}, u32[]{:S(2)}) collective-permute-start(bf16[3,512,2048]{2,1,0:T(8,128)(2,1)} %bitcast.636), channel_id=1, source_target_pairs={{0,16},{16,0},{1,17},{17,1},{2,18},{18,2},{3,19},{19,3},{4,20},{20... | collective-permute-start | bytes 18874376 | tf_op jit(solution)/shard_map/ppermute | solution.py:62
  39.5 27.2 %collective-permute-start.8 = (bf16[360,1024]{1,0:T(8,128)(2,1)}, bf16[360,1024]{1,0:T(8,128)(2,1)}, u32[]{:S(2)}, u32[]{:S(2)}) collective-permute-start(bf16[360,1024]{1,0:T(8,128)(2,1)} %get-tuple-element.377), channel_id=1, source_target_pairs={{0,4},{1,5},{2,6},{3,7},{4,8},{5,9},{6,10},{7,11},{8,12},{9,13},{1... | collective-permute-start | bytes 2211848 | tf_op jit(solution)/shard_map/ppermute | solution.py:58
  40.6 351.9 %reduce-scatter.2.cloned.1.call-start = ((), (), s32[]{:S(2)}) async-start(), calls=%async_computation.2 | async-start | bytes 1114112 | tf_op jit(solution)/shard_map/reduce_scatter | solution.py:339
  69.6 38.0 %collective-permute-start.11 = (bf16[360,1024]{1,0:T(8,128)(2,1)}, bf16[360,1024]{1,0:T(8,128)(2,1)S(1)}, u32[]{:S(2)}, u32[]{:S(2)}) collective-permute-start(bf16[360,1024]{1,0:T(8,128)(2,1)} %collective-permute-done.8), channel_id=1, source_target_pairs={{0,2},{1,3},{2,0},{3,1},{4,6},{5,7},{6,4},{7,5},{8,10},{9,11},{10,... | collective-permute-start | bytes 2211848 | tf_op jit(solution)/shard_map/ppermute | solution.py:58
  69.8 39.9 %collective-permute-start.12 = (bf16[360,1024]{1,0:T(8,128)(2,1)}, bf16[360,1024]{1,0:T(8,128)(2,1)S(1)}, u32[]{:S(2)}, u32[]{:S(2)}) collective-permute-start(bf16[360,1024]{1,0:T(8,128)(2,1)} %collective-permute-done.8), channel_id=1, source_target_pairs={{0,1},{1,0},{2,3},{3,2},{4,5},{5,4},{6,7},{7,6},{8,9},{9,8},{10,11... | collective-permute-start | bytes 2211848 | tf_op jit(solution)/shard_map/ppermute | solution.py:58
  69.9 42.3 %collective-permute-start.13 = (bf16[360,1024]{1,0:T(8,128)(2,1)}, bf16[360,1024]{1,0:T(8,128)(2,1)S(1)}, u32[]{:S(2)}, u32[]{:S(2)}) collective-permute-start(bf16[360,1024]{1,0:T(8,128)(2,1)} %collective-permute-done.8), channel_id=1, source_target_pairs={{0,4},{1,5},{2,6},{3,7},{4,8},{5,9},{6,10},{7,11},{8,12},{9,13},{1... | collective-permute-start | bytes 2211848 | tf_op jit(solution)/shard_map/ppermute | solution.py:58
  79.0 33.3 %collective-permute-start.14 = (bf16[360,1024]{1,0:T(8,128)(2,1)}, bf16[360,1024]{1,0:T(8,128)(2,1)S(1)}, u32[]{:S(2)}, u32[]{:S(2)}) collective-permute-start(bf16[360,1024]{1,0:T(8,128)(2,1)} %collective-permute-done.6), channel_id=1, source_target_pairs={{0,16},{16,0},{1,17},{17,1},{2,18},{18,2},{3,19},{19,3},{4,20},{20... | collective-permute-start | bytes 2211848 | tf_op jit(solution)/shard_map/ppermute | solution.py:62
  121.8 35.2 %collective-permute-start.18 = (bf16[360,1024]{1,0:T(8,128)(2,1)S(1)}, bf16[360,1024]{1,0:T(8,128)(2,1)S(1)}, u32[]{:S(2)}, u32[]{:S(2)}) collective-permute-start(bf16[360,1024]{1,0:T(8,128)(2,1)S(1)} %collective-permute-done.13), channel_id=1, source_target_pairs={{0,2},{1,3},{2,0},{3,1},{4,6},{5,7},{6,4},{7,5},{8,10},{9,11},{10,... | collective-permute-start | bytes 2211848 | tf_op jit(solution)/shard_map/ppermute | solution.py:58
  123.1 33.9 %collective-permute-start.19 = (bf16[360,1024]{1,0:T(8,128)(2,1)S(1)}, bf16[360,1024]{1,0:T(8,128)(2,1)S(1)}, u32[]{:S(2)}, u32[]{:S(2)}) collective-permute-start(bf16[360,1024]{1,0:T(8,128)(2,1)S(1)} %collective-permute-done.13), channel_id=1, source_target_pairs={{0,1},{1,0},{2,3},{3,2},{4,5},{5,4},{6,7},{7,6},{8,9},{9,8},{10,11... | collective-permute-start | bytes 2211848 | tf_op jit(solution)/shard_map/ppermute | solution.py:58
  124.1 32.9 %collective-permute-start.20 = (bf16[360,1024]{1,0:T(8,128)(2,1)S(1)}, bf16[360,1024]{1,0:T(8,128)(2,1)S(1)}, u32[]{:S(2)}, u32[]{:S(2)}) collective-permute-start(bf16[360,1024]{1,0:T(8,128)(2,1)S(1)} %collective-permute-done.13), channel_id=1, source_target_pairs={{0,4},{1,5},{2,6},{3,7},{4,8},{5,9},{6,10},{7,11},{8,12},{9,13},{1... | collective-permute-start | bytes 2211848 | tf_op jit(solution)/shard_map/ppermute | solution.py:58
  157.0 56.8 %collective-permute-start.27 = (bf16[360,1024]{1,0:T(8,128)(2,1)S(1)}, bf16[360,1024]{1,0:T(8,128)(2,1)S(1)}, u32[]{:S(2)}, u32[]{:S(2)}) collective-permute-start(bf16[360,1024]{1,0:T(8,128)(2,1)S(1)} %collective-permute-done.20), channel_id=1, source_target_pairs={{0,2},{1,3},{2,0},{3,1},{4,6},{5,7},{6,4},{7,5},{8,10},{9,11},{10,... | collective-permute-start | bytes 2211848 | tf_op jit(solution)/shard_map/ppermute | solution.py:58
  158.1 55.7 %collective-permute-start.28 = (bf16[360,1024]{1,0:T(8,128)(2,1)S(1)}, bf16[360,1024]{1,0:T(8,128)(2,1)S(1)}, u32[]{:S(2)}, u32[]{:S(2)}) collective-permute-start(bf16[360,1024]{1,0:T(8,128)(2,1)S(1)} %collective-permute-done.20), channel_id=1, source_target_pairs={{0,1},{1,0},{2,3},{3,2},{4,5},{5,4},{6,7},{7,6},{8,9},{9,8},{10,11... | collective-permute-start | bytes 2211848 | tf_op jit(solution)/shard_map/ppermute | solution.py:58
  158.1 55.7 %collective-permute-start.29 = (bf16[360,1024]{1,0:T(8,128)(2,1)S(1)}, bf16[360,1024]{1,0:T(8,128)(2,1)S(1)}, u32[]{:S(2)}, u32[]{:S(2)}) collective-permute-start(bf16[360,1024]{1,0:T(8,128)(2,1)S(1)} %collective-permute-done.17), channel_id=1, source_target_pairs={{0,16},{16,0},{1,17},{17,1},{2,18},{18,2},{3,19},{19,3},{4,20},{20... | collective-permute-start | bytes 2211848 | tf_op jit(solution)/shard_map/ppermute | solution.py:62
  161.5 53.3 %collective-permute-start.30 = (bf16[360,1024]{1,0:T(8,128)(2,1)S(1)}, bf16[360,1024]{1,0:T(8,128)(2,1)S(1)}, u32[]{:S(2)}, u32[]{:S(2)}) collective-permute-start(bf16[360,1024]{1,0:T(8,128)(2,1)S(1)} %collective-permute-done.18), channel_id=1, source_target_pairs={{0,16},{16,0},{1,17},{17,1},{2,18},{18,2},{3,19},{19,3},{4,20},{20... | collective-permute-start | bytes 2211848 | tf_op jit(solution)/shard_map/ppermute | solution.py:62
  161.5 50.6 %collective-permute-start.26 = (bf16[360,1024]{1,0:T(8,128)(2,1)S(1)}, bf16[360,1024]{1,0:T(8,128)(2,1)S(1)}, u32[]{:S(2)}, u32[]{:S(2)}) collective-permute-start(bf16[360,1024]{1,0:T(8,128)(2,1)S(1)} %collective-permute-done.19), channel_id=1, source_target_pairs={{0,2},{1,3},{2,0},{3,1},{4,6},{5,7},{6,4},{7,5},{8,10},{9,11},{10,... | collective-permute-start | bytes 2211848 | tf_op jit(solution)/shard_map/ppermute | solution.py:58
  243.7 46.5 %collective-permute-start.53 = (bf16[256,2048]{1,0:T(8,128)(2,1)}, bf16[256,2048]{1,0:T(8,128)(2,1)}, u32[]{:S(2)}, u32[]{:S(2)}) collective-permute-start(bf16[256,2048]{1,0:T(8,128)(2,1)} %get-tuple-element.198), channel_id=1, source_target_pairs={{0,1},{1,0},{2,3},{3,2},{4,5},{5,4},{6,7},{7,6},{8,9},{9,8},{10,11... | collective-permute-start | bytes 3145736 | tf_op jit(solution)/shard_map/ppermute | solution.py:58
  252.4 23.6 %collective-permute-start.42 = (bf16[64,1024]{1,0:T(8,128)(2,1)S(1)}, bf16[64,1024]{1,0:T(8,128)(2,1)S(1)}, u32[]{:S(2)}, u32[]{:S(2)}) collective-permute-start(bf16[64,1024]{1,0:T(8,128)(2,1)S(1)} %collective-permute-done.41), channel_id=1, source_target_pairs={{0,2},{1,3},{2,0},{3,1},{4,6},{5,7},{6,4},{7,5},{8,10},{9,11},{10,... | collective-permute-start | bytes 393224 | tf_op jit(solution)/shard_map/ppermute | solution.py:58
  259.2 24.0 %collective-permute-start.46 = (bf16[64,1024]{1,0:T(8,128)(2,1)S(1)}, bf16[64,1024]{1,0:T(8,128)(2,1)S(1)}, u32[]{:S(2)}, u32[]{:S(2)}) collective-permute-start(bf16[64,1024]{1,0:T(8,128)(2,1)S(1)} %collective-permute-done.45), channel_id=1, source_target_pairs={{0,2},{1,3},{2,0},{3,1},{4,6},{5,7},{6,4},{7,5},{8,10},{9,11},{10,... | collective-permute-start | bytes 393224 | tf_op jit(solution)/shard_map/ppermute | solution.py:58
  290.1 24.1 %collective-permute-start.54 = (bf16[256,2048]{1,0:T(8,128)(2,1)}, bf16[256,2048]{1,0:T(8,128)(2,1)}, u32[]{:S(2)}, u32[]{:S(2)}) collective-permute-start(bf16[256,2048]{1,0:T(8,128)(2,1)} %get-tuple-element.202), channel_id=1, source_target_pairs={{0,1},{1,0},{2,3},{3,2},{4,5},{5,4},{6,7},{7,6},{8,9},{9,8},{10,11... | collective-permute-start | bytes 3145736 | tf_op jit(solution)/shard_map/ppermute | solution.py:58
  315.6 429.7 %all-gather.7.cloned.1.call-start = ((), (), s32[]{:S(2)}) async-start(), calls=%async_computation.4 | async-start | bytes 4456448 | tf_op jit(solution)/shard_map/all_gather | solution.py:665
  315.7 43.0 %collective-permute-start.63 = (bf16[256,2048]{1,0:T(8,128)(2,1)}, bf16[256,2048]{1,0:T(8,128)(2,1)}, u32[]{:S(2)}, u32[]{:S(2)}) collective-permute-start(bf16[256,2048]{1,0:T(8,128)(2,1)} %collective-permute-done.53), channel_id=1, source_target_pairs={{0,16},{16,0},{1,17},{17,1},{2,18},{18,2},{3,19},{19,3},{4,20},{20... | collective-permute-start | bytes 3145736 | tf_op jit(solution)/shard_map/ppermute | solution.py:62
  317.9 35.0 %collective-permute-start.62 = (bf16[256,2048]{1,0:T(8,128)(2,1)}, bf16[256,2048]{1,0:T(8,128)(2,1)}, u32[]{:S(2)}, u32[]{:S(2)}) collective-permute-start(bf16[256,2048]{1,0:T(8,128)(2,1)} %get-tuple-element.204), channel_id=1, source_target_pairs={{0,1},{1,0},{2,3},{3,2},{4,5},{5,4},{6,7},{7,6},{8,9},{9,8},{10,11... | collective-permute-start | bytes 3145736 | tf_op jit(solution)/shard_map/ppermute | solution.py:58
  332.3 84.4 %collective-permute-start.74 = (bf16[5760,1024]{1,0:T(8,128)(2,1)}, bf16[5760,1024]{1,0:T(8,128)(2,1)}, u32[]{:S(2)}, u32[]{:S(2)}) collective-permute-start(bf16[5760,1024]{1,0:T(8,128)(2,1)} %all-gather.5.cloned.1.call-done), channel_id=1, source_target_pairs={{0,16},{16,0},{1,17},{17,1},{2,18},{18,2},{3,19},{19,3},{4,20},{20... | collective-permute-start | bytes 35389448 | tf_op jit(solution)/shard_map/ppermute | solution.py:62
  337.3 27.1 %collective-permute-start.64 = (bf16[256,2048]{1,0:T(8,128)(2,1)}, bf16[256,2048]{1,0:T(8,128)(2,1)S(1)}, u32[]{:S(2)}, u32[]{:S(2)}) collective-permute-start(bf16[256,2048]{1,0:T(8,128)(2,1)} %collective-permute-done.54), channel_id=1, source_target_pairs={{0,16},{16,0},{1,17},{17,1},{2,18},{18,2},{3,19},{19,3},{4,20},{20... | collective-permute-start | bytes 3145736 | tf_op jit(solution)/shard_map/ppermute | solution.py:62
  431.0 43.6 %collective-permute-start.91 = (bf16[256,2048]{1,0:T(8,128)(2,1)S(1)}, bf16[256,2048]{1,0:T(8,128)(2,1)}, u32[]{:S(2)}, u32[]{:S(2)}) collective-permute-start(bf16[256,2048]{1,0:T(8,128)(2,1)S(1)} %get-tuple-element.214), channel_id=1, source_target_pairs={{0,1},{1,0},{2,3},{3,2},{4,5},{5,4},{6,7},{7,6},{8,9},{9,8},{10,11... | collective-permute-start | bytes 3145736 | tf_op jit(solution)/shard_map/ppermute | solution.py:58
  498.0 36.6 %collective-permute-start.100 = (bf16[256,2048]{1,0:T(8,128)(2,1)}, bf16[256,2048]{1,0:T(8,128)(2,1)S(1)}, u32[]{:S(2)}, u32[]{:S(2)}) collective-permute-start(bf16[256,2048]{1,0:T(8,128)(2,1)} %collective-permute-done.75), channel_id=1, source_target_pairs={{0,16},{16,0},{1,17},{17,1},{2,18},{18,2},{3,19},{19,3},{4,20},{20... | collective-permute-start | bytes 3145736 | tf_op jit(solution)/shard_map/ppermute | solution.py:62
  505.4 34.4 %collective-permute-start.101 = (bf16[256,2048]{1,0:T(8,128)(2,1)}, bf16[256,2048]{1,0:T(8,128)(2,1)S(1)}, u32[]{:S(2)}, u32[]{:S(2)}) collective-permute-start(bf16[256,2048]{1,0:T(8,128)(2,1)} %collective-permute-done.91), channel_id=1, source_target_pairs={{0,16},{16,0},{1,17},{17,1},{2,18},{18,2},{3,19},{19,3},{4,20},{20... | collective-permute-start | bytes 3145736 | tf_op jit(solution)/shard_map/ppermute | solution.py:62
  505.4 40.7 %collective-permute-start.102 = (bf16[256,2048]{1,0:T(8,128)(2,1)}, bf16[256,2048]{1,0:T(8,128)(2,1)S(1)}, u32[]{:S(2)}, u32[]{:S(2)}) collective-permute-start(bf16[256,2048]{1,0:T(8,128)(2,1)} %collective-permute-done.92), channel_id=1, source_target_pairs={{0,16},{16,0},{1,17},{17,1},{2,18},{18,2},{3,19},{19,3},{4,20},{20... | collective-permute-start | bytes 3145736 | tf_op jit(solution)/shard_map/ppermute | solution.py:62
  592.4 414.7 %all-gather.9.cloned.1.call-start = ((), (), s32[]{:S(2)}) async-start(), calls=%async_computation.5 | async-start | bytes 1114112 | tf_op jit(solution)/shard_map/all_gather | solution.py:681
  647.0 50.2 %collective-permute-start.127 = (bf16[256,2048]{1,0:T(8,128)(2,1)}, bf16[256,2048]{1,0:T(8,128)(2,1)S(1)}, u32[]{:S(2)}, u32[]{:S(2)}) collective-permute-start(bf16[256,2048]{1,0:T(8,128)(2,1)} %convolution_convert_fusion.12), channel_id=1, source_target_pairs={{0,16},{16,0},{1,17},{17,1},{2,18},{18,2},{3,19},{19,3},{4,20},{20... | collective-permute-start | bytes 3145736 | tf_op jit(solution)/shard_map/ppermute | solution.py:62
  667.3 31.7 %collective-permute-start.126 = (bf16[256,2048]{1,0:T(8,128)(2,1)S(1)}, bf16[256,2048]{1,0:T(8,128)(2,1)S(1)}, u32[]{:S(2)}, u32[]{:S(2)}) collective-permute-start(bf16[256,2048]{1,0:T(8,128)(2,1)S(1)} %convolution_convert_fusion.14), channel_id=1, source_target_pairs={{0,16},{16,0},{1,17},{17,1},{2,18},{18,2},{3,19},{19,3},{4,20},{20... | collective-permute-start | bytes 3145736 | tf_op jit(solution)/shard_map/ppermute | solution.py:62
  668.4 32.4 %collective-permute-start.125 = (bf16[256,2048]{1,0:T(8,128)(2,1)S(1)}, bf16[256,2048]{1,0:T(8,128)(2,1)S(1)}, u32[]{:S(2)}, u32[]{:S(2)}) collective-permute-start(bf16[256,2048]{1,0:T(8,128)(2,1)S(1)} %convolution_convert_fusion.16), channel_id=1, source_target_pairs={{0,16},{16,0},{1,17},{17,1},{2,18},{18,2},{3,19},{19,3},{4,20},{20... | collective-permute-start | bytes 3145736 | tf_op jit(solution)/shard_map/ppermute | solution.py:62
  759.3 24.8 %collective-permute-start.144 = (bf16[64,2624]{1,0:T(8,128)(2,1)S(1)}, bf16[64,2624]{1,0:T(8,128)(2,1)S(1)}, u32[]{:S(2)}, u32[]{:S(2)}) collective-permute-start(bf16[64,2624]{1,0:T(8,128)(2,1)S(1)} %concatenate.262), channel_id=1, source_target_pairs={{0,16},{16,0},{1,17},{17,1},{2,18},{18,2},{3,19},{19,3},{4,20},{20... | collective-permute-start | bytes 1007624 | tf_op jit(solution)/shard_map/ppermute | solution.py:62
  779.0 25.3 %collective-permute-start.146 = (bf16[256,2048]{1,0:T(8,128)(2,1)S(1)}, bf16[256,2048]{1,0:T(8,128)(2,1)S(1)}, u32[]{:S(2)}, u32[]{:S(2)}) collective-permute-start(bf16[256,2048]{1,0:T(8,128)(2,1)S(1)} %copy-done.111), channel_id=1, source_target_pairs={{0,1},{1,0},{2,3},{3,2},{4,5},{5,4},{6,7},{7,6},{8,9},{9,8},{10,11... | collective-permute-start | bytes 3145736 | tf_op jit(solution)/shard_map/ppermute | solution.py:58
  779.6 24.6 %collective-permute-start.129 = (bf16[64,1024]{1,0:T(8,128)(2,1)S(1)}, bf16[64,1024]{1,0:T(8,128)(2,1)S(1)}, u32[]{:S(2)}, u32[]{:S(2)}) collective-permute-start(bf16[64,1024]{1,0:T(8,128)(2,1)S(1)} %copy-done.222), channel_id=1, source_target_pairs={{0,2},{1,3},{2,0},{3,1},{4,6},{5,7},{6,4},{7,5},{8,10},{9,11},{10,... | collective-permute-start | bytes 393224 | tf_op jit(solution)/shard_map/ppermute | solution.py:58
  824.6 191.5 %all-gather.11.cloned.1.call-start = ((), (), s32[]{:S(2)}) async-start(), calls=%async_computation.6 | async-start | bytes 4456448 | tf_op jit(solution)/shard_map/all_gather | solution.py:672
  832.8 30.6 %collective-permute-start.155 = (bf16[184,1024]{1,0:T(8,128)(2,1)}, bf16[184,1024]{1,0:T(8,128)(2,1)}, u32[]{:S(2)}, u32[]{:S(2)}) collective-permute-start(bf16[184,1024]{1,0:T(8,128)(2,1)} %get-tuple-element.387), channel_id=1, source_target_pairs={{0,2},{1,3},{2,0},{3,1},{4,6},{5,7},{6,4},{7,5},{8,10},{9,11},{10,... | collective-permute-start | bytes 1130504 | tf_op jit(solution)/shard_map/ppermute | solution.py:58
  834.1 30.3 %collective-permute-start.154 = (bf16[256,2048]{1,0:T(8,128)(2,1)}, bf16[256,2048]{1,0:T(8,128)(2,1)}, u32[]{:S(2)}, u32[]{:S(2)}) collective-permute-start(bf16[256,2048]{1,0:T(8,128)(2,1)} %fusion.54), channel_id=1, source_target_pairs={{0,1},{1,0},{2,3},{3,2},{4,5},{5,4},{6,7},{7,6},{8,9},{9,8},{10,11... | collective-permute-start | bytes 3145736 | tf_op jit(solution)/shard_map/ppermute | solution.py:58
  834.3 123.5 %collective-permute-start.166 = (bf16[184,1024]{1,0:T(8,128)(2,1)}, bf16[184,1024]{1,0:T(8,128)(2,1)}, u32[]{:S(2)}, u32[]{:S(2)}) collective-permute-start(bf16[184,1024]{1,0:T(8,128)(2,1)} %get-tuple-element.386), channel_id=1, source_target_pairs={{0,2},{1,3},{2,0},{3,1},{4,6},{5,7},{6,4},{7,5},{8,10},{9,11},{10,... | collective-permute-start | bytes 1130504 | tf_op jit(solution)/shard_map/ppermute | solution.py:58
  895.8 40.4 %collective-permute-start.165 = (bf16[256,2048]{1,0:T(8,128)(2,1)S(1)}, bf16[256,2048]{1,0:T(8,128)(2,1)S(1)}, u32[]{:S(2)}, u32[]{:S(2)}) collective-permute-start(bf16[256,2048]{1,0:T(8,128)(2,1)S(1)} %copy-done.122), channel_id=1, source_target_pairs={{0,16},{16,0},{1,17},{17,1},{2,18},{18,2},{3,19},{19,3},{4,20},{20... | collective-permute-start | bytes 3145736 | tf_op jit(solution)/shard_map/ppermute | solution.py:62
  900.0 51.7 %collective-permute-start.164 = (bf16[256,2048]{1,0:T(8,128)(2,1)S(1)}, bf16[256,2048]{1,0:T(8,128)(2,1)S(1)}, u32[]{:S(2)}, u32[]{:S(2)}) collective-permute-start(bf16[256,2048]{1,0:T(8,128)(2,1)S(1)} %convolution_convert_fusion.8), channel_id=1, source_target_pairs={{0,16},{16,0},{1,17},{17,1},{2,18},{18,2},{3,19},{19,3},{4,20},{20... | collective-permute-start | bytes 3145736 | tf_op jit(solution)/shard_map/ppermute | solution.py:62
  925.5 29.4 %collective-permute-start.163 = (bf16[256,2048]{1,0:T(8,128)(2,1)S(1)}, bf16[256,2048]{1,0:T(8,128)(2,1)S(1)}, u32[]{:S(2)}, u32[]{:S(2)}) collective-permute-start(bf16[256,2048]{1,0:T(8,128)(2,1)S(1)} %convolution_convert_fusion.10), channel_id=1, source_target_pairs={{0,16},{16,0},{1,17},{17,1},{2,18},{18,2},{3,19},{19,3},{4,20},{20... | collective-permute-start | bytes 3145736 | tf_op jit(solution)/shard_map/ppermute | solution.py:62
  951.3 55.8 %collective-permute-start.170 = (bf16[184,1024]{1,0:T(8,128)(2,1)}, bf16[184,1024]{1,0:T(8,128)(2,1)}, u32[]{:S(2)}, u32[]{:S(2)}) collective-permute-start(bf16[184,1024]{1,0:T(8,128)(2,1)} %get-tuple-element.384), channel_id=1, source_target_pairs={{0,2},{1,3},{2,0},{3,1},{4,6},{5,7},{6,4},{7,5},{8,10},{9,11},{10,... | collective-permute-start | bytes 1130504 | tf_op jit(solution)/shard_map/ppermute | solution.py:58
  954.9 52.2 %collective-permute-start.171 = (bf16[184,1024]{1,0:T(8,128)(2,1)}, bf16[184,1024]{1,0:T(8,128)(2,1)}, u32[]{:S(2)}, u32[]{:S(2)}) collective-permute-start(bf16[184,1024]{1,0:T(8,128)(2,1)} %get-tuple-element.383), channel_id=1, source_target_pairs={{0,2},{1,3},{2,0},{3,1},{4,6},{5,7},{6,4},{7,5},{8,10},{9,11},{10,... | collective-permute-start | bytes 1130504 | tf_op jit(solution)/shard_map/ppermute | solution.py:58
  969.6 37.4 %collective-permute-start.172 = (bf16[184,1024]{1,0:T(8,128)(2,1)}, bf16[184,1024]{1,0:T(8,128)(2,1)}, u32[]{:S(2)}, u32[]{:S(2)}) collective-permute-start(bf16[184,1024]{1,0:T(8,128)(2,1)} %get-tuple-element.405), channel_id=1, source_target_pairs={{0,1},{1,0},{2,3},{3,2},{4,5},{5,4},{6,7},{7,6},{8,9},{9,8},{10,11... | collective-permute-start | bytes 1130504 | tf_op jit(solution)/shard_map/ppermute | solution.py:58
  970.4 36.7 %collective-permute-start.173 = (bf16[184,1024]{1,0:T(8,128)(2,1)}, bf16[184,1024]{1,0:T(8,128)(2,1)}, u32[]{:S(2)}, u32[]{:S(2)}) collective-permute-start(bf16[184,1024]{1,0:T(8,128)(2,1)} %get-tuple-element.404), channel_id=1, source_target_pairs={{0,12},{1,13},{2,14},{3,15},{4,0},{5,1},{6,2},{7,3},{8,4},{9,5},{1... | collective-permute-start | bytes 1130504 | tf_op jit(solution)/shard_map/ppermute | solution.py:58
  991.2 24.8 %collective-permute-start.174 = (bf16[256,2048]{1,0:T(8,128)(2,1)}, bf16[256,2048]{1,0:T(8,128)(2,1)}, u32[]{:S(2)}, u32[]{:S(2)}) collective-permute-start(bf16[256,2048]{1,0:T(8,128)(2,1)} %fusion.57), channel_id=1, source_target_pairs={{0,1},{1,0},{2,3},{3,2},{4,5},{5,4},{6,7},{7,6},{8,9},{9,8},{10,11... | collective-permute-start | bytes 3145736 | tf_op jit(solution)/shard_map/ppermute | solution.py:58
  1017.1 37.4 %collective-permute-start.190 = (bf16[64,2624]{1,0:T(8,128)(2,1)S(1)}, bf16[64,2624]{1,0:T(8,128)(2,1)S(1)}, u32[]{:S(2)}, u32[]{:S(2)}) collective-permute-start(bf16[64,2624]{1,0:T(8,128)(2,1)S(1)} %concatenate.273), channel_id=1, source_target_pairs={{0,16},{16,0},{1,17},{17,1},{2,18},{18,2},{3,19},{19,3},{4,20},{20... | collective-permute-start | bytes 1007624 | tf_op jit(solution)/shard_map/ppermute | solution.py:62
  1027.8 27.3 %collective-permute-start.191 = (bf16[4,64,1024]{2,1,0:T(8,128)(2,1)S(1)}, bf16[4,64,1024]{2,1,0:T(8,128)(2,1)S(1)}, u32[]{:S(2)}, u32[]{:S(2)}) collective-permute-start(bf16[4,64,1024]{2,1,0:T(8,128)(2,1)S(1)} %get-tuple-element.464), channel_id=1, source_target_pairs={{0,16},{16,0},{1,17},{17,1},{2,18},{18,2},{3,19},{19,3},{4,20},{20... | collective-permute-start | bytes 1572872 | tf_op jit(solution)/shard_map/ppermute | solution.py:62
  1050.2 38.2 %collective-permute-start.192 = (bf16[184,1024]{1,0:T(8,128)(2,1)S(1)}, bf16[184,1024]{1,0:T(8,128)(2,1)S(1)}, u32[]{:S(2)}, u32[]{:S(2)}) collective-permute-start(bf16[184,1024]{1,0:T(8,128)(2,1)S(1)} %copy-done.175), channel_id=1, source_target_pairs={{0,2},{1,3},{2,0},{3,1},{4,6},{5,7},{6,4},{7,5},{8,10},{9,11},{10,... | collective-permute-start | bytes 1130504 | tf_op jit(solution)/shard_map/ppermute | solution.py:58
  1051.1 42.7 %collective-permute-start.196 = (bf16[256,2048]{1,0:T(8,128)(2,1)S(1)}, bf16[256,2048]{1,0:T(8,128)(2,1)S(1)}, u32[]{:S(2)}, u32[]{:S(2)}) collective-permute-start(bf16[256,2048]{1,0:T(8,128)(2,1)S(1)} %copy-done.110), channel_id=1, source_target_pairs={{0,1},{1,0},{2,3},{3,2},{4,5},{5,4},{6,7},{7,6},{8,9},{9,8},{10,11... | collective-permute-start | bytes 3145736 | tf_op jit(solution)/shard_map/ppermute | solution.py:58
  1052.7 28.3 %collective-permute-start.175 = (bf16[64,1024]{1,0:T(8,128)(2,1)S(1)}, bf16[64,1024]{1,0:T(8,128)(2,1)S(1)}, u32[]{:S(2)}, u32[]{:S(2)}) collective-permute-start(bf16[64,1024]{1,0:T(8,128)(2,1)S(1)} %get-tuple-element.414), channel_id=1, source_target_pairs={{0,2},{1,3},{2,0},{3,1},{4,6},{5,7},{6,4},{7,5},{8,10},{9,11},{10,... | collective-permute-start | bytes 393224 | tf_op jit(solution)/shard_map/ppermute | solution.py:58
  1054.5 27.7 %collective-permute-start.177 = (bf16[64,1024]{1,0:T(8,128)(2,1)S(1)}, bf16[64,1024]{1,0:T(8,128)(2,1)S(1)}, u32[]{:S(2)}, u32[]{:S(2)}) collective-permute-start(bf16[64,1024]{1,0:T(8,128)(2,1)S(1)} %get-tuple-element.422), channel_id=1, source_target_pairs={{0,1},{1,0},{2,3},{3,2},{4,5},{5,4},{6,7},{7,6},{8,9},{9,8},{10,11... | collective-permute-start | bytes 393224 | tf_op jit(solution)/shard_map/ppermute | solution.py:58
  1055.1 27.6 %collective-permute-start.189 = (bf16[64,1024]{1,0:T(8,128)(2,1)S(1)}, bf16[64,1024]{1,0:T(8,128)(2,1)S(1)}, u32[]{:S(2)}, u32[]{:S(2)}) collective-permute-start(bf16[64,1024]{1,0:T(8,128)(2,1)S(1)} %add_convert_fusion.9), channel_id=1, source_target_pairs={{0,12},{1,13},{2,14},{3,15},{4,0},{5,1},{6,2},{7,3},{8,4},{9,5},{1... | collective-permute-start | bytes 393224 | tf_op jit(solution)/shard_map/ppermute | solution.py:58
  1103.0 50.0 %collective-permute-start.209 = (bf16[256,2048]{1,0:T(8,128)(2,1)}, bf16[256,2048]{1,0:T(8,128)(2,1)}, u32[]{:S(2)}, u32[]{:S(2)}) collective-permute-start(bf16[256,2048]{1,0:T(8,128)(2,1)} %fusion.63), channel_id=1, source_target_pairs={{0,1},{1,0},{2,3},{3,2},{4,5},{5,4},{6,7},{7,6},{8,9},{9,8},{10,11... | collective-permute-start | bytes 3145736 | tf_op jit(solution)/shard_map/ppermute | solution.py:58
  1108.4 26.8 %collective-permute-start.207 = (bf16[184,1024]{1,0:T(8,128)(2,1)S(1)}, bf16[184,1024]{1,0:T(8,128)(2,1)S(1)}, u32[]{:S(2)}, u32[]{:S(2)}) collective-permute-start(bf16[184,1024]{1,0:T(8,128)(2,1)S(1)} %get-tuple-element.391), channel_id=1, source_target_pairs={{0,2},{1,3},{2,0},{3,1},{4,6},{5,7},{6,4},{7,5},{8,10},{9,11},{10,... | collective-permute-start | bytes 1130504 | tf_op jit(solution)/shard_map/ppermute | solution.py:58
  1108.4 42.5 %collective-permute-start.205 = (bf16[184,1024]{1,0:T(8,128)(2,1)}, bf16[184,1024]{1,0:T(8,128)(2,1)}, u32[]{:S(2)}, u32[]{:S(2)}) collective-permute-start(bf16[184,1024]{1,0:T(8,128)(2,1)} %get-tuple-element.393), channel_id=1, source_target_pairs={{0,2},{1,3},{2,0},{3,1},{4,6},{5,7},{6,4},{7,5},{8,10},{9,11},{10,... | collective-permute-start | bytes 1130504 | tf_op jit(solution)/shard_map/ppermute | solution.py:58
  1109.9 43.1 %collective-permute-start.206 = (bf16[184,1024]{1,0:T(8,128)(2,1)}, bf16[184,1024]{1,0:T(8,128)(2,1)}, u32[]{:S(2)}, u32[]{:S(2)}) collective-permute-start(bf16[184,1024]{1,0:T(8,128)(2,1)} %get-tuple-element.392), channel_id=1, source_target_pairs={{0,2},{1,3},{2,0},{3,1},{4,6},{5,7},{6,4},{7,5},{8,10},{9,11},{10,... | collective-permute-start | bytes 1130504 | tf_op jit(solution)/shard_map/ppermute | solution.py:58
  1143.0 56.4 %all-to-all-start = ((bf16[16,72,720]{2,1,0:T(8,128)(2,1)}), bf16[16,72,720]{2,1,0:T(8,128)(2,1)}, u32[]{:S(2)}, u32[]{:S(2)}) async-start(bf16[16,72,720]{2,1,0:T(8,128)(2,1)} %copy.212), calls=%async_computation.1 | async-start | bytes 3538944 | tf_op jit(solution)/shard_map/all_to_all | solution.py:707
  1168.9 60.5 %collective-permute-start.214 = (bf16[3,512,2048]{2,1,0:T(8,128)(2,1)}, bf16[3,512,2048]{2,1,0:T(8,128)(2,1)}, u32[]{:S(2)}, u32[]{:S(2)}) collective-permute-start(bf16[3,512,2048]{2,1,0:T(8,128)(2,1)} %select_convert_fusion), channel_id=1, source_target_pairs={{0,16},{16,0},{1,17},{17,1},{2,18},{18,2},{3,19},{19,3},{4,20},{20... | collective-permute-start | bytes 18874376 | tf_op jit(solution)/shard_map/ppermute | solution.py:62
  1222.9 29.4 %collective-permute-start.220 = (bf16[184,1024]{1,0:T(8,128)(2,1)S(1)}, bf16[184,1024]{1,0:T(8,128)(2,1)S(1)}, u32[]{:S(2)}, u32[]{:S(2)}) collective-permute-start(bf16[184,1024]{1,0:T(8,128)(2,1)S(1)} %fusion.211), channel_id=1, source_target_pairs={{0,8},{1,9},{2,10},{3,11},{4,12},{5,13},{6,14},{7,15},{16,24},{17,... | collective-permute-start | bytes 1130504 | tf_op jit(solution)/shard_map/ppermute | solution.py:498
  1242.8 23.2 %collective-permute-start.216 = (bf16[184,1024]{1,0:T(8,128)(2,1)S(1)}, bf16[184,1024]{1,0:T(8,128)(2,1)S(1)}, u32[]{:S(2)}, u32[]{:S(2)}) collective-permute-start(bf16[184,1024]{1,0:T(8,128)(2,1)S(1)} %fusion.226), channel_id=1, source_target_pairs={{0,8},{1,9},{2,10},{3,11},{4,12},{5,13},{6,14},{7,15},{16,24},{17,... | collective-permute-start | bytes 1130504 | tf_op jit(solution)/shard_map/ppermute | solution.py:498
  1244.5 24.5 %collective-permute-start.197 = (bf16[64,2048]{1,0:T(8,128)(2,1)S(1)}, bf16[64,2048]{1,0:T(8,128)(2,1)S(1)}, u32[]{:S(2)}, u32[]{:S(2)}) collective-permute-start(bf16[64,2048]{1,0:T(8,128)(2,1)S(1)} %get-tuple-element.352), channel_id=1, source_target_pairs={{0,16},{16,0},{1,17},{17,1},{2,18},{18,2},{3,19},{19,3},{4,20},{20... | collective-permute-start | bytes 786440 | tf_op jit(solution)/shard_map/ppermute | solution.py:62
  (523 other events, 6999.3 us)
Sparse Core Ops, SparseCore 0:
  40.7 191.6 all-gather.4
  315.7 63.7 reduce-scatter.1
  592.5 88.8 all-gather.6
  824.7 55.7 all-gather.8
  883.6 88.4 all-gather.10
